TPU v7x, 1024 devices: a whole 4x8x16 slice. The times are simulated.
1024 devices in a mesh: pair: 64 (over x, z), virt: 16 (over y, core).
Axes of the slice: x: 4, y: 8, z: 16, core: 2. Of those that a mesh axis runs over, the one named last changes fastest.
Arguments:
- amps: bfloat16 [128, 4096, 512], P('pair', 'virt'), may hold values from -6 to 6
- fock: bfloat16 [4096, 4096], P('virt'), may hold values from -0.15625 to 0.15625
- ladder: bfloat16 [4096, 4096], P('virt'), may hold values from -0.15625 to 0.15625
- couple: bfloat16 [512, 512], replicated, may hold values from -0.25 to 0.25
- tile_list: int32 [128, 32, 12], P('pair', 'virt'), may hold values from 0 to 31, as said below
Outputs:
- residual: bfloat16 [128, 4096, 512], P('pair', 'virt')
Inputs may be any that keep to these rules, and one draw needn't show every extreme that they name: `tile_list`: within one row of the last dimension the 12 tiles are distinct.
All inputs are finite; a program needn't handle non-finite values.
Results may differ from a plain program's by a relative error of at most 0.0053.
Values may be sent and summed in bfloat16 or wider, within the bound.
No kernel may reach another device: no remote copies, remote signals or barrier semaphores. Data moves between devices by JAX's collectives and lax.ppermute only.
A program may use at most 64 MiB of HBM per device.

v0:
```python
import jax
import jax.numpy as jnp
from jax import lax
from jax.sharding import PartitionSpec as P

TILE = 128


def partner(block, axis, distance):
    count = lax.axis_size(axis)
    route = []
    for low in range(count):
        high = low | 1 << distance
        if high != low and high < count:
            route += [(low, high), (high, low)]
    return lax.ppermute(block, axis, route)


def per_device(amps, fock, ladder, couple, tile_list):
    pairs_here = amps.shape[0]
    rows_here = amps.shape[1]
    width_b = amps.shape[2]
    total_tiles = fock.shape[1] // TILE
    row_tiles = rows_here // TILE
    fock_tiles = fock.reshape(row_tiles, TILE, total_tiles, TILE).transpose(0, 2, 1, 3)
    ladder_tiles = ladder.reshape(row_tiles, TILE, total_tiles, TILE).transpose(0, 2, 1, 3)
    row_index = jnp.arange(row_tiles, dtype=jnp.int32)[:, None]

    def pick_ops(listed):
        return (fock_tiles[row_index, listed], ladder_tiles[row_index, listed])

    fock_sel, ladder_sel = jax.vmap(pick_ops)(tile_list)
    whole = lax.all_gather(amps, "virt", axis=1, tiled=True)
    whole_tiles = whole.reshape(pairs_here, total_tiles, TILE, width_b)

    def pick_amps(amp_pair, listed):
        return amp_pair[listed]

    amp_sel = jax.vmap(pick_amps)(whole_tiles, tile_list)
    cycle = jnp.einsum("prkxy,prkyb->prxb", fock_sel, amp_sel, preferred_element_type=jnp.float32)
    lad = jnp.einsum("prkxy,prkyb->prxb", ladder_sel, amp_sel, preferred_element_type=jnp.float32)
    cycle = cycle.reshape(pairs_here, rows_here, width_b)
    lad_rounded = lad.reshape(pairs_here, rows_here, width_b).astype(jnp.bfloat16)
    inner = jnp.einsum("pab,bc->pac", lad_rounded, couple, preferred_element_type=jnp.float32)
    half_term = (cycle + inner).astype(jnp.bfloat16)
    dev_index = lax.axis_index("pair")
    nbits = lax.axis_size("pair").bit_length() - 1
    current = half_term
    for low_bit in range((nbits + 1) // 2):
        high_bit = nbits - 1 - low_bit
        first_swap = partner(current, "pair", low_bit)
        second_swap = partner(first_swap, "pair", high_bit)
        differ = jnp.right_shift(dev_index, low_bit) % 2 != jnp.right_shift(dev_index, high_bit) % 2
        current = jnp.where(differ, current, second_swap)
    return (half_term.astype(jnp.float32) + current.astype(jnp.float32)).astype(jnp.bfloat16)


def solution(mesh):
    in_specs = (
        P("pair", "virt", None),
        P("virt", None),
        P("virt", None),
        P(),
        P("pair", "virt", None),
    )
    out_specs = P("pair", "virt", None)
    return jax.shard_map(
        per_device, mesh=mesh, in_specs=in_specs, out_specs=out_specs, check_vma=False
    )
```

profile of v0, /device:TPU:28, one launch (start us, length us, event | category | flops | bytes accessed | tf_op | source)
XLA Modules:
  0.0 298.2 jit_solution(11640413203705476557)
XLA Ops:
  6.5 0.7 all-gather.2.cloned.1.call-update
  7.3 0.7 shift-left_or_fusion
  7.9 0.1 reshape.30
  8.0 0.1 reshape.18
  8.1 2.1 copy.12
  10.2 0.8 copy.17
  11.0 0.8 copy-done.2
  11.8 0.5 copy.13
  12.3 2.2 copy.16
  14.5 2.1 gather_fusion
  16.6 2.6 gather_fusion.1
  19.2 61.7 %all-gather.2.cloned.1.call-done = bf16[2,4096,512]{2,1,0:T(8,128)(2,1)} async-done(((bf16[2,256,512]{2,1,0:T(8,128)(2,1)}), bf16[2,4096,512]{2,1,0:T(8,128)(2,1)}) %all-gather.2.cloned.1.call-update) | async-done | bytes 8388624 | tf_op jit(solution)/shard_map/all_gather | solution.py:33
  80.9 8.7 %gather_fusion.2 = bf16[48,128,512]{2,1,0:T(8,128)(2,1)} fusion(bf16[2,32,128,512]{3,2,1,0:T(8,128)(2,1)} %bitcast.52, s32[48]{0:T(128)S(1)} %reshape.30), kind=kCustom, calls=%fused_computation.2 | custom fusion | bytes 12583296 | tf_op jit(solution)/shard_map/vmap()/gather | solution.py:37
  89.6 4.4 %fusion.6 = f32[2,2,128,512,1]{3,2,4,1,0:T(8,128)S(1)} fusion(bf16[2,2,12,128,128]{4,3,2,1,0:T(8,128)(2,1)} %bitcast.51, bf16[2,2,12,128,512]{4,3,2,1,0:T(8,128)(2,1)} %bitcast.44), kind=kOutput, calls=%fused_computation.19 | convolution fusion | flops 805306368 | bytes 8912896 | tf_op jit(solution)/shard_map/prkxy,prkyb->prxb/dot_general | solution.py:40
  94.0 0.6 copy-done.1
  94.6 1.0 fusion
  95.7 0.4 fusion.1
  96.1 3.6 %collective-permute-start = (bf16[2,256,512]{2,1,0:T(8,128)(2,1)S(1)}, bf16[2,256,512]{2,1,0:T(8,128)(2,1)S(1)}, u32[]{:S(2)}, u32[]{:S(2)}) collective-permute-start(bf16[2,256,512]{2,1,0:T(8,128)(2,1)S(1)} %fusion.1), channel_id=1, source_target_pairs={{0,16},{16,0},{32,48},{48,32},{64,80},{80,64},{96,112},{112,96},{1... | collective-permute-start | bytes 1572872 | tf_op jit(solution)/shard_map/ppermute | solution.py:16
  99.7 12.4 %collective-permute-done = bf16[2,256,512]{2,1,0:T(8,128)(2,1)S(1)} collective-permute-done((bf16[2,256,512]{2,1,0:T(8,128)(2,1)S(1)}, bf16[2,256,512]{2,1,0:T(8,128)(2,1)S(1)}, u32[]{:S(2)}, u32[]{:S(2)}) %collective-permute-start) | collective-permute-done | bytes 524320 | tf_op jit(solution)/shard_map/ppermute | solution.py:16
  112.1 2.4 collective-permute-start.1
  114.6 14.2 %collective-permute-done.1 = bf16[2,256,512]{2,1,0:T(8,128)(2,1)S(1)} collective-permute-done((bf16[2,256,512]{2,1,0:T(8,128)(2,1)S(1)}, bf16[2,256,512]{2,1,0:T(8,128)(2,1)S(1)}, u32[]{:S(2)}, u32[]{:S(2)}) %collective-permute-start.1) | collective-permute-done | bytes 524320 | tf_op jit(solution)/shard_map/ppermute | solution.py:16
  128.7 0.1 broadcast_select_fusion
  128.8 4.6 %collective-permute-start.2 = (bf16[2,256,512]{2,1,0:T(8,128)(2,1)S(1)}, bf16[2,256,512]{2,1,0:T(8,128)(2,1)S(1)}, u32[]{:S(2)}, u32[]{:S(2)}) collective-permute-start(bf16[2,256,512]{2,1,0:T(8,128)(2,1)S(1)} %broadcast_select_fusion), channel_id=1, source_target_pairs={{0,32},{32,0},{16,48},{48,16},{64,96},{96,64},{80,112},{112,80},{1... | collective-permute-start | bytes 1572872 | tf_op jit(solution)/shard_map/ppermute | solution.py:16
  133.4 21.8 %collective-permute-done.2 = bf16[2,256,512]{2,1,0:T(8,128)(2,1)S(1)} collective-permute-done((bf16[2,256,512]{2,1,0:T(8,128)(2,1)S(1)}, bf16[2,256,512]{2,1,0:T(8,128)(2,1)S(1)}, u32[]{:S(2)}, u32[]{:S(2)}) %collective-permute-start.2) | collective-permute-done | bytes 524320 | tf_op jit(solution)/shard_map/ppermute | solution.py:16
  155.2 3.1 %collective-permute-start.3 = (bf16[2,256,512]{2,1,0:T(8,128)(2,1)S(1)}, bf16[2,256,512]{2,1,0:T(8,128)(2,1)S(1)}, u32[]{:S(2)}, u32[]{:S(2)}) collective-permute-start(bf16[2,256,512]{2,1,0:T(8,128)(2,1)S(1)} %collective-permute-done.2), channel_id=1, source_target_pairs={{0,256},{256,0},{16,272},{272,16},{32,288},{288,32},{48,304},{304,... | collective-permute-start | bytes 1572872 | tf_op jit(solution)/shard_map/ppermute | solution.py:16
  158.3 11.4 %collective-permute-done.3 = bf16[2,256,512]{2,1,0:T(8,128)(2,1)S(1)} collective-permute-done((bf16[2,256,512]{2,1,0:T(8,128)(2,1)S(1)}, bf16[2,256,512]{2,1,0:T(8,128)(2,1)S(1)}, u32[]{:S(2)}, u32[]{:S(2)}) %collective-permute-start.3) | collective-permute-done | bytes 524320 | tf_op jit(solution)/shard_map/ppermute | solution.py:16
  169.7 0.1 broadcast_select_fusion.1
  169.8 7.9 %collective-permute-start.4 = (bf16[2,256,512]{2,1,0:T(8,128)(2,1)S(1)}, bf16[2,256,512]{2,1,0:T(8,128)(2,1)S(1)}, u32[]{:S(2)}, u32[]{:S(2)}) collective-permute-start(bf16[2,256,512]{2,1,0:T(8,128)(2,1)S(1)} %broadcast_select_fusion.1), channel_id=1, source_target_pairs={{0,64},{64,0},{16,80},{80,16},{32,96},{96,32},{48,112},{112,48},{1... | collective-permute-start | bytes 1572872 | tf_op jit(solution)/shard_map/ppermute | solution.py:16
  177.7 54.0 %collective-permute-done.4 = bf16[2,256,512]{2,1,0:T(8,128)(2,1)S(1)} collective-permute-done((bf16[2,256,512]{2,1,0:T(8,128)(2,1)S(1)}, bf16[2,256,512]{2,1,0:T(8,128)(2,1)S(1)}, u32[]{:S(2)}, u32[]{:S(2)}) %collective-permute-start.4) | collective-permute-done | bytes 524320 | tf_op jit(solution)/shard_map/ppermute | solution.py:16
  231.7 35.3 %collective-permute-start.5 = (bf16[2,256,512]{2,1,0:T(8,128)(2,1)S(1)}, bf16[2,256,512]{2,1,0:T(8,128)(2,1)S(1)}, u32[]{:S(2)}, u32[]{:S(2)}) collective-permute-start(bf16[2,256,512]{2,1,0:T(8,128)(2,1)S(1)} %collective-permute-done.4), channel_id=1, source_target_pairs={{0,128},{128,0},{16,144},{144,16},{32,160},{160,32},{48,176},{176,... | collective-permute-start | bytes 1572872 | tf_op jit(solution)/shard_map/ppermute | solution.py:16
  267.1 23.3 %collective-permute-done.5 = bf16[2,256,512]{2,1,0:T(8,128)(2,1)S(1)} collective-permute-done((bf16[2,256,512]{2,1,0:T(8,128)(2,1)S(1)}, bf16[2,256,512]{2,1,0:T(8,128)(2,1)S(1)}, u32[]{:S(2)}, u32[]{:S(2)}) %collective-permute-start.5) | collective-permute-done | bytes 524320 | tf_op jit(solution)/shard_map/ppermute | solution.py:16
  290.4 1.0 add_convert_fusion
  (5 shorter events, 0.0 us)
Async XLA Ops:
  6.5 89.1 %copy-start = (bf16[512,512]{1,0:T(8,128)(2,1)S(1)}, bf16[512,512]{1,0:T(8,128)(2,1)}, u32[]{:S(2)}) copy-start(bf16[512,512]{1,0:T(8,128)(2,1)} %param.8) | copy-start | bytes 1572868
  6.5 74.4 %all-gather.2.cloned.1.call-start = ((), (), s32[]{:S(2)}) async-start(), calls=%async_computation | async-start | bytes 8912896 | tf_op jit(solution)/shard_map/all_gather | solution.py:33
  10.2 1.6 copy-start.2
  89.6 5.0 %copy-start.1 = (bf16[48,128,512]{2,1,0:T(8,128)(2,1)S(1)}, bf16[48,128,512]{2,1,0:T(8,128)(2,1)}, u32[]{:S(2)}) copy-start(bf16[48,128,512]{2,1,0:T(8,128)(2,1)} %gather_fusion.2) | copy-start | bytes 18874372
  96.1 16.0 %collective-permute-start = (bf16[2,256,512]{2,1,0:T(8,128)(2,1)S(1)}, bf16[2,256,512]{2,1,0:T(8,128)(2,1)S(1)}, u32[]{:S(2)}, u32[]{:S(2)}) collective-permute-start(bf16[2,256,512]{2,1,0:T(8,128)(2,1)S(1)} %fusion.1), channel_id=1, source_target_pairs={{0,16},{16,0},{32,48},{48,32},{64,80},{80,64},{96,112},{112,96},{1... | collective-permute-start | bytes 1572872 | tf_op jit(solution)/shard_map/ppermute | solution.py:16
  112.1 16.7 %collective-permute-start.1 = (bf16[2,256,512]{2,1,0:T(8,128)(2,1)S(1)}, bf16[2,256,512]{2,1,0:T(8,128)(2,1)S(1)}, u32[]{:S(2)}, u32[]{:S(2)}) collective-permute-start(bf16[2,256,512]{2,1,0:T(8,128)(2,1)S(1)} %collective-permute-done), channel_id=1, source_target_pairs={{0,512},{512,0},{16,528},{528,16},{32,544},{544,32},{48,560},{560,... | collective-permute-start | bytes 1572872 | tf_op jit(solution)/shard_map/ppermute | solution.py:16
  128.8 26.4 %collective-permute-start.2 = (bf16[2,256,512]{2,1,0:T(8,128)(2,1)S(1)}, bf16[2,256,512]{2,1,0:T(8,128)(2,1)S(1)}, u32[]{:S(2)}, u32[]{:S(2)}) collective-permute-start(bf16[2,256,512]{2,1,0:T(8,128)(2,1)S(1)} %broadcast_select_fusion), channel_id=1, source_target_pairs={{0,32},{32,0},{16,48},{48,16},{64,96},{96,64},{80,112},{112,80},{1... | collective-permute-start | bytes 1572872 | tf_op jit(solution)/shard_map/ppermute | solution.py:16
  155.2 14.5 %collective-permute-start.3 = (bf16[2,256,512]{2,1,0:T(8,128)(2,1)S(1)}, bf16[2,256,512]{2,1,0:T(8,128)(2,1)S(1)}, u32[]{:S(2)}, u32[]{:S(2)}) collective-permute-start(bf16[2,256,512]{2,1,0:T(8,128)(2,1)S(1)} %collective-permute-done.2), channel_id=1, source_target_pairs={{0,256},{256,0},{16,272},{272,16},{32,288},{288,32},{48,304},{304,... | collective-permute-start | bytes 1572872 | tf_op jit(solution)/shard_map/ppermute | solution.py:16
  169.8 62.0 %collective-permute-start.4 = (bf16[2,256,512]{2,1,0:T(8,128)(2,1)S(1)}, bf16[2,256,512]{2,1,0:T(8,128)(2,1)S(1)}, u32[]{:S(2)}, u32[]{:S(2)}) collective-permute-start(bf16[2,256,512]{2,1,0:T(8,128)(2,1)S(1)} %broadcast_select_fusion.1), channel_id=1, source_target_pairs={{0,64},{64,0},{16,80},{80,16},{32,96},{96,32},{48,112},{112,48},{1... | collective-permute-start | bytes 1572872 | tf_op jit(solution)/shard_map/ppermute | solution.py:16
  231.7 58.6 %collective-permute-start.5 = (bf16[2,256,512]{2,1,0:T(8,128)(2,1)S(1)}, bf16[2,256,512]{2,1,0:T(8,128)(2,1)S(1)}, u32[]{:S(2)}, u32[]{:S(2)}) collective-permute-start(bf16[2,256,512]{2,1,0:T(8,128)(2,1)S(1)} %collective-permute-done.4), channel_id=1, source_target_pairs={{0,128},{128,0},{16,144},{144,16},{32,160},{160,32},{48,176},{176,... | collective-permute-start | bytes 1572872 | tf_op jit(solution)/shard_map/ppermute | solution.py:16
Sparse Core Ops, SparseCore 0:
  10.1 70.7 all-gather.1
where the time goes:
time: 299 us; the launch traced here: 298 us
  waiting for transfers between devices  200 us (67%)
  starting transfers between devices  57 us (19%)
  local copies, waits for them, and re-layouts  20.5 us (7%)
  between operations  13.6 us (5%)
  matrix products  5.84 us (2%)
    ppermute x6, waiting for transfers between devices, partner(): return lax.ppermute(block, axis, route)  137 us
    all_gather x1, waiting for transfers between devices, per_device(): whole = lax.all_gather(amps, 'virt', axis=1, tiled=True)  61.7 us
    ppermute x6, starting transfers between devices, partner(): return lax.ppermute(block, axis, route)  57 us
    gather x2, local copies, waits for them, and re-layouts, pick_amps(): return amp_pair[listed]  8.75 us
  transfers between devices with their start and end apart: 7, of which 7 were waited for; matrix products, arithmetic and copies ran while one was open for 4% of the time, Pallas kernels for 0%

commit v1 on v0

v1 whole, which is shorter than its diff:
```python
import functools

import jax
import jax.numpy as jnp
from jax import lax
from jax.experimental import pallas as pl
from jax.experimental.pallas import tpu as pltpu
from jax.sharding import PartitionSpec as P

TILE = 128
HALF = 256
EXTRA = 16
SLOTS = 8
GROUP = 4


def core_swap(block):
    count = lax.axis_size("virt")
    return lax.ppermute(block, "virt", [(v, v ^ 1) for v in range(count)])


def ring_step(block):
    chips = lax.axis_size("virt") // 2
    route = [(2 * c, 2 * ((c + 1) % chips)) for c in range(chips)]
    route += [(2 * c + 1, 2 * ((c - 1) % chips) + 1) for c in range(chips)]
    return lax.ppermute(block, "virt", route)


def mirror_swap(block):
    count = lax.axis_size("pair")
    nbits = count.bit_length() - 1
    route = []
    for low in range(count):
        flipped = sum(((low >> b) & 1) << (nbits - 1 - b) for b in range(nbits))
        route.append((low, count - 1 - flipped))
    return lax.ppermute(block, "pair", route)


def message(amp_pair, listed):
    flat = listed.reshape(1, -1).astype(amp_pair.dtype)
    tail = jnp.pad(flat, ((0, EXTRA - 1), (0, amp_pair.shape[1] - flat.shape[1])))
    return jnp.concatenate([amp_pair, tail], axis=0)


def lists_of(msg, nnz):
    rows = HALF // TILE
    return msg[HALF, : rows * nnz].astype(jnp.int32).reshape(rows, nnz)


def gather_halves(own, other):
    slots = [own]
    x, s = own, other
    for _ in range(3):
        x, s = ring_step(x), ring_step(s)
        slots += [x, s]
    slots.append(ring_step(x))
    return slots


def part_kernel(units, slot_ref, mask_ref, *refs):
    a_refs = refs[: units * SLOTS]
    f_refs = refs[units * SLOTS : units * SLOTS + 4]
    couple_hbm = refs[units * SLOTS + 4]
    own_ref, sib_ref = refs[units * SLOTS + 5 : units * SLOTS + 7]
    a_buf, f_buf, m_buf, acc, couple_buf, a_sem, f_sem, c_sem = refs[units * SLOTS + 7 :]

    def f_copy(i, s):
        col = pl.multiple_of(slot_ref[s] * TILE, HALF)
        return pltpu.make_async_copy(f_refs[i].at[:, pl.ds(col, HALF)], f_buf.at[i, s], f_sem.at[i, s])

    def a_copy(u, s):
        return pltpu.make_async_copy(
            a_refs[u * SLOTS + s].at[pl.ds(0, HALF)], a_buf.at[u, pl.ds(HALF * s, HALF)], a_sem.at[u, s]
        )

    c_copy = pltpu.make_async_copy(couple_hbm, couple_buf, c_sem)
    for s in range(SLOTS):
        for i in range(4):
            f_copy(i, s).start()
        a_copy(0, s).start()
    for u in range(1, units):
        for s in range(SLOTS):
            a_copy(u, s).start()
    c_copy.start()
    for u in range(units):
        for g in range(SLOTS // GROUP):
            for sg in range(GROUP):
                s = g * GROUP + sg
                if u == 0:
                    for i in range(4):
                        f_copy(i, s).wait()
                a_copy(u, s).wait()
                for i in range(4):
                    for rt in range(2):
                        for q in range(2):
                            keep = mask_ref[u * 4 + (i % 2) * 2 + rt, slot_ref[s] + q] != 0
                            tile = f_buf[i, s, rt * TILE : (rt + 1) * TILE, q * TILE : (q + 1) * TILE]
                            m_buf[
                                i * HALF + rt * TILE : i * HALF + (rt + 1) * TILE,
                                sg * HALF + q * TILE : sg * HALF + (q + 1) * TILE,
                            ] = jnp.where(keep, tile, jnp.zeros_like(tile))
            prod = jnp.dot(
                m_buf[...],
                a_buf[u, g * GROUP * HALF : (g + 1) * GROUP * HALF, :],
                preferred_element_type=jnp.float32,
            )
            if u == 0 and g == 0:
                acc[...] = prod
            else:
                acc[...] += prod
    c_copy.wait()
    lad = acc[2 * HALF :, :].astype(jnp.bfloat16)
    total = acc[: 2 * HALF, :] + jnp.dot(lad, couple_buf[...], preferred_element_type=jnp.float32)
    own_ref[...] = total[:HALF, :]
    sib_ref[...] = total[HALF:, :]


def partial_sums(slot_tiles, masks, unit_slots, mats, couple):
    units = len(unit_slots)
    width = couple.shape[0]
    flat = [block for slots in unit_slots for block in slots]
    smem = pl.BlockSpec(memory_space=pltpu.SMEM)
    anywhere = pl.BlockSpec(memory_space=pl.ANY)
    vmem = pl.BlockSpec(memory_space=pltpu.VMEM)
    flops = 2 * units * 4 * HALF * SLOTS * HALF * width + 2 * 2 * HALF * width * width
    return pl.pallas_call(
        functools.partial(part_kernel, units),
        out_shape=[jax.ShapeDtypeStruct((HALF, width), jnp.float32)] * 2,
        in_specs=[smem, smem] + [anywhere] * (len(flat) + 5),
        out_specs=[vmem, vmem],
        scratch_shapes=[
            pltpu.VMEM((units, SLOTS * HALF, width), jnp.bfloat16),
            pltpu.VMEM((4, SLOTS, HALF, HALF), jnp.bfloat16),
            pltpu.VMEM((4 * HALF, GROUP * HALF), jnp.bfloat16),
            pltpu.VMEM((4 * HALF, width), jnp.float32),
            pltpu.VMEM((width, width), jnp.bfloat16),
            pltpu.SemaphoreType.DMA((units, SLOTS)),
            pltpu.SemaphoreType.DMA((4, SLOTS)),
            pltpu.SemaphoreType.DMA,
        ],
        compiler_params=pltpu.CompilerParams(vmem_limit_bytes=36 * 1024 * 1024),
        cost_estimate=pl.CostEstimate(flops=flops, bytes_accessed=8 << 20, transcendentals=0),
        name="partial_sums",
    )(slot_tiles, masks, *flat, *mats, couple)


def per_device(amps, fock, ladder, couple, tile_list):
    chips = lax.axis_size("virt") // 2
    per_chip = 2 * HALF // TILE
    total_tiles = fock.shape[1] // TILE
    nnz = tile_list.shape[2]
    place = lax.axis_index("virt")
    chip, core = place // 2, place % 2
    way = jnp.where(core == 0, -1, 1)

    def slot_tile(hops, other):
        half = jnp.where(other, 1 - core, core)
        return ((chip + way * hops + chips) % chips) * per_chip + half * (HALF // TILE)

    slot_tiles = jnp.stack(
        [slot_tile(h, o) for h, o in ((0, 0), (1, 0), (1, 1), (2, 0), (2, 1), (3, 0), (3, 1), (4, 0))]
    ).astype(jnp.int32)
    columns = jnp.arange(total_tiles, dtype=jnp.int32)

    def mask_of(own_msg, other_msg):
        listed = jnp.concatenate([lists_of(own_msg, nnz), lists_of(other_msg, nnz)], axis=0)
        return jnp.any(listed[:, :, None] == columns, axis=1).astype(jnp.int32)

    msg0 = message(amps[0], tile_list[0])
    msg1 = message(amps[1], tile_list[1])
    far0 = mirror_swap(msg0)
    msg1_other = core_swap(msg1)
    slots1 = gather_halves(msg1, msg1_other)
    mats = (fock, core_swap(fock), ladder, core_swap(ladder))

    own1, sib1 = partial_sums(slot_tiles, mask_of(msg1, msg1_other), [slots1], mats, couple)
    half1 = (own1 + core_swap(sib1)).astype(jnp.bfloat16)
    half1_far = mirror_swap(half1)

    msg0_other = core_swap(msg0)
    far0_other = core_swap(far0)
    slots0 = gather_halves(msg0, msg0_other)
    slots_far = gather_halves(far0, far0_other)
    masks = jnp.concatenate([mask_of(msg0, msg0_other), mask_of(far0, far0_other)], axis=0)
    own0, sib0 = partial_sums(slot_tiles, masks, [slots0, slots_far], mats, couple)
    res0 = (own0 + core_swap(sib0)).astype(jnp.bfloat16)
    res1 = (half1.astype(jnp.float32) + half1_far.astype(jnp.float32)).astype(jnp.bfloat16)
    return jnp.stack([res0, res1])


def solution(mesh):
    in_specs = (
        P("pair", "virt", None),
        P("virt", None),
        P("virt", None),
        P(),
        P("pair", "virt", None),
    )
    out_specs = P("pair", "virt", None)
    return jax.shard_map(
        per_device, mesh=mesh, in_specs=in_specs, out_specs=out_specs, check_vma=False
    )
```

time: 299 us -> 176 us (0.59)
  the two profiles are of different devices: /device:TPU:28 before, /device:TPU:1 now
where the time goes in v1:
time: 176 us; the launch traced here: 175 us
  starting transfers between devices  112 us (64%)
  waiting for transfers between devices  37.3 us (21%)
  Pallas kernels  15 us (9%)
  local copies, waits for them, and re-layouts  8.07 us (5%)
  other arithmetic  2.3 us (1%)
    ppermute x21, starting transfers between devices, ring_step(): return lax.ppermute(block, 'virt', route)  60.8 us
    ppermute x2, waiting for transfers between devices, mirror_swap(): return lax.ppermute(block, 'pair', route)  37.2 us
    ppermute x7, starting transfers between devices, core_swap(): return lax.ppermute(block, 'virt', [(v, v ^ 1) for v in range(count)])  33.7 us
    ppermute x2, starting transfers between devices, mirror_swap(): return lax.ppermute(block, 'pair', route)  17.2 us
    pallas_call x2, Pallas kernels, partial_sums(): pl.pallas_call(functools.partial(part_kernel, units), out_shape=[jax.Shap...  15 us
  transfers between devices with their start and end apart: 30, of which 2 were waited for; matrix products, arithmetic and copies ran while one was open for 2% of the time, Pallas kernels for 9%

profile of v1, /device:TPU:1, one launch (start us, length us, event | category | flops | bytes accessed | tf_op | source)
XLA Modules:
  0.0 175.1 jit_solution(17258649412989009158)
XLA Ops:
  2.0 16.1 %collective-permute-start.20 = (bf16[272,512]{1,0:T(8,128)(2,1)S(1)}, bf16[272,512]{1,0:T(8,128)(2,1)}, u32[]{:S(2)}, u32[]{:S(2)}) collective-permute-start(bf16[272,512]{1,0:T(8,128)(2,1)S(1)} %fusion.3.refs_0_), channel_id=1, source_target_pairs={{0,1},{1,0},{2,3},{3,2},{4,5},{5,4},{6,7},{7,6},{8,9},{9,8},{10,11... | collective-permute-start | bytes 835592 | tf_op jit(solution)/shard_map/ppermute | solution.py:19
  18.1 1.9 %collective-permute-start.21 = (bf16[272,512]{1,0:T(8,128)(2,1)S(1)}, bf16[272,512]{1,0:T(8,128)(2,1)S(1)}, u32[]{:S(2)}, u32[]{:S(2)}) collective-permute-start(bf16[272,512]{1,0:T(8,128)(2,1)S(1)} %fusion.3.refs_0_), channel_id=1, source_target_pairs={{0,2},{2,4},{4,6},{6,8},{8,10},{10,12},{12,14},{14,0},{1,15},{3,1}... | collective-permute-start | bytes 835592 | tf_op jit(solution)/shard_map/ppermute | solution.py:26
  20.1 10.7 %collective-permute-start.1 = (bf16[272,512]{1,0:T(8,128)(2,1)S(1)}, bf16[272,512]{1,0:T(8,128)(2,1)}, u32[]{:S(2)}, u32[]{:S(2)}) collective-permute-start(bf16[272,512]{1,0:T(8,128)(2,1)S(1)} %fusion.2.refs_0_), channel_id=1, source_target_pairs={{0,1008},{16,496},{32,752},{48,240},{64,880},{80,368},{96,624},{11... | collective-permute-start | bytes 835592 | tf_op jit(solution)/shard_map/ppermute | solution.py:36
  30.8 1.9 %collective-permute-start.17 = (bf16[256,4096]{1,0:T(8,128)(2,1)S(1)}, bf16[256,4096]{1,0:T(8,128)(2,1)}, u32[]{:S(2)}, u32[]{:S(2)}) collective-permute-start(bf16[256,4096]{1,0:T(8,128)(2,1)S(1)} %copy-done), channel_id=1, source_target_pairs={{0,1},{1,0},{2,3},{3,2},{4,5},{5,4},{6,7},{7,6},{8,9},{9,8},{10,11... | collective-permute-start | bytes 6291464 | tf_op jit(solution)/shard_map/ppermute | solution.py:19
  32.8 2.4 %collective-permute-start.18 = (bf16[256,4096]{1,0:T(8,128)(2,1)}, bf16[256,4096]{1,0:T(8,128)(2,1)}, u32[]{:S(2)}, u32[]{:S(2)}) collective-permute-start(bf16[256,4096]{1,0:T(8,128)(2,1)} %refs_10_.1), channel_id=1, source_target_pairs={{0,1},{1,0},{2,3},{3,2},{4,5},{5,4},{6,7},{7,6},{8,9},{9,8},{10,11... | collective-permute-start | bytes 6291464 | tf_op jit(solution)/shard_map/ppermute | solution.py:19
  35.2 1.9 %collective-permute-start = (bf16[272,512]{1,0:T(8,128)(2,1)S(1)}, bf16[272,512]{1,0:T(8,128)(2,1)S(1)}, u32[]{:S(2)}, u32[]{:S(2)}) collective-permute-start(bf16[272,512]{1,0:T(8,128)(2,1)S(1)} %fusion.2.refs_0_), channel_id=1, source_target_pairs={{0,1},{1,0},{2,3},{3,2},{4,5},{5,4},{6,7},{7,6},{8,9},{9,8},{10,11... | collective-permute-start | bytes 835592 | tf_op jit(solution)/shard_map/ppermute | solution.py:19
  37.1 3.0 %collective-permute-start.3 = (bf16[272,512]{1,0:T(8,128)(2,1)S(1)}, bf16[272,512]{1,0:T(8,128)(2,1)}, u32[]{:S(2)}, u32[]{:S(2)}) collective-permute-start(bf16[272,512]{1,0:T(8,128)(2,1)S(1)} %fusion.2.refs_0_), channel_id=1, source_target_pairs={{0,2},{2,4},{4,6},{6,8},{8,10},{10,12},{12,14},{14,0},{1,15},{3,1}... | collective-permute-start | bytes 835592 | tf_op jit(solution)/shard_map/ppermute | solution.py:26
  40.8 13.6 %collective-permute-done.1.refs_8_ = bf16[272,512]{1,0:T(8,128)(2,1)} collective-permute-done((bf16[272,512]{1,0:T(8,128)(2,1)S(1)}, bf16[272,512]{1,0:T(8,128)(2,1)}, u32[]{:S(2)}, u32[]{:S(2)}) %collective-permute-start.1) | collective-permute-done | bytes 278560 | tf_op jit(solution)/shard_map/ppermute | solution.py:36
  54.5 3.5 %collective-permute-start.22 = (bf16[272,512]{1,0:T(8,128)(2,1)}, bf16[272,512]{1,0:T(8,128)(2,1)S(1)}, u32[]{:S(2)}, u32[]{:S(2)}) collective-permute-start(bf16[272,512]{1,0:T(8,128)(2,1)} %collective-permute-done.20), channel_id=1, source_target_pairs={{0,2},{2,4},{4,6},{6,8},{8,10},{10,12},{12,14},{14,0},{1,15},{3,1}... | collective-permute-start | bytes 835592 | tf_op jit(solution)/shard_map/ppermute | solution.py:26
  58.0 3.7 %collective-permute-start.23 = (bf16[272,512]{1,0:T(8,128)(2,1)S(1)}, bf16[272,512]{1,0:T(8,128)(2,1)S(1)}, u32[]{:S(2)}, u32[]{:S(2)}) collective-permute-start(bf16[272,512]{1,0:T(8,128)(2,1)S(1)} %collective-permute-done.21.refs_1_), channel_id=1, source_target_pairs={{0,2},{2,4},{4,6},{6,8},{8,10},{10,12},{12,14},{14,0},{1,15},{3,1}... | collective-permute-start | bytes 835592 | tf_op jit(solution)/shard_map/ppermute | solution.py:26
  63.7 3.0 %collective-permute-start.4 = (bf16[272,512]{1,0:T(8,128)(2,1)S(1)}, bf16[272,512]{1,0:T(8,128)(2,1)}, u32[]{:S(2)}, u32[]{:S(2)}) collective-permute-start(bf16[272,512]{1,0:T(8,128)(2,1)S(1)} %collective-permute-done), channel_id=1, source_target_pairs={{0,2},{2,4},{4,6},{6,8},{8,10},{10,12},{12,14},{14,0},{1,15},{3,1}... | collective-permute-start | bytes 835592 | tf_op jit(solution)/shard_map/ppermute | solution.py:26
  66.7 3.5 %collective-permute-start.5 = (bf16[272,512]{1,0:T(8,128)(2,1)}, bf16[272,512]{1,0:T(8,128)(2,1)}, u32[]{:S(2)}, u32[]{:S(2)}) collective-permute-start(bf16[272,512]{1,0:T(8,128)(2,1)} %collective-permute-done.3.refs_1_), channel_id=1, source_target_pairs={{0,2},{2,4},{4,6},{6,8},{8,10},{10,12},{12,14},{14,0},{1,15},{3,1}... | collective-permute-start | bytes 835592 | tf_op jit(solution)/shard_map/ppermute | solution.py:26
  70.3 2.3 %collective-permute-start.10 = (bf16[272,512]{1,0:T(8,128)(2,1)}, bf16[272,512]{1,0:T(8,128)(2,1)}, u32[]{:S(2)}, u32[]{:S(2)}) collective-permute-start(bf16[272,512]{1,0:T(8,128)(2,1)} %collective-permute-done.1.refs_8_), channel_id=1, source_target_pairs={{0,2},{2,4},{4,6},{6,8},{8,10},{10,12},{12,14},{14,0},{1,15},{3,1}... | collective-permute-start | bytes 835592 | tf_op jit(solution)/shard_map/ppermute | solution.py:26
  72.6 3.0 %collective-permute-start.24 = (bf16[272,512]{1,0:T(8,128)(2,1)S(1)}, bf16[272,512]{1,0:T(8,128)(2,1)S(1)}, u32[]{:S(2)}, u32[]{:S(2)}) collective-permute-start(bf16[272,512]{1,0:T(8,128)(2,1)S(1)} %collective-permute-done.22.refs_2_), channel_id=1, source_target_pairs={{0,2},{2,4},{4,6},{6,8},{8,10},{10,12},{12,14},{14,0},{1,15},{3,1}... | collective-permute-start | bytes 835592 | tf_op jit(solution)/shard_map/ppermute | solution.py:26
  76.5 3.9 %collective-permute-start.25 = (bf16[272,512]{1,0:T(8,128)(2,1)S(1)}, bf16[272,512]{1,0:T(8,128)(2,1)}, u32[]{:S(2)}, u32[]{:S(2)}) collective-permute-start(bf16[272,512]{1,0:T(8,128)(2,1)S(1)} %collective-permute-done.23.refs_3_), channel_id=1, source_target_pairs={{0,2},{2,4},{4,6},{6,8},{8,10},{10,12},{12,14},{14,0},{1,15},{3,1}... | collective-permute-start | bytes 835592 | tf_op jit(solution)/shard_map/ppermute | solution.py:26
  80.5 2.3 %collective-permute-start.6 = (bf16[272,512]{1,0:T(8,128)(2,1)}, bf16[272,512]{1,0:T(8,128)(2,1)}, u32[]{:S(2)}, u32[]{:S(2)}) collective-permute-start(bf16[272,512]{1,0:T(8,128)(2,1)} %collective-permute-done.4.refs_2_), channel_id=1, source_target_pairs={{0,2},{2,4},{4,6},{6,8},{8,10},{10,12},{12,14},{14,0},{1,15},{3,1}... | collective-permute-start | bytes 835592 | tf_op jit(solution)/shard_map/ppermute | solution.py:26
  82.8 2.1 %collective-permute-start.7 = (bf16[272,512]{1,0:T(8,128)(2,1)}, bf16[272,512]{1,0:T(8,128)(2,1)}, u32[]{:S(2)}, u32[]{:S(2)}) collective-permute-start(bf16[272,512]{1,0:T(8,128)(2,1)} %collective-permute-done.5.refs_3_), channel_id=1, source_target_pairs={{0,2},{2,4},{4,6},{6,8},{8,10},{10,12},{12,14},{14,0},{1,15},{3,1}... | collective-permute-start | bytes 835592 | tf_op jit(solution)/shard_map/ppermute | solution.py:26
  85.8 4.1 %collective-permute-start.11 = (bf16[272,512]{1,0:T(8,128)(2,1)}, bf16[272,512]{1,0:T(8,128)(2,1)}, u32[]{:S(2)}, u32[]{:S(2)}) collective-permute-start(bf16[272,512]{1,0:T(8,128)(2,1)} %copy-done.5), channel_id=1, source_target_pairs={{0,2},{2,4},{4,6},{6,8},{8,10},{10,12},{12,14},{14,0},{1,15},{3,1}... | collective-permute-start | bytes 835592 | tf_op jit(solution)/shard_map/ppermute | solution.py:26
  89.9 2.1 %collective-permute-start.12 = (bf16[272,512]{1,0:T(8,128)(2,1)}, bf16[272,512]{1,0:T(8,128)(2,1)}, u32[]{:S(2)}, u32[]{:S(2)}) collective-permute-start(bf16[272,512]{1,0:T(8,128)(2,1)} %collective-permute-done.10.refs_9_), channel_id=1, source_target_pairs={{0,2},{2,4},{4,6},{6,8},{8,10},{10,12},{12,14},{14,0},{1,15},{3,1}... | collective-permute-start | bytes 835592 | tf_op jit(solution)/shard_map/ppermute | solution.py:26
  92.1 3.0 %collective-permute-start.26 = (bf16[272,512]{1,0:T(8,128)(2,1)S(1)}, bf16[272,512]{1,0:T(8,128)(2,1)}, u32[]{:S(2)}, u32[]{:S(2)}) collective-permute-start(bf16[272,512]{1,0:T(8,128)(2,1)S(1)} %collective-permute-done.24.refs_4_), channel_id=1, source_target_pairs={{0,2},{2,4},{4,6},{6,8},{8,10},{10,12},{12,14},{14,0},{1,15},{3,1}... | collective-permute-start | bytes 835592 | tf_op jit(solution)/shard_map/ppermute | solution.py:26
  96.1 2.8 %collective-permute-start.27 = (bf16[272,512]{1,0:T(8,128)(2,1)}, bf16[272,512]{1,0:T(8,128)(2,1)}, u32[]{:S(2)}, u32[]{:S(2)}) collective-permute-start(bf16[272,512]{1,0:T(8,128)(2,1)} %collective-permute-done.25.refs_5_), channel_id=1, source_target_pairs={{0,2},{2,4},{4,6},{6,8},{8,10},{10,12},{12,14},{14,0},{1,15},{3,1}... | collective-permute-start | bytes 835592 | tf_op jit(solution)/shard_map/ppermute | solution.py:26
  98.9 2.8 %collective-permute-start.13 = (bf16[272,512]{1,0:T(8,128)(2,1)}, bf16[272,512]{1,0:T(8,128)(2,1)}, u32[]{:S(2)}, u32[]{:S(2)}) collective-permute-start(bf16[272,512]{1,0:T(8,128)(2,1)} %collective-permute-done.11.refs_10_), channel_id=1, source_target_pairs={{0,2},{2,4},{4,6},{6,8},{8,10},{10,12},{12,14},{14,0},{1,15},{3,1}... | collective-permute-start | bytes 835592 | tf_op jit(solution)/shard_map/ppermute | solution.py:26
  101.7 3.2 %collective-permute-start.14 = (bf16[272,512]{1,0:T(8,128)(2,1)}, bf16[272,512]{1,0:T(8,128)(2,1)}, u32[]{:S(2)}, u32[]{:S(2)}) collective-permute-start(bf16[272,512]{1,0:T(8,128)(2,1)} %collective-permute-done.12.refs_11_), channel_id=1, source_target_pairs={{0,2},{2,4},{4,6},{6,8},{8,10},{10,12},{12,14},{14,0},{1,15},{3,1}... | collective-permute-start | bytes 835592 | tf_op jit(solution)/shard_map/ppermute | solution.py:26
  105.9 2.3 %collective-permute-start.8 = (bf16[272,512]{1,0:T(8,128)(2,1)}, bf16[272,512]{1,0:T(8,128)(2,1)S(1)}, u32[]{:S(2)}, u32[]{:S(2)}) collective-permute-start(bf16[272,512]{1,0:T(8,128)(2,1)} %collective-permute-done.6.refs_4_), channel_id=1, source_target_pairs={{0,2},{2,4},{4,6},{6,8},{8,10},{10,12},{12,14},{14,0},{1,15},{3,1}... | collective-permute-start | bytes 835592 | tf_op jit(solution)/shard_map/ppermute | solution.py:26
  108.2 2.4 %collective-permute-start.9 = (bf16[272,512]{1,0:T(8,128)(2,1)}, bf16[272,512]{1,0:T(8,128)(2,1)S(1)}, u32[]{:S(2)}, u32[]{:S(2)}) collective-permute-start(bf16[272,512]{1,0:T(8,128)(2,1)} %collective-permute-done.7.refs_5_), channel_id=1, source_target_pairs={{0,2},{2,4},{4,6},{6,8},{8,10},{10,12},{12,14},{14,0},{1,15},{3,1}... | collective-permute-start | bytes 835592 | tf_op jit(solution)/shard_map/ppermute | solution.py:26
  110.7 3.8 %collective-permute-start.15 = (bf16[272,512]{1,0:T(8,128)(2,1)}, bf16[272,512]{1,0:T(8,128)(2,1)S(1)}, u32[]{:S(2)}, u32[]{:S(2)}) collective-permute-start(bf16[272,512]{1,0:T(8,128)(2,1)} %collective-permute-done.13.refs_12_), channel_id=1, source_target_pairs={{0,2},{2,4},{4,6},{6,8},{8,10},{10,12},{12,14},{14,0},{1,15},{3,1}... | collective-permute-start | bytes 835592 | tf_op jit(solution)/shard_map/ppermute | solution.py:26
  114.5 2.1 %collective-permute-start.16 = (bf16[272,512]{1,0:T(8,128)(2,1)}, bf16[272,512]{1,0:T(8,128)(2,1)S(1)}, u32[]{:S(2)}, u32[]{:S(2)}) collective-permute-start(bf16[272,512]{1,0:T(8,128)(2,1)} %collective-permute-done.14.refs_13_), channel_id=1, source_target_pairs={{0,2},{2,4},{4,6},{6,8},{8,10},{10,12},{12,14},{14,0},{1,15},{3,1}... | collective-permute-start | bytes 835592 | tf_op jit(solution)/shard_map/ppermute | solution.py:26
  119.3 5.8 %partial_sums.3 = (f32[256,512]{1,0:T(8,128)S(1)}, f32[256,512]{1,0:T(8,128)S(1)}) custom-call(s32[8]{0:T(128)S(1)} %stack.44.slot_ref, s32[4,32]{1,0:T(4,128)S(1)} %convert_element_type.98.mask_ref, bf16[272,512]{1,0:T(8,128)(2,1)S(1)} %fusion.3.refs_0_, bf16[272,512]{1,0:T(8,128)(2,1)S(1)} %collective-permute-done.21.refs_1_, ...), custom_call_target="tpu_custom_call" | custom-call | flops 2415919104 | bytes 8388608 | tf_op jit(solution)/shard_map/partial_sums/pallas_call | solution.py:126
  125.1 7.5 %collective-permute-start.28 = (f32[256,512]{1,0:T(8,128)S(1)}, f32[256,512]{1,0:T(8,128)S(1)}, u32[]{:S(2)}, u32[]{:S(2)}) collective-permute-start(f32[256,512]{1,0:T(8,128)S(1)} %get-tuple-element.12), channel_id=1, source_target_pairs={{0,1},{1,0},{2,3},{3,2},{4,5},{5,4},{6,7},{7,6},{8,9},{9,8},{10,11... | collective-permute-start | bytes 1572872 | tf_op jit(solution)/shard_map/ppermute | solution.py:19
  132.6 9.2 %partial_sums.2 = (f32[256,512]{1,0:T(8,128)S(1)}, f32[256,512]{1,0:T(8,128)S(1)}) custom-call(s32[8]{0:T(128)S(1)} %stack.44.slot_ref, s32[8,32]{1,0:T(8,128)S(1)} %add_convert_fusion.3.mask_ref, bf16[272,512]{1,0:T(8,128)(2,1)S(1)} %copy-done.4, bf16[272,512]{1,0:T(8,128)(2,1)} %collective-permute-done.3.refs_1_, ...), custom_call_target="tpu_custom_call" | custom-call | flops 4563402752 | bytes 8388608 | tf_op jit(solution)/shard_map/partial_sums/pallas_call | solution.py:126
  143.9 6.6 %collective-permute-start.29 = (bf16[256,512]{1,0:T(8,128)(2,1)S(1)}, bf16[256,512]{1,0:T(8,128)(2,1)S(1)}, u32[]{:S(2)}, u32[]{:S(2)}) collective-permute-start(bf16[256,512]{1,0:T(8,128)(2,1)S(1)} %add_convert_fusion.1), channel_id=1, source_target_pairs={{0,1008},{16,496},{32,752},{48,240},{64,880},{80,368},{96,624},{11... | collective-permute-start | bytes 786440 | tf_op jit(solution)/shard_map/ppermute | solution.py:36
  150.6 23.5 %collective-permute-done.29 = bf16[256,512]{1,0:T(8,128)(2,1)S(1)} collective-permute-done((bf16[256,512]{1,0:T(8,128)(2,1)S(1)}, bf16[256,512]{1,0:T(8,128)(2,1)S(1)}, u32[]{:S(2)}, u32[]{:S(2)}) %collective-permute-start.29) | collective-permute-done | bytes 262176 | tf_op jit(solution)/shard_map/ppermute | solution.py:36
  (74 shorter events, 14.3 us)
Async XLA Ops:
  0.0 30.8 %copy-start = (bf16[256,4096]{1,0:T(8,128)(2,1)S(1)}, bf16[256,4096]{1,0:T(8,128)(2,1)}, u32[]{:S(2)}) copy-start(bf16[256,4096]{1,0:T(8,128)(2,1)} %refs_8_.1) | copy-start | bytes 6291460
  2.0 33.1 %collective-permute-start.20 = (bf16[272,512]{1,0:T(8,128)(2,1)S(1)}, bf16[272,512]{1,0:T(8,128)(2,1)}, u32[]{:S(2)}, u32[]{:S(2)}) collective-permute-start(bf16[272,512]{1,0:T(8,128)(2,1)S(1)} %fusion.3.refs_0_), channel_id=1, source_target_pairs={{0,1},{1,0},{2,3},{3,2},{4,5},{5,4},{6,7},{7,6},{8,9},{9,8},{10,11... | collective-permute-start | bytes 835592 | tf_op jit(solution)/shard_map/ppermute | solution.py:19
  18.1 19.0 %collective-permute-start.21 = (bf16[272,512]{1,0:T(8,128)(2,1)S(1)}, bf16[272,512]{1,0:T(8,128)(2,1)S(1)}, u32[]{:S(2)}, u32[]{:S(2)}) collective-permute-start(bf16[272,512]{1,0:T(8,128)(2,1)S(1)} %fusion.3.refs_0_), channel_id=1, source_target_pairs={{0,2},{2,4},{4,6},{6,8},{8,10},{10,12},{12,14},{14,0},{1,15},{3,1}... | collective-permute-start | bytes 835592 | tf_op jit(solution)/shard_map/ppermute | solution.py:26
  20.1 34.3 %collective-permute-start.1 = (bf16[272,512]{1,0:T(8,128)(2,1)S(1)}, bf16[272,512]{1,0:T(8,128)(2,1)}, u32[]{:S(2)}, u32[]{:S(2)}) collective-permute-start(bf16[272,512]{1,0:T(8,128)(2,1)S(1)} %fusion.2.refs_0_), channel_id=1, source_target_pairs={{0,1008},{16,496},{32,752},{48,240},{64,880},{80,368},{96,624},{11... | collective-permute-start | bytes 835592 | tf_op jit(solution)/shard_map/ppermute | solution.py:36
  30.8 83.7 %collective-permute-start.17 = (bf16[256,4096]{1,0:T(8,128)(2,1)S(1)}, bf16[256,4096]{1,0:T(8,128)(2,1)}, u32[]{:S(2)}, u32[]{:S(2)}) collective-permute-start(bf16[256,4096]{1,0:T(8,128)(2,1)S(1)} %copy-done), channel_id=1, source_target_pairs={{0,1},{1,0},{2,3},{3,2},{4,5},{5,4},{6,7},{7,6},{8,9},{9,8},{10,11... | collective-permute-start | bytes 6291464 | tf_op jit(solution)/shard_map/ppermute | solution.py:19
  32.8 83.9 %collective-permute-start.18 = (bf16[256,4096]{1,0:T(8,128)(2,1)}, bf16[256,4096]{1,0:T(8,128)(2,1)}, u32[]{:S(2)}, u32[]{:S(2)}) collective-permute-start(bf16[256,4096]{1,0:T(8,128)(2,1)} %refs_10_.1), channel_id=1, source_target_pairs={{0,1},{1,0},{2,3},{3,2},{4,5},{5,4},{6,7},{7,6},{8,9},{9,8},{10,11... | collective-permute-start | bytes 6291464 | tf_op jit(solution)/shard_map/ppermute | solution.py:19
  35.2 22.8 %collective-permute-start = (bf16[272,512]{1,0:T(8,128)(2,1)S(1)}, bf16[272,512]{1,0:T(8,128)(2,1)S(1)}, u32[]{:S(2)}, u32[]{:S(2)}) collective-permute-start(bf16[272,512]{1,0:T(8,128)(2,1)S(1)} %fusion.2.refs_0_), channel_id=1, source_target_pairs={{0,1},{1,0},{2,3},{3,2},{4,5},{5,4},{6,7},{7,6},{8,9},{9,8},{10,11... | collective-permute-start | bytes 835592 | tf_op jit(solution)/shard_map/ppermute | solution.py:19
  37.1 24.6 %collective-permute-start.3 = (bf16[272,512]{1,0:T(8,128)(2,1)S(1)}, bf16[272,512]{1,0:T(8,128)(2,1)}, u32[]{:S(2)}, u32[]{:S(2)}) collective-permute-start(bf16[272,512]{1,0:T(8,128)(2,1)S(1)} %fusion.2.refs_0_), channel_id=1, source_target_pairs={{0,2},{2,4},{4,6},{6,8},{8,10},{10,12},{12,14},{14,0},{1,15},{3,1}... | collective-permute-start | bytes 835592 | tf_op jit(solution)/shard_map/ppermute | solution.py:26
  54.5 9.2 %collective-permute-start.22 = (bf16[272,512]{1,0:T(8,128)(2,1)}, bf16[272,512]{1,0:T(8,128)(2,1)S(1)}, u32[]{:S(2)}, u32[]{:S(2)}) collective-permute-start(bf16[272,512]{1,0:T(8,128)(2,1)} %collective-permute-done.20), channel_id=1, source_target_pairs={{0,2},{2,4},{4,6},{6,8},{8,10},{10,12},{12,14},{14,0},{1,15},{3,1}... | collective-permute-start | bytes 835592 | tf_op jit(solution)/shard_map/ppermute | solution.py:26
  58.0 14.5 %copy-start.6 = (bf16[272,512]{1,0:T(8,128)(2,1)}, bf16[272,512]{1,0:T(8,128)(2,1)S(1)}, u32[]{:S(2)}) copy-start(bf16[272,512]{1,0:T(8,128)(2,1)S(1)} %collective-permute-done) | copy-start | bytes 835588
  58.0 8.7 %collective-permute-start.23 = (bf16[272,512]{1,0:T(8,128)(2,1)S(1)}, bf16[272,512]{1,0:T(8,128)(2,1)S(1)}, u32[]{:S(2)}, u32[]{:S(2)}) collective-permute-start(bf16[272,512]{1,0:T(8,128)(2,1)S(1)} %collective-permute-done.21.refs_1_), channel_id=1, source_target_pairs={{0,2},{2,4},{4,6},{6,8},{8,10},{10,12},{12,14},{14,0},{1,15},{3,1}... | collective-permute-start | bytes 835592 | tf_op jit(solution)/shard_map/ppermute | solution.py:26
  61.8 8.5 %collective-permute-start.2 = (bf16[272,512]{1,0:T(8,128)(2,1)}, bf16[272,512]{1,0:T(8,128)(2,1)S(1)}, u32[]{:S(2)}, u32[]{:S(2)}) collective-permute-start(bf16[272,512]{1,0:T(8,128)(2,1)} %collective-permute-done.1.refs_8_), channel_id=1, source_target_pairs={{0,1},{1,0},{2,3},{3,2},{4,5},{5,4},{6,7},{7,6},{8,9},{9,8},{10,11... | collective-permute-start | bytes 835592 | tf_op jit(solution)/shard_map/ppermute | solution.py:19
  63.7 8.9 %collective-permute-start.4 = (bf16[272,512]{1,0:T(8,128)(2,1)S(1)}, bf16[272,512]{1,0:T(8,128)(2,1)}, u32[]{:S(2)}, u32[]{:S(2)}) collective-permute-start(bf16[272,512]{1,0:T(8,128)(2,1)S(1)} %collective-permute-done), channel_id=1, source_target_pairs={{0,2},{2,4},{4,6},{6,8},{8,10},{10,12},{12,14},{14,0},{1,15},{3,1}... | collective-permute-start | bytes 835592 | tf_op jit(solution)/shard_map/ppermute | solution.py:26
  66.7 9.8 %collective-permute-start.5 = (bf16[272,512]{1,0:T(8,128)(2,1)}, bf16[272,512]{1,0:T(8,128)(2,1)}, u32[]{:S(2)}, u32[]{:S(2)}) collective-permute-start(bf16[272,512]{1,0:T(8,128)(2,1)} %collective-permute-done.3.refs_1_), channel_id=1, source_target_pairs={{0,2},{2,4},{4,6},{6,8},{8,10},{10,12},{12,14},{14,0},{1,15},{3,1}... | collective-permute-start | bytes 835592 | tf_op jit(solution)/shard_map/ppermute | solution.py:26
  70.3 10.2 %collective-permute-start.10 = (bf16[272,512]{1,0:T(8,128)(2,1)}, bf16[272,512]{1,0:T(8,128)(2,1)}, u32[]{:S(2)}, u32[]{:S(2)}) collective-permute-start(bf16[272,512]{1,0:T(8,128)(2,1)} %collective-permute-done.1.refs_8_), channel_id=1, source_target_pairs={{0,2},{2,4},{4,6},{6,8},{8,10},{10,12},{12,14},{14,0},{1,15},{3,1}... | collective-permute-start | bytes 835592 | tf_op jit(solution)/shard_map/ppermute | solution.py:26
  72.6 10.2 %collective-permute-start.24 = (bf16[272,512]{1,0:T(8,128)(2,1)S(1)}, bf16[272,512]{1,0:T(8,128)(2,1)S(1)}, u32[]{:S(2)}, u32[]{:S(2)}) collective-permute-start(bf16[272,512]{1,0:T(8,128)(2,1)S(1)} %collective-permute-done.22.refs_2_), channel_id=1, source_target_pairs={{0,2},{2,4},{4,6},{6,8},{8,10},{10,12},{12,14},{14,0},{1,15},{3,1}... | collective-permute-start | bytes 835592 | tf_op jit(solution)/shard_map/ppermute | solution.py:26
  76.5 9.3 %collective-permute-start.25 = (bf16[272,512]{1,0:T(8,128)(2,1)S(1)}, bf16[272,512]{1,0:T(8,128)(2,1)}, u32[]{:S(2)}, u32[]{:S(2)}) collective-permute-start(bf16[272,512]{1,0:T(8,128)(2,1)S(1)} %collective-permute-done.23.refs_3_), channel_id=1, source_target_pairs={{0,2},{2,4},{4,6},{6,8},{8,10},{10,12},{12,14},{14,0},{1,15},{3,1}... | collective-permute-start | bytes 835592 | tf_op jit(solution)/shard_map/ppermute | solution.py:26
  80.5 9.4 %collective-permute-start.6 = (bf16[272,512]{1,0:T(8,128)(2,1)}, bf16[272,512]{1,0:T(8,128)(2,1)}, u32[]{:S(2)}, u32[]{:S(2)}) collective-permute-start(bf16[272,512]{1,0:T(8,128)(2,1)} %collective-permute-done.4.refs_2_), channel_id=1, source_target_pairs={{0,2},{2,4},{4,6},{6,8},{8,10},{10,12},{12,14},{14,0},{1,15},{3,1}... | collective-permute-start | bytes 835592 | tf_op jit(solution)/shard_map/ppermute | solution.py:26
  82.8 9.3 %collective-permute-start.7 = (bf16[272,512]{1,0:T(8,128)(2,1)}, bf16[272,512]{1,0:T(8,128)(2,1)}, u32[]{:S(2)}, u32[]{:S(2)}) collective-permute-start(bf16[272,512]{1,0:T(8,128)(2,1)} %collective-permute-done.5.refs_3_), channel_id=1, source_target_pairs={{0,2},{2,4},{4,6},{6,8},{8,10},{10,12},{12,14},{14,0},{1,15},{3,1}... | collective-permute-start | bytes 835592 | tf_op jit(solution)/shard_map/ppermute | solution.py:26
  85.8 10.3 %collective-permute-start.11 = (bf16[272,512]{1,0:T(8,128)(2,1)}, bf16[272,512]{1,0:T(8,128)(2,1)}, u32[]{:S(2)}, u32[]{:S(2)}) collective-permute-start(bf16[272,512]{1,0:T(8,128)(2,1)} %copy-done.5), channel_id=1, source_target_pairs={{0,2},{2,4},{4,6},{6,8},{8,10},{10,12},{12,14},{14,0},{1,15},{3,1}... | collective-permute-start | bytes 835592 | tf_op jit(solution)/shard_map/ppermute | solution.py:26
  89.9 9.0 %collective-permute-start.12 = (bf16[272,512]{1,0:T(8,128)(2,1)}, bf16[272,512]{1,0:T(8,128)(2,1)}, u32[]{:S(2)}, u32[]{:S(2)}) collective-permute-start(bf16[272,512]{1,0:T(8,128)(2,1)} %collective-permute-done.10.refs_9_), channel_id=1, source_target_pairs={{0,2},{2,4},{4,6},{6,8},{8,10},{10,12},{12,14},{14,0},{1,15},{3,1}... | collective-permute-start | bytes 835592 | tf_op jit(solution)/shard_map/ppermute | solution.py:26
  92.1 9.7 %collective-permute-start.26 = (bf16[272,512]{1,0:T(8,128)(2,1)S(1)}, bf16[272,512]{1,0:T(8,128)(2,1)}, u32[]{:S(2)}, u32[]{:S(2)}) collective-permute-start(bf16[272,512]{1,0:T(8,128)(2,1)S(1)} %collective-permute-done.24.refs_4_), channel_id=1, source_target_pairs={{0,2},{2,4},{4,6},{6,8},{8,10},{10,12},{12,14},{14,0},{1,15},{3,1}... | collective-permute-start | bytes 835592 | tf_op jit(solution)/shard_map/ppermute | solution.py:26
  96.1 9.8 %collective-permute-start.27 = (bf16[272,512]{1,0:T(8,128)(2,1)}, bf16[272,512]{1,0:T(8,128)(2,1)}, u32[]{:S(2)}, u32[]{:S(2)}) collective-permute-start(bf16[272,512]{1,0:T(8,128)(2,1)} %collective-permute-done.25.refs_5_), channel_id=1, source_target_pairs={{0,2},{2,4},{4,6},{6,8},{8,10},{10,12},{12,14},{14,0},{1,15},{3,1}... | collective-permute-start | bytes 835592 | tf_op jit(solution)/shard_map/ppermute | solution.py:26
  98.9 9.3 %collective-permute-start.13 = (bf16[272,512]{1,0:T(8,128)(2,1)}, bf16[272,512]{1,0:T(8,128)(2,1)}, u32[]{:S(2)}, u32[]{:S(2)}) collective-permute-start(bf16[272,512]{1,0:T(8,128)(2,1)} %collective-permute-done.11.refs_10_), channel_id=1, source_target_pairs={{0,2},{2,4},{4,6},{6,8},{8,10},{10,12},{12,14},{14,0},{1,15},{3,1}... | collective-permute-start | bytes 835592 | tf_op jit(solution)/shard_map/ppermute | solution.py:26
  101.7 9.0 %collective-permute-start.14 = (bf16[272,512]{1,0:T(8,128)(2,1)}, bf16[272,512]{1,0:T(8,128)(2,1)}, u32[]{:S(2)}, u32[]{:S(2)}) collective-permute-start(bf16[272,512]{1,0:T(8,128)(2,1)} %collective-permute-done.12.refs_11_), channel_id=1, source_target_pairs={{0,2},{2,4},{4,6},{6,8},{8,10},{10,12},{12,14},{14,0},{1,15},{3,1}... | collective-permute-start | bytes 835592 | tf_op jit(solution)/shard_map/ppermute | solution.py:26
  105.9 26.7 %collective-permute-start.8 = (bf16[272,512]{1,0:T(8,128)(2,1)}, bf16[272,512]{1,0:T(8,128)(2,1)S(1)}, u32[]{:S(2)}, u32[]{:S(2)}) collective-permute-start(bf16[272,512]{1,0:T(8,128)(2,1)} %collective-permute-done.6.refs_4_), channel_id=1, source_target_pairs={{0,2},{2,4},{4,6},{6,8},{8,10},{10,12},{12,14},{14,0},{1,15},{3,1}... | collective-permute-start | bytes 835592 | tf_op jit(solution)/shard_map/ppermute | solution.py:26
  108.2 24.4 %collective-permute-start.9 = (bf16[272,512]{1,0:T(8,128)(2,1)}, bf16[272,512]{1,0:T(8,128)(2,1)S(1)}, u32[]{:S(2)}, u32[]{:S(2)}) collective-permute-start(bf16[272,512]{1,0:T(8,128)(2,1)} %collective-permute-done.7.refs_5_), channel_id=1, source_target_pairs={{0,2},{2,4},{4,6},{6,8},{8,10},{10,12},{12,14},{14,0},{1,15},{3,1}... | collective-permute-start | bytes 835592 | tf_op jit(solution)/shard_map/ppermute | solution.py:26
  110.7 21.9 %collective-permute-start.15 = (bf16[272,512]{1,0:T(8,128)(2,1)}, bf16[272,512]{1,0:T(8,128)(2,1)S(1)}, u32[]{:S(2)}, u32[]{:S(2)}) collective-permute-start(bf16[272,512]{1,0:T(8,128)(2,1)} %collective-permute-done.13.refs_12_), channel_id=1, source_target_pairs={{0,2},{2,4},{4,6},{6,8},{8,10},{10,12},{12,14},{14,0},{1,15},{3,1}... | collective-permute-start | bytes 835592 | tf_op jit(solution)/shard_map/ppermute | solution.py:26
  114.5 18.1 %collective-permute-start.16 = (bf16[272,512]{1,0:T(8,128)(2,1)}, bf16[272,512]{1,0:T(8,128)(2,1)S(1)}, u32[]{:S(2)}, u32[]{:S(2)}) collective-permute-start(bf16[272,512]{1,0:T(8,128)(2,1)} %collective-permute-done.14.refs_13_), channel_id=1, source_target_pairs={{0,2},{2,4},{4,6},{6,8},{8,10},{10,12},{12,14},{14,0},{1,15},{3,1}... | collective-permute-start | bytes 835592 | tf_op jit(solution)/shard_map/ppermute | solution.py:26
  125.1 18.7 %collective-permute-start.28 = (f32[256,512]{1,0:T(8,128)S(1)}, f32[256,512]{1,0:T(8,128)S(1)}, u32[]{:S(2)}, u32[]{:S(2)}) collective-permute-start(f32[256,512]{1,0:T(8,128)S(1)} %get-tuple-element.12), channel_id=1, source_target_pairs={{0,1},{1,0},{2,3},{3,2},{4,5},{5,4},{6,7},{7,6},{8,9},{9,8},{10,11... | collective-permute-start | bytes 1572872 | tf_op jit(solution)/shard_map/ppermute | solution.py:19
  141.9 8.6 %collective-permute-start.19 = (f32[256,512]{1,0:T(8,128)S(1)}, f32[256,512]{1,0:T(8,128)S(1)}, u32[]{:S(2)}, u32[]{:S(2)}) collective-permute-start(f32[256,512]{1,0:T(8,128)S(1)} %get-tuple-element.10), channel_id=1, source_target_pairs={{0,1},{1,0},{2,3},{3,2},{4,5},{5,4},{6,7},{7,6},{8,9},{9,8},{10,11... | collective-permute-start | bytes 1572872 | tf_op jit(solution)/shard_map/ppermute | solution.py:19
  143.9 30.2 %collective-permute-start.29 = (bf16[256,512]{1,0:T(8,128)(2,1)S(1)}, bf16[256,512]{1,0:T(8,128)(2,1)S(1)}, u32[]{:S(2)}, u32[]{:S(2)}) collective-permute-start(bf16[256,512]{1,0:T(8,128)(2,1)S(1)} %add_convert_fusion.1), channel_id=1, source_target_pairs={{0,1008},{16,496},{32,752},{48,240},{64,880},{80,368},{96,624},{11... | collective-permute-start | bytes 786440 | tf_op jit(solution)/shard_map/ppermute | solution.py:36
  (5 other events, 19.0 us)

commit v2 on v0

v2 whole, which is shorter than its diff:
```python
import functools

import jax
import jax.numpy as jnp
from jax import lax
from jax.experimental import pallas as pl
from jax.experimental.pallas import tpu as pltpu
from jax.sharding import PartitionSpec as P

TILE = 128
HALF = 256
EXTRA = 16
VMEM_LIMIT = 24 * 1024 * 1024


def core_swap(block):
    count = lax.axis_size("virt")
    return lax.ppermute(block, "virt", [(v, v ^ 1) for v in range(count)])


def ring_step(block):
    chips = lax.axis_size("virt") // 2
    route = [(2 * c, 2 * ((c + 1) % chips)) for c in range(chips)]
    route += [(2 * c + 1, 2 * ((c - 1) % chips) + 1) for c in range(chips)]
    return lax.ppermute(block, "virt", route)


def mirror_swap(block):
    count = lax.axis_size("pair")
    nbits = count.bit_length() - 1
    route = []
    for low in range(count):
        flipped = sum(((low >> b) & 1) << (nbits - 1 - b) for b in range(nbits))
        route.append((low, count - 1 - flipped))
    return lax.ppermute(block, "pair", route)


def message(amp_pairs, listed):
    pairs, rows, width = amp_pairs.shape
    flat = listed.reshape(pairs, -1).astype(amp_pairs.dtype)
    tail = jnp.pad(flat, ((0, EXTRA - pairs), (0, width - flat.shape[1])))
    return jnp.concatenate([amp_pairs.reshape(pairs * rows, width), tail], axis=0)


def masks_of(own_msg, other_msg, pairs, nnz, total_tiles):
    start, rows = pairs * HALF, HALF // TILE
    lists = [m[start : start + pairs, : rows * nnz].reshape(pairs, rows, nnz) for m in (own_msg, other_msg)]
    listed = jnp.concatenate(lists, axis=1).astype(jnp.int32).reshape(pairs * 2 * rows, nnz)
    columns = jnp.arange(total_tiles, dtype=jnp.int32)
    return jnp.any(listed[:, :, None] == columns, axis=1).astype(jnp.int32)


def after(block, *earlier):
    return lax.optimization_barrier((block, *earlier))[0]


def add_kernel(slots, pairs, has_acc, last, slot_ref, mask_ref, *refs):
    count = len(slots)
    refs = list(refs)
    a_refs = [refs.pop(0) for _ in range(count)]
    f_refs = [refs.pop(0) for _ in range(4)]
    couple_ref = refs.pop(0) if last else None
    acc_in = refs.pop(0) if has_acc else None
    outs = [refs.pop(0) for _ in range(2 if last else 1)]
    m_buf, a_buf = refs[:2]
    depth = count * HALF
    for p in range(pairs):
        for n, slot in enumerate(slots):
            a_buf[n * HALF : (n + 1) * HALF, :] = a_refs[n][p * HALF : (p + 1) * HALF, :]
            for q in range(HALF // TILE):
                tile = slot_ref[slot] + q
                col = pl.multiple_of(tile * TILE, TILE)
                for i in range(4):
                    for rt in range(HALF // TILE):
                        keep = mask_ref[p * 4 + (i % 2) * 2 + rt, tile] != 0
                        block = f_refs[i][rt * TILE : (rt + 1) * TILE, pl.ds(col, TILE)]
                        m_buf[
                            i * HALF + rt * TILE : i * HALF + (rt + 1) * TILE,
                            n * HALF + q * TILE : n * HALF + (q + 1) * TILE,
                        ] = jnp.where(keep, block, jnp.zeros_like(block))
        acc = jnp.dot(m_buf[:, :depth], a_buf[:depth, :], preferred_element_type=jnp.float32)
        if has_acc:
            acc = acc_in[p] + acc
        if last:
            lad = acc[2 * HALF :, :].astype(jnp.bfloat16)
            total = acc[: 2 * HALF, :] + jnp.dot(lad, couple_ref[...], preferred_element_type=jnp.float32)
            outs[0][p] = total[:HALF, :]
            outs[1][p] = total[HALF:, :]
        else:
            outs[0][p] = acc


def add_slots(name, slot_tiles, masks, blocks, slots, pairs, mats, acc=None, couple=None):
    width = blocks[0].shape[1]
    last = couple is not None
    smem = pl.BlockSpec(memory_space=pltpu.SMEM)
    vmem = pl.BlockSpec(memory_space=pltpu.VMEM)
    operands = [*blocks, *mats] + ([couple] if last else []) + ([acc] if acc is not None else [])
    wide = jax.ShapeDtypeStruct((pairs, 4 * HALF, width), jnp.float32)
    half = jax.ShapeDtypeStruct((pairs, HALF, width), jnp.float32)
    flops = 2 * pairs * (4 * HALF * len(slots) * HALF * width + (2 * HALF * width * width if last else 0))
    return pl.pallas_call(
        functools.partial(add_kernel, slots, pairs, acc is not None, last),
        out_shape=[half, half] if last else [wide],
        in_specs=[smem, smem] + [vmem] * len(operands),
        out_specs=[vmem] * (2 if last else 1),
        scratch_shapes=[
            pltpu.VMEM((4 * HALF, len(slots) * HALF), jnp.bfloat16),
            pltpu.VMEM((len(slots) * HALF, width), jnp.bfloat16),
        ],
        compiler_params=pltpu.CompilerParams(vmem_limit_bytes=VMEM_LIMIT),
        cost_estimate=pl.CostEstimate(flops=flops, bytes_accessed=1 << 20, transcendentals=0),
        name=name,
    )(slot_tiles, masks, *operands)


def per_device(amps, fock, ladder, couple, tile_list):
    chips = lax.axis_size("virt") // 2
    per_chip = 2 * HALF // TILE
    total_tiles = fock.shape[1] // TILE
    pairs, _, nnz = tile_list.shape
    place = lax.axis_index("virt")
    chip, core = place // 2, place % 2
    way = jnp.where(core == 0, -1, 1)

    hops = jnp.array([0, 1, 1, 2, 2, 3, 3, 4], dtype=jnp.int32)
    other = jnp.array([0, 0, 1, 0, 1, 0, 1, 0], dtype=jnp.int32)
    half_of = jnp.where(other == 1, 1 - core, core)
    slot_tiles = ((chip + way * hops + chips) % chips * per_chip + half_of * (HALF // TILE)).astype(jnp.int32)

    x0 = message(amps, tile_list)
    s0 = core_swap(x0)
    mats = (fock, core_swap(after(fock, s0)), ladder, core_swap(after(ladder, s0)))
    masks = masks_of(x0, s0, pairs, nnz, total_tiles)
    add = functools.partial(add_slots, slot_tiles=slot_tiles, masks=masks, pairs=pairs, mats=mats)

    x1, s1 = ring_step(x0), ring_step(s0)
    x2, s2 = ring_step(x1), ring_step(s1)
    x3, s3 = ring_step(x2), ring_step(s2)
    (part,) = add("first_slots", blocks=[x0, x1, s1, x2], slots=(0, 1, 2, 3))
    x4 = ring_step(after(x3, part))
    (part,) = add("next_slots", blocks=[s2, x3], slots=(4, 5), acc=part)
    own, sib = add("last_slots", blocks=[s3, x4], slots=(6, 7), acc=part, couple=couple)
    half_term = (own + core_swap(sib)).astype(jnp.bfloat16)
    mirrored = mirror_swap(half_term)
    return (half_term.astype(jnp.float32) + mirrored.astype(jnp.float32)).astype(jnp.bfloat16)


def solution(mesh):
    in_specs = (
        P("pair", "virt", None),
        P("virt", None),
        P("virt", None),
        P(),
        P("pair", "virt", None),
    )
    out_specs = P("pair", "virt", None)
    return jax.shard_map(
        per_device, mesh=mesh, in_specs=in_specs, out_specs=out_specs, check_vma=False
    )
```

time: 299 us -> 142 us (0.47)
  the two profiles are of different devices: /device:TPU:28 before, /device:TPU:1 now
where the time goes in v2:
time: 142 us; the launch traced here: 141 us
  waiting for transfers between devices  68.8 us (48%)
  starting transfers between devices  52 us (37%)
  Pallas kernels  12.3 us (9%)
  local copies, waits for them, and re-layouts  4.13 us (3%)
  other arithmetic  3.74 us (3%)
    ppermute x1, waiting for transfers between devices, mirror_swap(): return lax.ppermute(block, 'pair', route)  46.1 us
    ppermute x4, starting transfers between devices, core_swap(): return lax.ppermute(block, 'virt', [(v, v ^ 1) for v in range(count)])  27 us
    ppermute x7, waiting for transfers between devices, ring_step(): return lax.ppermute(block, 'virt', route)  18.9 us
    ppermute x7, starting transfers between devices, ring_step(): return lax.ppermute(block, 'virt', route)  17.2 us
    pallas_call x3, Pallas kernels, add_slots(): pl.pallas_call(functools.partial(add_kernel, slots, pairs, acc is not Non...  12.3 us
    ppermute x1, starting transfers between devices, mirror_swap(): return lax.ppermute(block, 'pair', route)  7.73 us
    ppermute x4, waiting for transfers between devices, core_swap(): return lax.ppermute(block, 'virt', [(v, v ^ 1) for v in range(count)])  3.81 us
    unnamed x12, local copies, waits for them, and re-layouts  3.19 us
  transfers between devices with their start and end apart: 12, of which 8 were waited for; matrix products, arithmetic and copies ran while one was open for 1% of the time, Pallas kernels for 6%

profile of v2, /device:TPU:1, one launch (start us, length us, event | category | flops | bytes accessed | tf_op | source)
XLA Modules:
  0.0 141.2 jit_solution(17838754675160868367)
XLA Ops:
  0.0 0.7 convert_element_type.34
  0.7 0.1 convert_element_type.35
  0.8 1.1 fusion.1.refs_0_
  1.9 16.1 %collective-permute-start = (bf16[528,512]{1,0:T(8,128)(2,1)S(1)}, bf16[528,512]{1,0:T(8,128)(2,1)S(1)}, u32[]{:S(2)}, u32[]{:S(2)}) collective-permute-start(bf16[528,512]{1,0:T(8,128)(2,1)S(1)} %fusion.1.refs_0_), channel_id=1, source_target_pairs={{0,1},{1,0},{2,3},{3,2},{4,5},{5,4},{6,7},{7,6},{8,9},{9,8},{10,11... | collective-permute-start | bytes 1622024 | tf_op jit(solution)/shard_map/ppermute | solution.py:18
  17.9 1.5 %collective-permute-done = bf16[528,512]{1,0:T(8,128)(2,1)S(1)} collective-permute-done((bf16[528,512]{1,0:T(8,128)(2,1)S(1)}, bf16[528,512]{1,0:T(8,128)(2,1)S(1)}, u32[]{:S(2)}, u32[]{:S(2)}) %collective-permute-start) | collective-permute-done | bytes 540704 | tf_op jit(solution)/shard_map/ppermute | solution.py:18
  19.5 2.3 %collective-permute-start.7 = (bf16[256,4096]{1,0:T(8,128)(2,1)}, bf16[256,4096]{1,0:T(8,128)(2,1)S(1)}, u32[]{:S(2)}, u32[]{:S(2)}) collective-permute-start(bf16[256,4096]{1,0:T(8,128)(2,1)} %refs_2_.3), channel_id=1, source_target_pairs={{0,1},{1,0},{2,3},{3,2},{4,5},{5,4},{6,7},{7,6},{8,9},{9,8},{10,11... | collective-permute-start | bytes 6291464 | tf_op jit(solution)/shard_map/ppermute | solution.py:18
  21.7 2.0 %collective-permute-start.8 = (bf16[256,4096]{1,0:T(8,128)(2,1)}, bf16[256,4096]{1,0:T(8,128)(2,1)}, u32[]{:S(2)}, u32[]{:S(2)}) collective-permute-start(bf16[256,4096]{1,0:T(8,128)(2,1)} %refs_4_.5), channel_id=1, source_target_pairs={{0,1},{1,0},{2,3},{3,2},{4,5},{5,4},{6,7},{7,6},{8,9},{9,8},{10,11... | collective-permute-start | bytes 6291464 | tf_op jit(solution)/shard_map/ppermute | solution.py:18
  23.8 1.9 %collective-permute-start.4 = (bf16[528,512]{1,0:T(8,128)(2,1)S(1)}, bf16[528,512]{1,0:T(8,128)(2,1)S(1)}, u32[]{:S(2)}, u32[]{:S(2)}) collective-permute-start(bf16[528,512]{1,0:T(8,128)(2,1)S(1)} %fusion.1.refs_0_), channel_id=1, source_target_pairs={{0,2},{2,4},{4,6},{6,8},{8,10},{10,12},{12,14},{14,0},{1,15},{3,1}... | collective-permute-start | bytes 1622024 | tf_op jit(solution)/shard_map/ppermute | solution.py:25
  25.7 1.9 %collective-permute-start.1 = (bf16[528,512]{1,0:T(8,128)(2,1)S(1)}, bf16[528,512]{1,0:T(8,128)(2,1)}, u32[]{:S(2)}, u32[]{:S(2)}) collective-permute-start(bf16[528,512]{1,0:T(8,128)(2,1)S(1)} %collective-permute-done), channel_id=1, source_target_pairs={{0,2},{2,4},{4,6},{6,8},{8,10},{10,12},{12,14},{14,0},{1,15},{3,1}... | collective-permute-start | bytes 1622024 | tf_op jit(solution)/shard_map/ppermute | solution.py:25
  27.7 6.5 %collective-permute-done.4.refs_1_ = bf16[528,512]{1,0:T(8,128)(2,1)S(1)} collective-permute-done((bf16[528,512]{1,0:T(8,128)(2,1)S(1)}, bf16[528,512]{1,0:T(8,128)(2,1)S(1)}, u32[]{:S(2)}, u32[]{:S(2)}) %collective-permute-start.4) | collective-permute-done | bytes 540704 | tf_op jit(solution)/shard_map/ppermute | solution.py:25
  34.2 2.8 %collective-permute-start.5 = (bf16[528,512]{1,0:T(8,128)(2,1)S(1)}, bf16[528,512]{1,0:T(8,128)(2,1)}, u32[]{:S(2)}, u32[]{:S(2)}) collective-permute-start(bf16[528,512]{1,0:T(8,128)(2,1)S(1)} %collective-permute-done.4.refs_1_), channel_id=1, source_target_pairs={{0,2},{2,4},{4,6},{6,8},{8,10},{10,12},{12,14},{14,0},{1,15},{3,1}... | collective-permute-start | bytes 1622024 | tf_op jit(solution)/shard_map/ppermute | solution.py:25
  37.0 3.1 %collective-permute-done.1.refs_2_ = bf16[528,512]{1,0:T(8,128)(2,1)} collective-permute-done((bf16[528,512]{1,0:T(8,128)(2,1)S(1)}, bf16[528,512]{1,0:T(8,128)(2,1)}, u32[]{:S(2)}, u32[]{:S(2)}) %collective-permute-start.1) | collective-permute-done | bytes 540704 | tf_op jit(solution)/shard_map/ppermute | solution.py:25
  40.1 2.8 %collective-permute-start.2 = (bf16[528,512]{1,0:T(8,128)(2,1)}, bf16[528,512]{1,0:T(8,128)(2,1)}, u32[]{:S(2)}, u32[]{:S(2)}) collective-permute-start(bf16[528,512]{1,0:T(8,128)(2,1)} %collective-permute-done.1.refs_2_), channel_id=1, source_target_pairs={{0,2},{2,4},{4,6},{6,8},{8,10},{10,12},{12,14},{14,0},{1,15},{3,1}... | collective-permute-start | bytes 1622024 | tf_op jit(solution)/shard_map/ppermute | solution.py:25
  43.0 2.9 %collective-permute-done.5.refs_3_ = bf16[528,512]{1,0:T(8,128)(2,1)} collective-permute-done((bf16[528,512]{1,0:T(8,128)(2,1)S(1)}, bf16[528,512]{1,0:T(8,128)(2,1)}, u32[]{:S(2)}, u32[]{:S(2)}) %collective-permute-start.5) | collective-permute-done | bytes 540704 | tf_op jit(solution)/shard_map/ppermute | solution.py:25
  45.9 2.8 %collective-permute-start.6 = (bf16[528,512]{1,0:T(8,128)(2,1)}, bf16[528,512]{1,0:T(8,128)(2,1)}, u32[]{:S(2)}, u32[]{:S(2)}) collective-permute-start(bf16[528,512]{1,0:T(8,128)(2,1)} %collective-permute-done.5.refs_3_), channel_id=1, source_target_pairs={{0,2},{2,4},{4,6},{6,8},{8,10},{10,12},{12,14},{14,0},{1,15},{3,1}... | collective-permute-start | bytes 1622024 | tf_op jit(solution)/shard_map/ppermute | solution.py:25
  48.7 0.7 fusion.4.slot_ref
  49.4 0.7 slice.5
  50.4 1.3 collective-permute-done.2.refs_0_
  51.7 2.9 %collective-permute-start.3 = (bf16[528,512]{1,0:T(8,128)(2,1)}, bf16[528,512]{1,0:T(8,128)(2,1)S(1)}, u32[]{:S(2)}, u32[]{:S(2)}) collective-permute-start(bf16[528,512]{1,0:T(8,128)(2,1)} %collective-permute-done.2.refs_0_), channel_id=1, source_target_pairs={{0,2},{2,4},{4,6},{6,8},{8,10},{10,12},{12,14},{14,0},{1,15},{3,1}... | collective-permute-start | bytes 1622024 | tf_op jit(solution)/shard_map/ppermute | solution.py:25
  54.6 1.6 %copy-done = bf16[256,4096]{1,0:T(8,128)(2,1)S(1)} copy-done((bf16[256,4096]{1,0:T(8,128)(2,1)S(1)}, bf16[256,4096]{1,0:T(8,128)(2,1)}, u32[]{:S(2)}) %copy-start) | copy-done | bytes 2097176
  56.2 1.6 %copy-done.2 = bf16[256,4096]{1,0:T(8,128)(2,1)S(1)} copy-done((bf16[256,4096]{1,0:T(8,128)(2,1)S(1)}, bf16[256,4096]{1,0:T(8,128)(2,1)}, u32[]{:S(2)}) %copy-start.2) | copy-done | bytes 2097176
  57.8 5.0 %first_slots.1.refs_6_ = f32[2,1024,512]{2,1,0:T(8,128)S(1)} custom-call(s32[8]{0:T(128)S(1)} %fusion.4.slot_ref, s32[8,32]{1,0:T(8,128)S(1)} %convert_element_type.38.mask_ref, bf16[528,512]{1,0:T(8,128)(2,1)S(1)} %fusion.1.refs_0_, bf16[528,512]{1,0:T(8,128)(2,1)S(1)} %collective-permute-done.4.refs_1_, bf16[528,512]{1,0:T(8,128)(2,1)} %collective-permute-done.1.refs_2_, ...), custom_call_target="tpu_custom_call" | custom-call | flops 2147483648 | bytes 1048576 | tf_op jit(solution)/shard_map/first_slots/pallas_call | solution.py:102
  62.8 2.1 %collective-permute-start.9 = (bf16[528,512]{1,0:T(8,128)(2,1)}, bf16[528,512]{1,0:T(8,128)(2,1)S(1)}, u32[]{:S(2)}, u32[]{:S(2)}) collective-permute-start(bf16[528,512]{1,0:T(8,128)(2,1)} %collective-permute-done.6.refs_1_), channel_id=1, source_target_pairs={{0,2},{2,4},{4,6},{6,8},{8,10},{10,12},{12,14},{14,0},{1,15},{3,1}... | collective-permute-start | bytes 1622024 | tf_op jit(solution)/shard_map/ppermute | solution.py:25
  64.9 3.6 %next_slots.1.refs_7_ = f32[2,1024,512]{2,1,0:T(8,128)S(1)} custom-call(s32[8]{0:T(128)S(1)} %fusion.4.slot_ref, s32[8,32]{1,0:T(8,128)S(1)} %convert_element_type.38.mask_ref, bf16[528,512]{1,0:T(8,128)(2,1)} %collective-permute-done.2.refs_0_, bf16[528,512]{1,0:T(8,128)(2,1)} %collective-permute-done.6.refs_1_, bf16[256,4096]{1,0:T(8,128)(2,1)S(1)} %copy-done.1, ...), custom_call_target="tpu_custom_call" | custom-call | flops 1073741824 | bytes 1048576 | tf_op jit(solution)/shard_map/next_slots/pallas_call | solution.py:102
  68.5 5.1 %collective-permute-done.9.refs_1_ = bf16[528,512]{1,0:T(8,128)(2,1)S(1)} collective-permute-done((bf16[528,512]{1,0:T(8,128)(2,1)}, bf16[528,512]{1,0:T(8,128)(2,1)S(1)}, u32[]{:S(2)}, u32[]{:S(2)}) %collective-permute-start.9) | collective-permute-done | bytes 540704 | tf_op jit(solution)/shard_map/ppermute | solution.py:25
  73.5 3.7 %last_slots.1 = (f32[2,256,512]{2,1,0:T(8,128)S(1)}, f32[2,256,512]{2,1,0:T(8,128)S(1)}) custom-call(s32[8]{0:T(128)S(1)} %fusion.4.slot_ref, s32[8,32]{1,0:T(8,128)S(1)} %convert_element_type.38.mask_ref, bf16[528,512]{1,0:T(8,128)(2,1)S(1)} %collective-permute-done.3.refs_0_, bf16[528,512]{1,0:T(8,128)(2,1)S(1)} %collective-permute-done.9.refs_1_, ...), custom_call_target="tpu_custom_call" | custom-call | flops 1610612736 | bytes 1048576 | tf_op jit(solution)/shard_map/last_slots/pallas_call | solution.py:102
  77.3 6.6 %collective-permute-start.10 = (f32[2,256,512]{2,1,0:T(8,128)S(1)}, f32[2,256,512]{2,1,0:T(8,128)S(1)}, u32[]{:S(2)}, u32[]{:S(2)}) collective-permute-start(f32[2,256,512]{2,1,0:T(8,128)S(1)} %get-tuple-element.14), channel_id=1, source_target_pairs={{0,1},{1,0},{2,3},{3,2},{4,5},{5,4},{6,7},{7,6},{8,9},{9,8},{10,11... | collective-permute-start | bytes 3145736 | tf_op jit(solution)/shard_map/ppermute | solution.py:18
  83.9 2.3 %collective-permute-done.10 = f32[2,256,512]{2,1,0:T(8,128)S(1)} collective-permute-done((f32[2,256,512]{2,1,0:T(8,128)S(1)}, f32[2,256,512]{2,1,0:T(8,128)S(1)}, u32[]{:S(2)}, u32[]{:S(2)}) %collective-permute-start.10) | collective-permute-done | bytes 1048608 | tf_op jit(solution)/shard_map/ppermute | solution.py:18
  86.1 0.3 add_convert_fusion.1
  86.4 7.7 %collective-permute-start.11 = (bf16[2,256,512]{2,1,0:T(8,128)(2,1)S(1)}, bf16[2,256,512]{2,1,0:T(8,128)(2,1)S(1)}, u32[]{:S(2)}, u32[]{:S(2)}) collective-permute-start(bf16[2,256,512]{2,1,0:T(8,128)(2,1)S(1)} %add_convert_fusion.1), channel_id=1, source_target_pairs={{0,1008},{16,496},{32,752},{48,240},{64,880},{80,368},{96,624},{11... | collective-permute-start | bytes 1572872 | tf_op jit(solution)/shard_map/ppermute | solution.py:35
  94.1 46.1 %collective-permute-done.11 = bf16[2,256,512]{2,1,0:T(8,128)(2,1)S(1)} collective-permute-done((bf16[2,256,512]{2,1,0:T(8,128)(2,1)S(1)}, bf16[2,256,512]{2,1,0:T(8,128)(2,1)S(1)}, u32[]{:S(2)}, u32[]{:S(2)}) %collective-permute-start.11) | collective-permute-done | bytes 524320 | tf_op jit(solution)/shard_map/ppermute | solution.py:35
  140.2 0.9 add_convert_fusion
  (20 shorter events, 0.3 us)
Async XLA Ops:
  1.9 17.6 %collective-permute-start = (bf16[528,512]{1,0:T(8,128)(2,1)S(1)}, bf16[528,512]{1,0:T(8,128)(2,1)S(1)}, u32[]{:S(2)}, u32[]{:S(2)}) collective-permute-start(bf16[528,512]{1,0:T(8,128)(2,1)S(1)} %fusion.1.refs_0_), channel_id=1, source_target_pairs={{0,1},{1,0},{2,3},{3,2},{4,5},{5,4},{6,7},{7,6},{8,9},{9,8},{10,11... | collective-permute-start | bytes 1622024 | tf_op jit(solution)/shard_map/ppermute | solution.py:18
  19.5 14.7 %copy-start.5 = (bf16[528,512]{1,0:T(8,128)(2,1)}, bf16[528,512]{1,0:T(8,128)(2,1)S(1)}, u32[]{:S(2)}) copy-start(bf16[528,512]{1,0:T(8,128)(2,1)S(1)} %collective-permute-done) | copy-start | bytes 1622020
  19.5 35.1 %collective-permute-start.7 = (bf16[256,4096]{1,0:T(8,128)(2,1)}, bf16[256,4096]{1,0:T(8,128)(2,1)S(1)}, u32[]{:S(2)}, u32[]{:S(2)}) collective-permute-start(bf16[256,4096]{1,0:T(8,128)(2,1)} %refs_2_.3), channel_id=1, source_target_pairs={{0,1},{1,0},{2,3},{3,2},{4,5},{5,4},{6,7},{7,6},{8,9},{9,8},{10,11... | collective-permute-start | bytes 6291464 | tf_op jit(solution)/shard_map/ppermute | solution.py:18
  21.7 32.8 %collective-permute-start.8 = (bf16[256,4096]{1,0:T(8,128)(2,1)}, bf16[256,4096]{1,0:T(8,128)(2,1)}, u32[]{:S(2)}, u32[]{:S(2)}) collective-permute-start(bf16[256,4096]{1,0:T(8,128)(2,1)} %refs_4_.5), channel_id=1, source_target_pairs={{0,1},{1,0},{2,3},{3,2},{4,5},{5,4},{6,7},{7,6},{8,9},{9,8},{10,11... | collective-permute-start | bytes 6291464 | tf_op jit(solution)/shard_map/ppermute | solution.py:18
  23.8 10.4 %collective-permute-start.4 = (bf16[528,512]{1,0:T(8,128)(2,1)S(1)}, bf16[528,512]{1,0:T(8,128)(2,1)S(1)}, u32[]{:S(2)}, u32[]{:S(2)}) collective-permute-start(bf16[528,512]{1,0:T(8,128)(2,1)S(1)} %fusion.1.refs_0_), channel_id=1, source_target_pairs={{0,2},{2,4},{4,6},{6,8},{8,10},{10,12},{12,14},{14,0},{1,15},{3,1}... | collective-permute-start | bytes 1622024 | tf_op jit(solution)/shard_map/ppermute | solution.py:25
  25.7 14.4 %collective-permute-start.1 = (bf16[528,512]{1,0:T(8,128)(2,1)S(1)}, bf16[528,512]{1,0:T(8,128)(2,1)}, u32[]{:S(2)}, u32[]{:S(2)}) collective-permute-start(bf16[528,512]{1,0:T(8,128)(2,1)S(1)} %collective-permute-done), channel_id=1, source_target_pairs={{0,2},{2,4},{4,6},{6,8},{8,10},{10,12},{12,14},{14,0},{1,15},{3,1}... | collective-permute-start | bytes 1622024 | tf_op jit(solution)/shard_map/ppermute | solution.py:25
  34.2 11.7 %collective-permute-start.5 = (bf16[528,512]{1,0:T(8,128)(2,1)S(1)}, bf16[528,512]{1,0:T(8,128)(2,1)}, u32[]{:S(2)}, u32[]{:S(2)}) collective-permute-start(bf16[528,512]{1,0:T(8,128)(2,1)S(1)} %collective-permute-done.4.refs_1_), channel_id=1, source_target_pairs={{0,2},{2,4},{4,6},{6,8},{8,10},{10,12},{12,14},{14,0},{1,15},{3,1}... | collective-permute-start | bytes 1622024 | tf_op jit(solution)/shard_map/ppermute | solution.py:25
  40.1 11.6 %collective-permute-start.2 = (bf16[528,512]{1,0:T(8,128)(2,1)}, bf16[528,512]{1,0:T(8,128)(2,1)}, u32[]{:S(2)}, u32[]{:S(2)}) collective-permute-start(bf16[528,512]{1,0:T(8,128)(2,1)} %collective-permute-done.1.refs_2_), channel_id=1, source_target_pairs={{0,2},{2,4},{4,6},{6,8},{8,10},{10,12},{12,14},{14,0},{1,15},{3,1}... | collective-permute-start | bytes 1622024 | tf_op jit(solution)/shard_map/ppermute | solution.py:25
  45.9 16.9 %collective-permute-start.6 = (bf16[528,512]{1,0:T(8,128)(2,1)}, bf16[528,512]{1,0:T(8,128)(2,1)}, u32[]{:S(2)}, u32[]{:S(2)}) collective-permute-start(bf16[528,512]{1,0:T(8,128)(2,1)} %collective-permute-done.5.refs_3_), channel_id=1, source_target_pairs={{0,2},{2,4},{4,6},{6,8},{8,10},{10,12},{12,14},{14,0},{1,15},{3,1}... | collective-permute-start | bytes 1622024 | tf_op jit(solution)/shard_map/ppermute | solution.py:25
  51.7 16.8 %collective-permute-start.3 = (bf16[528,512]{1,0:T(8,128)(2,1)}, bf16[528,512]{1,0:T(8,128)(2,1)S(1)}, u32[]{:S(2)}, u32[]{:S(2)}) collective-permute-start(bf16[528,512]{1,0:T(8,128)(2,1)} %collective-permute-done.2.refs_0_), channel_id=1, source_target_pairs={{0,2},{2,4},{4,6},{6,8},{8,10},{10,12},{12,14},{14,0},{1,15},{3,1}... | collective-permute-start | bytes 1622024 | tf_op jit(solution)/shard_map/ppermute | solution.py:25
  54.6 1.6 %copy-start = (bf16[256,4096]{1,0:T(8,128)(2,1)S(1)}, bf16[256,4096]{1,0:T(8,128)(2,1)}, u32[]{:S(2)}) copy-start(bf16[256,4096]{1,0:T(8,128)(2,1)} %refs_2_.3) | copy-start | bytes 6291460
  56.2 1.6 %copy-start.2 = (bf16[256,4096]{1,0:T(8,128)(2,1)S(1)}, bf16[256,4096]{1,0:T(8,128)(2,1)}, u32[]{:S(2)}) copy-start(bf16[256,4096]{1,0:T(8,128)(2,1)} %refs_4_.5) | copy-start | bytes 6291460
  57.8 7.1 %copy-start.1 = (bf16[256,4096]{1,0:T(8,128)(2,1)S(1)}, bf16[256,4096]{1,0:T(8,128)(2,1)}, u32[]{:S(2)}) copy-start(bf16[256,4096]{1,0:T(8,128)(2,1)} %refs_2_.3) | copy-start | bytes 6291460
  57.8 7.1 %copy-start.3 = (bf16[256,4096]{1,0:T(8,128)(2,1)S(1)}, bf16[256,4096]{1,0:T(8,128)(2,1)}, u32[]{:S(2)}) copy-start(bf16[256,4096]{1,0:T(8,128)(2,1)} %refs_4_.5) | copy-start | bytes 6291460
  62.8 10.8 %copy-start.4 = (bf16[512,512]{1,0:T(8,128)(2,1)S(1)}, bf16[512,512]{1,0:T(8,128)(2,1)}, u32[]{:S(2)}) copy-start(bf16[512,512]{1,0:T(8,128)(2,1)} %refs_6_.3) | copy-start | bytes 1572868
  62.8 10.7 %collective-permute-start.9 = (bf16[528,512]{1,0:T(8,128)(2,1)}, bf16[528,512]{1,0:T(8,128)(2,1)S(1)}, u32[]{:S(2)}, u32[]{:S(2)}) collective-permute-start(bf16[528,512]{1,0:T(8,128)(2,1)} %collective-permute-done.6.refs_1_), channel_id=1, source_target_pairs={{0,2},{2,4},{4,6},{6,8},{8,10},{10,12},{12,14},{14,0},{1,15},{3,1}... | collective-permute-start | bytes 1622024 | tf_op jit(solution)/shard_map/ppermute | solution.py:25
  77.3 8.9 %collective-permute-start.10 = (f32[2,256,512]{2,1,0:T(8,128)S(1)}, f32[2,256,512]{2,1,0:T(8,128)S(1)}, u32[]{:S(2)}, u32[]{:S(2)}) collective-permute-start(f32[2,256,512]{2,1,0:T(8,128)S(1)} %get-tuple-element.14), channel_id=1, source_target_pairs={{0,1},{1,0},{2,3},{3,2},{4,5},{5,4},{6,7},{7,6},{8,9},{9,8},{10,11... | collective-permute-start | bytes 3145736 | tf_op jit(solution)/shard_map/ppermute | solution.py:18
  86.4 53.8 %collective-permute-start.11 = (bf16[2,256,512]{2,1,0:T(8,128)(2,1)S(1)}, bf16[2,256,512]{2,1,0:T(8,128)(2,1)S(1)}, u32[]{:S(2)}, u32[]{:S(2)}) collective-permute-start(bf16[2,256,512]{2,1,0:T(8,128)(2,1)S(1)} %add_convert_fusion.1), channel_id=1, source_target_pairs={{0,1008},{16,496},{32,752},{48,240},{64,880},{80,368},{96,624},{11... | collective-permute-start | bytes 1572872 | tf_op jit(solution)/shard_map/ppermute | solution.py:35

commit v3 on v0

v3 whole, which is shorter than its diff:
```python
import functools

import jax
import jax.numpy as jnp
from jax import lax
from jax.experimental import pallas as pl
from jax.experimental.pallas import tpu as pltpu
from jax.sharding import PartitionSpec as P

TILE = 128
HALF = 256
SPLIT = HALF // TILE
VMEM_LIMIT = 24 * 1024 * 1024
HOPS = (None, (0, 0), (1, 0), (1, 1), (2, 0), (2, 1), (3, 0), (3, 1), (4, 0))
ORDER = (1, 2, 3, -1, -2, -3, 4, 5, -4, -5, 6, -6, -7, 7, 8, -8)


def core_swap(block):
    count = lax.axis_size("virt")
    return lax.ppermute(block, "virt", [(v, v ^ 1) for v in range(count)])


def ring_step(block, cross=0):
    chips = lax.axis_size("virt") // 2
    route = [(2 * c + cross, 2 * ((c + 1) % chips)) for c in range(chips)]
    route += [(2 * c + 1 - cross, 2 * ((c - 1) % chips) + 1) for c in range(chips)]
    return lax.ppermute(block, "virt", route)


def mirror_swap(block):
    count = lax.axis_size("pair")
    nbits = count.bit_length() - 1
    route = []
    for low in range(count):
        flipped = sum(((low >> b) & 1) << (nbits - 1 - b) for b in range(nbits))
        route.append((low, count - 1 - flipped))
    return lax.ppermute(block, "pair", route)


def after(block, *earlier):
    return lax.optimization_barrier((block, *earlier))[0]


def screen_kernel(pairs, slot_ref, mask_ref, fock, ladder, out_ref, buf, sem):
    count = buf.shape[1]

    def copies(n):
        col = pl.multiple_of(slot_ref[n] * TILE, HALF)
        return [
            pltpu.make_async_copy(mat.at[:, pl.ds(col, HALF)], buf.at[i, n], sem.at[i, n])
            for i, mat in enumerate((fock, ladder))
        ]

    jobs = [copies(n) for n in range(count)]
    for job in jobs:
        for copy in job:
            copy.start()
    for n, job in enumerate(jobs):
        for i, copy in enumerate(job):
            copy.wait()
            for r in range(SPLIT):
                for q in range(SPLIT):
                    block = buf[i, n, r * TILE : (r + 1) * TILE, q * TILE : (q + 1) * TILE]
                    for p in range(pairs):
                        keep = mask_ref[p * SPLIT + r, slot_ref[n] + q] != 0
                        out_ref[
                            p,
                            i * HALF + r * TILE : i * HALF + (r + 1) * TILE,
                            n * HALF + q * TILE : n * HALF + (q + 1) * TILE,
                        ] = jnp.where(keep, block, jnp.zeros_like(block))


def screened(slot_tiles, masks, fock, ladder, pairs):
    smem = pl.BlockSpec(memory_space=pltpu.SMEM)
    anywhere = pl.BlockSpec(memory_space=pl.ANY)
    count, dtype = slot_tiles.shape[0], fock.dtype
    return pl.pallas_call(
        functools.partial(screen_kernel, pairs),
        out_shape=jax.ShapeDtypeStruct((pairs, 2 * HALF, count * HALF), dtype),
        in_specs=[smem, smem, anywhere, anywhere],
        out_specs=pl.BlockSpec(memory_space=pltpu.VMEM),
        scratch_shapes=[pltpu.VMEM((2, count, HALF, HALF), dtype), pltpu.SemaphoreType.DMA((2, count))],
        compiler_params=pltpu.CompilerParams(vmem_limit_bytes=VMEM_LIMIT),
        cost_estimate=pl.CostEstimate(flops=0, bytes_accessed=4 << 20, transcendentals=0),
        name="screened",
    )(slot_tiles, masks, fock, ladder)


def sum_kernel(pairs, slots, has_acc, finish, *refs):
    refs = list(refs)
    take = lambda n: [refs.pop(0) for _ in range(n)]
    mat, blocks = take(1)[0], take(len(slots))
    acc_in = take(1)[0] if has_acc else None
    couple_ref = take(1)[0] if finish else None
    out, a_buf = refs
    lo, depth = slots[0] * HALF, len(slots) * HALF
    for p in range(pairs):
        for n, block in enumerate(blocks):
            a_buf[n * HALF : (n + 1) * HALF, :] = block[p]
        acc = jnp.dot(mat[p, :, lo : lo + depth], a_buf[...], preferred_element_type=jnp.float32)
        if has_acc:
            acc = acc_in[p] + acc
        if finish:
            lad = acc[HALF:, :].astype(jnp.bfloat16)
            acc = acc[:HALF, :] + jnp.dot(lad, couple_ref[...], preferred_element_type=jnp.float32)
        out[p] = acc.astype(out.dtype)


def sum_slots(name, mat, blocks, first, acc=None, couple=None):
    pairs, _, width = blocks[0].shape
    slots, finish = tuple(range(first, first + len(blocks))), couple is not None
    vmem = pl.BlockSpec(memory_space=pltpu.VMEM)
    operands = [mat, *blocks] + ([acc] if acc is not None else []) + ([couple] if finish else [])
    out_shape = jax.ShapeDtypeStruct((pairs, HALF if finish else 2 * HALF, width), jnp.bfloat16 if finish else jnp.float32)
    flops = 2 * pairs * 2 * HALF * width * (len(slots) * HALF + (width // 2 if finish else 0))
    return pl.pallas_call(
        functools.partial(sum_kernel, pairs, slots, acc is not None, finish),
        out_shape=out_shape,
        in_specs=[vmem] * len(operands),
        out_specs=vmem,
        scratch_shapes=[pltpu.VMEM((len(slots) * HALF, width), blocks[0].dtype)],
        compiler_params=pltpu.CompilerParams(vmem_limit_bytes=VMEM_LIMIT),
        cost_estimate=pl.CostEstimate(flops=flops, bytes_accessed=1 << 20, transcendentals=0),
        name=name,
    )(*operands)


def per_device(amps, fock, ladder, couple, tile_list):
    chips = lax.axis_size("virt") // 2
    total_tiles = fock.shape[1] // TILE
    pairs, _, nnz = tile_list.shape
    place = lax.axis_index("virt")
    chip, core = place // 2, place % 2

    hops = jnp.array([HOPS[abs(n)][0] * (-1 if n < 0 else 1) for n in ORDER], dtype=jnp.int32)
    other = jnp.array([HOPS[abs(n)][1] ^ (n < 0) for n in ORDER], dtype=jnp.int32)
    way = jnp.where(core == 0, -1, 1)
    half_of = jnp.where(other == 1, 1 - core, core)
    slot_tiles = ((chip + way * hops + chips) % chips * 2 * SPLIT + half_of * SPLIT).astype(jnp.int32)
    columns = jnp.arange(total_tiles, dtype=jnp.int32)
    masks = jnp.any(tile_list.reshape(pairs * SPLIT, nnz)[:, :, None] == columns, axis=1).astype(jnp.int32)

    x0 = amps
    x1, s1 = ring_step(x0), ring_step(x0, cross=1)
    mat = screened(slot_tiles, masks, fock, ladder, pairs)
    x2, s2 = ring_step(after(x1, mat)), ring_step(s1)
    acc = sum_slots("sum_1", mat, (x0, x1, s1, core_swap(x0)), 0)
    x3, s3 = ring_step(after(x2, acc)), ring_step(s2)
    acc = sum_slots("sum_2", mat, (core_swap(x1), core_swap(s1), x2, s2), 4, acc)
    x4 = ring_step(after(x3, acc))
    acc = sum_slots("sum_3", mat, (core_swap(x2), core_swap(s2), x3), 8, acc)
    acc = sum_slots("sum_4", mat, (core_swap(x3), core_swap(after(s3, acc)), s3, x4), 11, acc)
    half_term = sum_slots("sum_5", mat, (core_swap(x4),), 15, acc, couple)
    mirrored = mirror_swap(half_term)
    return (half_term.astype(jnp.float32) + mirrored.astype(jnp.float32)).astype(jnp.bfloat16)


def solution(mesh):
    in_specs = (
        P("pair", "virt", None),
        P("virt", None),
        P("virt", None),
        P(),
        P("pair", "virt", None),
    )
    out_specs = P("pair", "virt", None)
    return jax.shard_map(
        per_device, mesh=mesh, in_specs=in_specs, out_specs=out_specs, check_vma=False
    )
```

time: 299 us -> 130 us (0.43)
  the two profiles are of different devices: /device:TPU:28 before, /device:TPU:1 now
where the time goes in v3:
time: 130 us; the launch traced here: 129 us
  starting transfers between devices  64.8 us (50%)
  waiting for transfers between devices  49.1 us (38%)
  Pallas kernels  9.5 us (7%)
  local copies, waits for them, and re-layouts  3.96 us (3%)
  other arithmetic  1.71 us (1%)
    ppermute x1, waiting for transfers between devices, mirror_swap(): return lax.ppermute(block, 'pair', route)  46.1 us
    ppermute x8, starting transfers between devices, core_swap(): return lax.ppermute(block, 'virt', [(v, v ^ 1) for v in range(count)])  31.6 us
    ppermute x7, starting transfers between devices, ring_step(): return lax.ppermute(block, 'virt', route)  23.7 us
    ppermute x1, starting transfers between devices, mirror_swap(): return lax.ppermute(block, 'pair', route)  9.48 us
    pallas_call x5, Pallas kernels, sum_slots(): pl.pallas_call(functools.partial(sum_kernel, pairs, slots, acc is not Non...  5.59 us
    pallas_call x1, Pallas kernels, screened(): pl.pallas_call(functools.partial(screen_kernel, pairs), out_shape=jax.Sha...  3.91 us
    unnamed x8, local copies, waits for them, and re-layouts  3.19 us
    ppermute x7, waiting for transfers between devices, ring_step(): return lax.ppermute(block, 'virt', route)  2.73 us
  transfers between devices with their start and end apart: 16, of which 3 were waited for; matrix products, arithmetic and copies ran while one was open for 1% of the time, Pallas kernels for 7%

profile of v3, /device:TPU:1, one launch (start us, length us, event | category | flops | bytes accessed | tf_op | source)
XLA Modules:
  0.0 129.4 jit_solution(9815407569041769837)
XLA Ops:
  0.0 5.9 %collective-permute-start = (bf16[2,256,512]{2,1,0:T(8,128)(2,1)}, bf16[2,256,512]{2,1,0:T(8,128)(2,1)S(1)}, u32[]{:S(2)}, u32[]{:S(2)}) collective-permute-start(bf16[2,256,512]{2,1,0:T(8,128)(2,1)} %refs_1_.1), channel_id=1, source_target_pairs={{0,2},{2,4},{4,6},{6,8},{8,10},{10,12},{12,14},{14,0},{1,15},{3,1}... | collective-permute-start | bytes 1572872 | tf_op jit(solution)/shard_map/ppermute | solution.py:27
  5.9 2.2 %collective-permute-start.2 = (bf16[2,256,512]{2,1,0:T(8,128)(2,1)}, bf16[2,256,512]{2,1,0:T(8,128)(2,1)S(1)}, u32[]{:S(2)}, u32[]{:S(2)}) collective-permute-start(bf16[2,256,512]{2,1,0:T(8,128)(2,1)} %refs_1_.1), channel_id=1, source_target_pairs={{1,2},{3,4},{5,6},{7,8},{9,10},{11,12},{13,14},{15,0},{0,15},{2,1}... | collective-permute-start | bytes 1572872 | tf_op jit(solution)/shard_map/ppermute | solution.py:27
  8.1 11.8 %collective-permute-start.3 = (bf16[2,256,512]{2,1,0:T(8,128)(2,1)}, bf16[2,256,512]{2,1,0:T(8,128)(2,1)S(1)}, u32[]{:S(2)}, u32[]{:S(2)}) collective-permute-start(bf16[2,256,512]{2,1,0:T(8,128)(2,1)} %refs_1_.1), channel_id=1, source_target_pairs={{0,1},{1,0},{2,3},{3,2},{4,5},{5,4},{6,7},{7,6},{8,9},{9,8},{10,11... | collective-permute-start | bytes 1572872 | tf_op jit(solution)/shard_map/ppermute | solution.py:20
  19.9 0.7 fusion.2.slot_ref
  20.6 0.8 copy.8
  21.4 0.1 fusion
  21.5 0.0 copy-start
  21.5 1.6 %copy-done = bf16[256,4096]{1,0:T(8,128)(2,1)S(1)} copy-done((bf16[256,4096]{1,0:T(8,128)(2,1)S(1)}, bf16[256,4096]{1,0:T(8,128)(2,1)}, u32[]{:S(2)}) %copy-start) | copy-done | bytes 2097176
  23.1 1.6 %copy-done.1 = bf16[256,4096]{1,0:T(8,128)(2,1)S(1)} copy-done((bf16[256,4096]{1,0:T(8,128)(2,1)S(1)}, bf16[256,4096]{1,0:T(8,128)(2,1)}, u32[]{:S(2)}) %copy-start.1) | copy-done | bytes 2097176
  24.7 3.9 %screened.1.refs_0_ = bf16[2,512,4096]{2,1,0:T(8,128)(2,1)S(1)} custom-call(s32[16]{0:T(128)S(1)} %fusion.2.slot_ref, s32[4,32]{1,0:T(4,128)S(1)} %convert_element_type.12.mask_ref, bf16[256,4096]{1,0:T(8,128)(2,1)S(1)} %copy-done, bf16[256,4096]{1,0:T(8,128)(2,1)S(1)} %copy-done.1), custom_call_target="tpu_custom_call" | custom-call | bytes 4194304 | tf_op jit(solution)/shard_map/screened/pallas_call | solution.py:77
  28.6 4.9 %collective-permute-start.1 = (bf16[2,256,512]{2,1,0:T(8,128)(2,1)S(1)}, bf16[2,256,512]{2,1,0:T(8,128)(2,1)S(1)}, u32[]{:S(2)}, u32[]{:S(2)}) collective-permute-start(bf16[2,256,512]{2,1,0:T(8,128)(2,1)S(1)} %collective-permute-done.refs_2_), channel_id=1, source_target_pairs={{0,2},{2,4},{4,6},{6,8},{8,10},{10,12},{12,14},{14,0},{1,15},{3,1}... | collective-permute-start | bytes 1572872 | tf_op jit(solution)/shard_map/ppermute | solution.py:27
  33.5 3.3 %collective-permute-start.7 = (bf16[2,256,512]{2,1,0:T(8,128)(2,1)S(1)}, bf16[2,256,512]{2,1,0:T(8,128)(2,1)S(1)}, u32[]{:S(2)}, u32[]{:S(2)}) collective-permute-start(bf16[2,256,512]{2,1,0:T(8,128)(2,1)S(1)} %collective-permute-done.2.refs_3_), channel_id=1, source_target_pairs={{0,2},{2,4},{4,6},{6,8},{8,10},{10,12},{12,14},{14,0},{1,15},{3,1}... | collective-permute-start | bytes 1572872 | tf_op jit(solution)/shard_map/ppermute | solution.py:27
  36.8 1.9 %collective-permute-start.5 = (bf16[2,256,512]{2,1,0:T(8,128)(2,1)S(1)}, bf16[2,256,512]{2,1,0:T(8,128)(2,1)S(1)}, u32[]{:S(2)}, u32[]{:S(2)}) collective-permute-start(bf16[2,256,512]{2,1,0:T(8,128)(2,1)S(1)} %collective-permute-done.refs_2_), channel_id=1, source_target_pairs={{0,1},{1,0},{2,3},{3,2},{4,5},{5,4},{6,7},{7,6},{8,9},{9,8},{10,11... | collective-permute-start | bytes 1572872 | tf_op jit(solution)/shard_map/ppermute | solution.py:20
  38.7 2.4 %collective-permute-start.6 = (bf16[2,256,512]{2,1,0:T(8,128)(2,1)S(1)}, bf16[2,256,512]{2,1,0:T(8,128)(2,1)S(1)}, u32[]{:S(2)}, u32[]{:S(2)}) collective-permute-start(bf16[2,256,512]{2,1,0:T(8,128)(2,1)S(1)} %collective-permute-done.2.refs_3_), channel_id=1, source_target_pairs={{0,1},{1,0},{2,3},{3,2},{4,5},{5,4},{6,7},{7,6},{8,9},{9,8},{10,11... | collective-permute-start | bytes 1572872 | tf_op jit(solution)/shard_map/ppermute | solution.py:20
  41.1 1.2 sum_1.1.refs_5_
  42.4 2.3 %collective-permute-start.4 = (bf16[2,256,512]{2,1,0:T(8,128)(2,1)S(1)}, bf16[2,256,512]{2,1,0:T(8,128)(2,1)S(1)}, u32[]{:S(2)}, u32[]{:S(2)}) collective-permute-start(bf16[2,256,512]{2,1,0:T(8,128)(2,1)S(1)} %collective-permute-done.1.refs_3_), channel_id=1, source_target_pairs={{0,2},{2,4},{4,6},{6,8},{8,10},{10,12},{12,14},{14,0},{1,15},{3,1}... | collective-permute-start | bytes 1572872 | tf_op jit(solution)/shard_map/ppermute | solution.py:27
  44.7 2.3 %collective-permute-start.12 = (bf16[2,256,512]{2,1,0:T(8,128)(2,1)S(1)}, bf16[2,256,512]{2,1,0:T(8,128)(2,1)S(1)}, u32[]{:S(2)}, u32[]{:S(2)}) collective-permute-start(bf16[2,256,512]{2,1,0:T(8,128)(2,1)S(1)} %collective-permute-done.1.refs_3_), channel_id=1, source_target_pairs={{0,1},{1,0},{2,3},{3,2},{4,5},{5,4},{6,7},{7,6},{8,9},{9,8},{10,11... | collective-permute-start | bytes 1572872 | tf_op jit(solution)/shard_map/ppermute | solution.py:20
  47.0 3.7 %collective-permute-start.13 = (bf16[2,256,512]{2,1,0:T(8,128)(2,1)S(1)}, bf16[2,256,512]{2,1,0:T(8,128)(2,1)S(1)}, u32[]{:S(2)}, u32[]{:S(2)}) collective-permute-start(bf16[2,256,512]{2,1,0:T(8,128)(2,1)S(1)} %collective-permute-done.7.refs_4_), channel_id=1, source_target_pairs={{0,1},{1,0},{2,3},{3,2},{4,5},{5,4},{6,7},{7,6},{8,9},{9,8},{10,11... | collective-permute-start | bytes 1572872 | tf_op jit(solution)/shard_map/ppermute | solution.py:20
  50.7 3.1 %collective-permute-start.11 = (bf16[2,256,512]{2,1,0:T(8,128)(2,1)S(1)}, bf16[2,256,512]{2,1,0:T(8,128)(2,1)S(1)}, u32[]{:S(2)}, u32[]{:S(2)}) collective-permute-start(bf16[2,256,512]{2,1,0:T(8,128)(2,1)S(1)} %collective-permute-done.7.refs_4_), channel_id=1, source_target_pairs={{0,2},{2,4},{4,6},{6,8},{8,10},{10,12},{12,14},{14,0},{1,15},{3,1}... | collective-permute-start | bytes 1572872 | tf_op jit(solution)/shard_map/ppermute | solution.py:27
  53.8 1.2 sum_2.1.refs_4_
  55.0 2.1 %collective-permute-start.8 = (bf16[2,256,512]{2,1,0:T(8,128)(2,1)S(1)}, bf16[2,256,512]{2,1,0:T(8,128)(2,1)S(1)}, u32[]{:S(2)}, u32[]{:S(2)}) collective-permute-start(bf16[2,256,512]{2,1,0:T(8,128)(2,1)S(1)} %collective-permute-done.4.refs_3_), channel_id=1, source_target_pairs={{0,2},{2,4},{4,6},{6,8},{8,10},{10,12},{12,14},{14,0},{1,15},{3,1}... | collective-permute-start | bytes 1572872 | tf_op jit(solution)/shard_map/ppermute | solution.py:27
  57.2 1.0 sum_3.1.refs_5_
  58.2 2.7 %collective-permute-done.11.refs_3_ = bf16[2,256,512]{2,1,0:T(8,128)(2,1)S(1)} collective-permute-done((bf16[2,256,512]{2,1,0:T(8,128)(2,1)S(1)}, bf16[2,256,512]{2,1,0:T(8,128)(2,1)S(1)}, u32[]{:S(2)}, u32[]{:S(2)}) %collective-permute-start.11) | collective-permute-done | bytes 524320 | tf_op jit(solution)/shard_map/ppermute | solution.py:27
  60.9 4.0 %collective-permute-start.14 = (bf16[2,256,512]{2,1,0:T(8,128)(2,1)S(1)}, bf16[2,256,512]{2,1,0:T(8,128)(2,1)S(1)}, u32[]{:S(2)}, u32[]{:S(2)}) collective-permute-start(bf16[2,256,512]{2,1,0:T(8,128)(2,1)S(1)} %collective-permute-done.11.refs_3_), channel_id=1, source_target_pairs={{0,1},{1,0},{2,3},{3,2},{4,5},{5,4},{6,7},{7,6},{8,9},{9,8},{10,11... | collective-permute-start | bytes 1572872 | tf_op jit(solution)/shard_map/ppermute | solution.py:20
  64.9 1.9 %collective-permute-start.10 = (bf16[2,256,512]{2,1,0:T(8,128)(2,1)S(1)}, bf16[2,256,512]{2,1,0:T(8,128)(2,1)S(1)}, u32[]{:S(2)}, u32[]{:S(2)}) collective-permute-start(bf16[2,256,512]{2,1,0:T(8,128)(2,1)S(1)} %collective-permute-done.4.refs_3_), channel_id=1, source_target_pairs={{0,1},{1,0},{2,3},{3,2},{4,5},{5,4},{6,7},{7,6},{8,9},{9,8},{10,11... | collective-permute-start | bytes 1572872 | tf_op jit(solution)/shard_map/ppermute | solution.py:20
  66.8 3.7 %collective-permute-start.9 = (bf16[2,256,512]{2,1,0:T(8,128)(2,1)S(1)}, bf16[2,256,512]{2,1,0:T(8,128)(2,1)S(1)}, u32[]{:S(2)}, u32[]{:S(2)}) collective-permute-start(bf16[2,256,512]{2,1,0:T(8,128)(2,1)S(1)} %collective-permute-done.8.refs_4_), channel_id=1, source_target_pairs={{0,1},{1,0},{2,3},{3,2},{4,5},{5,4},{6,7},{7,6},{8,9},{9,8},{10,11... | collective-permute-start | bytes 1572872 | tf_op jit(solution)/shard_map/ppermute | solution.py:20
  70.5 1.2 sum_4.1.refs_2_
  71.8 0.2 collective-permute-done.9.refs_1_
  72.0 0.9 sum_5.1
  72.9 9.5 %collective-permute-start.15 = (bf16[2,256,512]{2,1,0:T(8,128)(2,1)S(1)}, bf16[2,256,512]{2,1,0:T(8,128)(2,1)S(1)}, u32[]{:S(2)}, u32[]{:S(2)}) collective-permute-start(bf16[2,256,512]{2,1,0:T(8,128)(2,1)S(1)} %sum_5.1), channel_id=1, source_target_pairs={{0,1008},{16,496},{32,752},{48,240},{64,880},{80,368},{96,624},{11... | collective-permute-start | bytes 1572872 | tf_op jit(solution)/shard_map/ppermute | solution.py:37
  82.4 46.1 %collective-permute-done.15 = bf16[2,256,512]{2,1,0:T(8,128)(2,1)S(1)} collective-permute-done((bf16[2,256,512]{2,1,0:T(8,128)(2,1)S(1)}, bf16[2,256,512]{2,1,0:T(8,128)(2,1)S(1)}, u32[]{:S(2)}, u32[]{:S(2)}) %collective-permute-start.15) | collective-permute-done | bytes 524320 | tf_op jit(solution)/shard_map/ppermute | solution.py:37
  128.4 0.9 add_convert_fusion
  (19 shorter events, 0.1 us)
Async XLA Ops:
  0.0 28.6 %collective-permute-start = (bf16[2,256,512]{2,1,0:T(8,128)(2,1)}, bf16[2,256,512]{2,1,0:T(8,128)(2,1)S(1)}, u32[]{:S(2)}, u32[]{:S(2)}) collective-permute-start(bf16[2,256,512]{2,1,0:T(8,128)(2,1)} %refs_1_.1), channel_id=1, source_target_pairs={{0,2},{2,4},{4,6},{6,8},{8,10},{10,12},{12,14},{14,0},{1,15},{3,1}... | collective-permute-start | bytes 1572872 | tf_op jit(solution)/shard_map/ppermute | solution.py:27
  5.9 27.6 %collective-permute-start.2 = (bf16[2,256,512]{2,1,0:T(8,128)(2,1)}, bf16[2,256,512]{2,1,0:T(8,128)(2,1)S(1)}, u32[]{:S(2)}, u32[]{:S(2)}) collective-permute-start(bf16[2,256,512]{2,1,0:T(8,128)(2,1)} %refs_1_.1), channel_id=1, source_target_pairs={{1,2},{3,4},{5,6},{7,8},{9,10},{11,12},{13,14},{15,0},{0,15},{2,1}... | collective-permute-start | bytes 1572872 | tf_op jit(solution)/shard_map/ppermute | solution.py:27
  8.1 33.0 %collective-permute-start.3 = (bf16[2,256,512]{2,1,0:T(8,128)(2,1)}, bf16[2,256,512]{2,1,0:T(8,128)(2,1)S(1)}, u32[]{:S(2)}, u32[]{:S(2)}) collective-permute-start(bf16[2,256,512]{2,1,0:T(8,128)(2,1)} %refs_1_.1), channel_id=1, source_target_pairs={{0,1},{1,0},{2,3},{3,2},{4,5},{5,4},{6,7},{7,6},{8,9},{9,8},{10,11... | collective-permute-start | bytes 1572872 | tf_op jit(solution)/shard_map/ppermute | solution.py:20
  21.5 1.6 %copy-start = (bf16[256,4096]{1,0:T(8,128)(2,1)S(1)}, bf16[256,4096]{1,0:T(8,128)(2,1)}, u32[]{:S(2)}) copy-start(bf16[256,4096]{1,0:T(8,128)(2,1)} %fock.1) | copy-start | bytes 6291460
  23.1 1.6 %copy-start.1 = (bf16[256,4096]{1,0:T(8,128)(2,1)S(1)}, bf16[256,4096]{1,0:T(8,128)(2,1)}, u32[]{:S(2)}) copy-start(bf16[256,4096]{1,0:T(8,128)(2,1)} %ladder.1) | copy-start | bytes 6291460
  24.7 16.4 %copy-start.2 = (bf16[2,256,512]{2,1,0:T(8,128)(2,1)S(1)}, bf16[2,256,512]{2,1,0:T(8,128)(2,1)}, u32[]{:S(2)}) copy-start(bf16[2,256,512]{2,1,0:T(8,128)(2,1)} %refs_1_.1) | copy-start | bytes 1572868
  28.6 13.8 %collective-permute-start.1 = (bf16[2,256,512]{2,1,0:T(8,128)(2,1)S(1)}, bf16[2,256,512]{2,1,0:T(8,128)(2,1)S(1)}, u32[]{:S(2)}, u32[]{:S(2)}) collective-permute-start(bf16[2,256,512]{2,1,0:T(8,128)(2,1)S(1)} %collective-permute-done.refs_2_), channel_id=1, source_target_pairs={{0,2},{2,4},{4,6},{6,8},{8,10},{10,12},{12,14},{14,0},{1,15},{3,1}... | collective-permute-start | bytes 1572872 | tf_op jit(solution)/shard_map/ppermute | solution.py:27
  33.5 13.5 %collective-permute-start.7 = (bf16[2,256,512]{2,1,0:T(8,128)(2,1)S(1)}, bf16[2,256,512]{2,1,0:T(8,128)(2,1)S(1)}, u32[]{:S(2)}, u32[]{:S(2)}) collective-permute-start(bf16[2,256,512]{2,1,0:T(8,128)(2,1)S(1)} %collective-permute-done.2.refs_3_), channel_id=1, source_target_pairs={{0,2},{2,4},{4,6},{6,8},{8,10},{10,12},{12,14},{14,0},{1,15},{3,1}... | collective-permute-start | bytes 1572872 | tf_op jit(solution)/shard_map/ppermute | solution.py:27
  36.8 13.9 %collective-permute-start.5 = (bf16[2,256,512]{2,1,0:T(8,128)(2,1)S(1)}, bf16[2,256,512]{2,1,0:T(8,128)(2,1)S(1)}, u32[]{:S(2)}, u32[]{:S(2)}) collective-permute-start(bf16[2,256,512]{2,1,0:T(8,128)(2,1)S(1)} %collective-permute-done.refs_2_), channel_id=1, source_target_pairs={{0,1},{1,0},{2,3},{3,2},{4,5},{5,4},{6,7},{7,6},{8,9},{9,8},{10,11... | collective-permute-start | bytes 1572872 | tf_op jit(solution)/shard_map/ppermute | solution.py:20
  38.7 15.1 %collective-permute-start.6 = (bf16[2,256,512]{2,1,0:T(8,128)(2,1)S(1)}, bf16[2,256,512]{2,1,0:T(8,128)(2,1)S(1)}, u32[]{:S(2)}, u32[]{:S(2)}) collective-permute-start(bf16[2,256,512]{2,1,0:T(8,128)(2,1)S(1)} %collective-permute-done.2.refs_3_), channel_id=1, source_target_pairs={{0,1},{1,0},{2,3},{3,2},{4,5},{5,4},{6,7},{7,6},{8,9},{9,8},{10,11... | collective-permute-start | bytes 1572872 | tf_op jit(solution)/shard_map/ppermute | solution.py:20
  42.4 12.6 %collective-permute-start.4 = (bf16[2,256,512]{2,1,0:T(8,128)(2,1)S(1)}, bf16[2,256,512]{2,1,0:T(8,128)(2,1)S(1)}, u32[]{:S(2)}, u32[]{:S(2)}) collective-permute-start(bf16[2,256,512]{2,1,0:T(8,128)(2,1)S(1)} %collective-permute-done.1.refs_3_), channel_id=1, source_target_pairs={{0,2},{2,4},{4,6},{6,8},{8,10},{10,12},{12,14},{14,0},{1,15},{3,1}... | collective-permute-start | bytes 1572872 | tf_op jit(solution)/shard_map/ppermute | solution.py:27
  44.7 12.4 %collective-permute-start.12 = (bf16[2,256,512]{2,1,0:T(8,128)(2,1)S(1)}, bf16[2,256,512]{2,1,0:T(8,128)(2,1)S(1)}, u32[]{:S(2)}, u32[]{:S(2)}) collective-permute-start(bf16[2,256,512]{2,1,0:T(8,128)(2,1)S(1)} %collective-permute-done.1.refs_3_), channel_id=1, source_target_pairs={{0,1},{1,0},{2,3},{3,2},{4,5},{5,4},{6,7},{7,6},{8,9},{9,8},{10,11... | collective-permute-start | bytes 1572872 | tf_op jit(solution)/shard_map/ppermute | solution.py:20
  47.0 10.2 %collective-permute-start.13 = (bf16[2,256,512]{2,1,0:T(8,128)(2,1)S(1)}, bf16[2,256,512]{2,1,0:T(8,128)(2,1)S(1)}, u32[]{:S(2)}, u32[]{:S(2)}) collective-permute-start(bf16[2,256,512]{2,1,0:T(8,128)(2,1)S(1)} %collective-permute-done.7.refs_4_), channel_id=1, source_target_pairs={{0,1},{1,0},{2,3},{3,2},{4,5},{5,4},{6,7},{7,6},{8,9},{9,8},{10,11... | collective-permute-start | bytes 1572872 | tf_op jit(solution)/shard_map/ppermute | solution.py:20
  50.7 10.2 %collective-permute-start.11 = (bf16[2,256,512]{2,1,0:T(8,128)(2,1)S(1)}, bf16[2,256,512]{2,1,0:T(8,128)(2,1)S(1)}, u32[]{:S(2)}, u32[]{:S(2)}) collective-permute-start(bf16[2,256,512]{2,1,0:T(8,128)(2,1)S(1)} %collective-permute-done.7.refs_4_), channel_id=1, source_target_pairs={{0,2},{2,4},{4,6},{6,8},{8,10},{10,12},{12,14},{14,0},{1,15},{3,1}... | collective-permute-start | bytes 1572872 | tf_op jit(solution)/shard_map/ppermute | solution.py:27
  55.0 11.7 %collective-permute-start.8 = (bf16[2,256,512]{2,1,0:T(8,128)(2,1)S(1)}, bf16[2,256,512]{2,1,0:T(8,128)(2,1)S(1)}, u32[]{:S(2)}, u32[]{:S(2)}) collective-permute-start(bf16[2,256,512]{2,1,0:T(8,128)(2,1)S(1)} %collective-permute-done.4.refs_3_), channel_id=1, source_target_pairs={{0,2},{2,4},{4,6},{6,8},{8,10},{10,12},{12,14},{14,0},{1,15},{3,1}... | collective-permute-start | bytes 1572872 | tf_op jit(solution)/shard_map/ppermute | solution.py:27
  58.1 13.8 %copy-start.3 = (bf16[512,512]{1,0:T(8,128)(2,1)S(1)}, bf16[512,512]{1,0:T(8,128)(2,1)}, u32[]{:S(2)}) copy-start(bf16[512,512]{1,0:T(8,128)(2,1)} %refs_3_.1) | copy-start | bytes 1572868
  60.9 9.6 %collective-permute-start.14 = (bf16[2,256,512]{2,1,0:T(8,128)(2,1)S(1)}, bf16[2,256,512]{2,1,0:T(8,128)(2,1)S(1)}, u32[]{:S(2)}, u32[]{:S(2)}) collective-permute-start(bf16[2,256,512]{2,1,0:T(8,128)(2,1)S(1)} %collective-permute-done.11.refs_3_), channel_id=1, source_target_pairs={{0,1},{1,0},{2,3},{3,2},{4,5},{5,4},{6,7},{7,6},{8,9},{9,8},{10,11... | collective-permute-start | bytes 1572872 | tf_op jit(solution)/shard_map/ppermute | solution.py:20
  64.9 5.6 %collective-permute-start.10 = (bf16[2,256,512]{2,1,0:T(8,128)(2,1)S(1)}, bf16[2,256,512]{2,1,0:T(8,128)(2,1)S(1)}, u32[]{:S(2)}, u32[]{:S(2)}) collective-permute-start(bf16[2,256,512]{2,1,0:T(8,128)(2,1)S(1)} %collective-permute-done.4.refs_3_), channel_id=1, source_target_pairs={{0,1},{1,0},{2,3},{3,2},{4,5},{5,4},{6,7},{7,6},{8,9},{9,8},{10,11... | collective-permute-start | bytes 1572872 | tf_op jit(solution)/shard_map/ppermute | solution.py:20
  66.8 5.2 %collective-permute-start.9 = (bf16[2,256,512]{2,1,0:T(8,128)(2,1)S(1)}, bf16[2,256,512]{2,1,0:T(8,128)(2,1)S(1)}, u32[]{:S(2)}, u32[]{:S(2)}) collective-permute-start(bf16[2,256,512]{2,1,0:T(8,128)(2,1)S(1)} %collective-permute-done.8.refs_4_), channel_id=1, source_target_pairs={{0,1},{1,0},{2,3},{3,2},{4,5},{5,4},{6,7},{7,6},{8,9},{9,8},{10,11... | collective-permute-start | bytes 1572872 | tf_op jit(solution)/shard_map/ppermute | solution.py:20
  72.9 55.6 %collective-permute-start.15 = (bf16[2,256,512]{2,1,0:T(8,128)(2,1)S(1)}, bf16[2,256,512]{2,1,0:T(8,128)(2,1)S(1)}, u32[]{:S(2)}, u32[]{:S(2)}) collective-permute-start(bf16[2,256,512]{2,1,0:T(8,128)(2,1)S(1)} %sum_5.1), channel_id=1, source_target_pairs={{0,1008},{16,496},{32,752},{48,240},{64,880},{80,368},{96,624},{11... | collective-permute-start | bytes 1572872 | tf_op jit(solution)/shard_map/ppermute | solution.py:37

commit v4 on v3

--- a/solution.py
+++ b/solution.py
@@ -11,8 +11,10 @@
 HALF = 256
 SPLIT = HALF // TILE
 VMEM_LIMIT = 24 * 1024 * 1024
+RING = 16
+ADD_FLOPS = 1 << 34
 HOPS = (None, (0, 0), (1, 0), (1, 1), (2, 0), (2, 1), (3, 0), (3, 1), (4, 0))
-ORDER = (1, 2, 3, -1, -2, -3, 4, 5, -4, -5, 6, -6, -7, 7, 8, -8)
+ORDER = (1, 2, 3, -2, -3, 4, 5, -4, -5, 6, -1, -6, -7, 7, 8, -8)
 
 
 def core_swap(block):
@@ -27,59 +29,73 @@
     return lax.ppermute(block, "virt", route)
 
 
+def mirror_of(place, count):
+    nbits = count.bit_length() - 1
+    return count - 1 - sum(((place >> b) & 1) << (nbits - 1 - b) for b in range(nbits))
+
+
 def mirror_swap(block):
-    count = lax.axis_size("pair")
-    nbits = count.bit_length() - 1
-    route = []
-    for low in range(count):
-        flipped = sum(((low >> b) & 1) << (nbits - 1 - b) for b in range(nbits))
-        route.append((low, count - 1 - flipped))
-    return lax.ppermute(block, "pair", route)
+    count, across = lax.axis_size("pair"), lax.axis_size("virt")
+    axes, quarter = ("pair", "virt"), RING // 4
+    stops = {}
+    for row in range(0, count, RING):
+        stops[row + quarter - 1] = row + RING // 2 + 1
+        stops[row + RING - quarter] = row + RING // 2 - 2
+    at = lambda place, v: place * across + v
+    legs = [(place, stop, mirror_of(place, count), v) for place, stop in stops.items() for v in range(0, across, 2)]
+    detour = {at(place, v) for place, _, _, v in legs}
+    direct = [(at(place, v), at(mirror_of(place, count), v)) for place in range(count) for v in range(across)]
+    halfway = lax.ppermute(block, axes, [(at(place, v), at(stop, v)) for place, stop, _, v in legs])
+    straight = lax.ppermute(block, axes, [leg for leg in direct if leg[0] not in detour])
+    return straight, lax.ppermute(halfway, axes, [(at(stop, v), at(end, v)) for _, stop, end, v in legs])
+
+
+def add_kernel(a_ref, b_ref, out_ref):
+    out_ref[...] = (a_ref[...].astype(jnp.float32) + b_ref[...].astype(jnp.float32)).astype(out_ref.dtype)
+
+
+def add(a, b):
+    vmem = pl.BlockSpec(memory_space=pltpu.VMEM)
+    return pl.pallas_call(
+        add_kernel,
+        out_shape=jax.ShapeDtypeStruct(a.shape, a.dtype),
+        in_specs=[vmem, vmem],
+        out_specs=vmem,
+        cost_estimate=pl.CostEstimate(flops=ADD_FLOPS, bytes_accessed=1 << 20, transcendentals=0),
+        name="add",
+    )(a, b)
 
 
 def after(block, *earlier):
     return lax.optimization_barrier((block, *earlier))[0]
 
 
-def screen_kernel(pairs, slot_ref, mask_ref, fock, ladder, out_ref, buf, sem):
-    count = buf.shape[1]
-
-    def copies(n):
-        col = pl.multiple_of(slot_ref[n] * TILE, HALF)
-        return [
-            pltpu.make_async_copy(mat.at[:, pl.ds(col, HALF)], buf.at[i, n], sem.at[i, n])
-            for i, mat in enumerate((fock, ladder))
-        ]
-
-    jobs = [copies(n) for n in range(count)]
-    for job in jobs:
-        for copy in job:
-            copy.start()
-    for n, job in enumerate(jobs):
-        for i, copy in enumerate(job):
-            copy.wait()
+def screen_kernel(pairs, slot_ref, mask_ref, fock, ladder, out_ref):
+    for n in range(out_ref.shape[2] // HALF):
+        for q in range(SPLIT):
+            tile = slot_ref[n] + q
+            columns = pl.ds(pl.multiple_of(tile * TILE, TILE), TILE)
             for r in range(SPLIT):
-                for q in range(SPLIT):
-                    block = buf[i, n, r * TILE : (r + 1) * TILE, q * TILE : (q + 1) * TILE]
+                keep = [mask_ref[p * SPLIT + r, tile] != 0 for p in range(pairs)]
+                for i, mat in enumerate((fock, ladder)):
+                    block = mat[r * TILE : (r + 1) * TILE, columns]
                     for p in range(pairs):
-                        keep = mask_ref[p * SPLIT + r, slot_ref[n] + q] != 0
                         out_ref[
                             p,
                             i * HALF + r * TILE : i * HALF + (r + 1) * TILE,
                             n * HALF + q * TILE : n * HALF + (q + 1) * TILE,
-                        ] = jnp.where(keep, block, jnp.zeros_like(block))
+                        ] = jnp.where(keep[p], block, jnp.zeros_like(block))
 
 
 def screened(slot_tiles, masks, fock, ladder, pairs):
     smem = pl.BlockSpec(memory_space=pltpu.SMEM)
-    anywhere = pl.BlockSpec(memory_space=pl.ANY)
+    vmem = pl.BlockSpec(memory_space=pltpu.VMEM)
     count, dtype = slot_tiles.shape[0], fock.dtype
     return pl.pallas_call(
         functools.partial(screen_kernel, pairs),
         out_shape=jax.ShapeDtypeStruct((pairs, 2 * HALF, count * HALF), dtype),
-        in_specs=[smem, smem, anywhere, anywhere],
-        out_specs=pl.BlockSpec(memory_space=pltpu.VMEM),
-        scratch_shapes=[pltpu.VMEM((2, count, HALF, HALF), dtype), pltpu.SemaphoreType.DMA((2, count))],
+        in_specs=[smem, smem, vmem, vmem],
+        out_specs=vmem,
         compiler_params=pltpu.CompilerParams(vmem_limit_bytes=VMEM_LIMIT),
         cost_estimate=pl.CostEstimate(flops=0, bytes_accessed=4 << 20, transcendentals=0),
         name="screened",
@@ -144,15 +160,16 @@
     x1, s1 = ring_step(x0), ring_step(x0, cross=1)
     mat = screened(slot_tiles, masks, fock, ladder, pairs)
     x2, s2 = ring_step(after(x1, mat)), ring_step(s1)
-    acc = sum_slots("sum_1", mat, (x0, x1, s1, core_swap(x0)), 0)
+    acc = sum_slots("sum_1", mat, (x0, x1, s1), 0)
     x3, s3 = ring_step(after(x2, acc)), ring_step(s2)
-    acc = sum_slots("sum_2", mat, (core_swap(x1), core_swap(s1), x2, s2), 4, acc)
+    acc = sum_slots("sum_2", mat, (core_swap(x1), core_swap(s1), x2, s2), 3, acc)
     x4 = ring_step(after(x3, acc))
-    acc = sum_slots("sum_3", mat, (core_swap(x2), core_swap(s2), x3), 8, acc)
-    acc = sum_slots("sum_4", mat, (core_swap(x3), core_swap(after(s3, acc)), s3, x4), 11, acc)
+    acc = sum_slots("sum_3", mat, (core_swap(x2), core_swap(s2), x3), 7, acc)
+    late = (core_swap(after(x0, acc)), core_swap(x3), core_swap(after(s3, acc)), s3, x4)
+    acc = sum_slots("sum_4", mat, late, 10, acc)
     half_term = sum_slots("sum_5", mat, (core_swap(x4),), 15, acc, couple)
-    mirrored = mirror_swap(half_term)
-    return (half_term.astype(jnp.float32) + mirrored.astype(jnp.float32)).astype(jnp.bfloat16)
+    straight, detoured = mirror_swap(half_term)
+    return (add(half_term, straight).astype(jnp.float32) + detoured.astype(jnp.float32)).astype(jnp.bfloat16)
 
 
 def solution(mesh):

time: 130 us -> 127 us (0.977)
  waiting for transfers between devices: 49.1 us -> 43 us
    ppermute x7, starting transfers between devices: 23.7 us -> 35.9 us  [ring_step(): return lax.ppermute(block, 'virt', route)]
    ppermute x8, starting transfers between devices: 31.6 us -> 21.1 us  [core_swap(): return lax.ppermute(block, 'virt', [(v, v ^ 1) for v in range(count)])]
    ppermute x1 -> x3, waiting for transfers between devices: 46.1 us -> 39.8 us  [the longest x1 39.8 us: mirror_swap(): lax.ppermute(block, axes, [leg for leg in direct if leg[0] not in detour])]
    pallas_call x0 -> x1, Pallas kernels: none -> 2.11 us  [add(): pl.pallas_call(add_kernel, out_shape=jax.ShapeDtypeStruct(a.shape, a.dtyp...]
    ppermute x1 -> x3, starting transfers between devices: 9.48 us -> 7.96 us  [the longest x1 6.57 us: mirror_swap(): lax.ppermute(block, axes, [leg for leg in direct if leg[0] not in detour])]
    unnamed x8 -> x12, local copies, waits for them, and re-layouts: 3.19 us -> 4 us
  transfers between devices with their start and end apart: 16 -> 18, of which waited for: 3 -> 3; matrix products, arithmetic and copies ran while one was open for 1% -> 1% of each run, Pallas kernels for 7% -> 8%
where the time goes in v4:
time: 127 us
  starting transfers between devices  64.9 us (51%)
  waiting for transfers between devices  43 us (34%)
  Pallas kernels  10.7 us (8%)
  local copies, waits for them, and re-layouts  4.77 us (4%)
  other arithmetic  2.76 us (2%)
    ppermute x1, waiting for transfers between devices, mirror_swap(): lax.ppermute(block, axes, [leg for leg in direct if leg[0] not in detour])  39.8 us
    ppermute x7, starting transfers between devices, ring_step(): return lax.ppermute(block, 'virt', route)  35.9 us
    ppermute x8, starting transfers between devices, core_swap(): return lax.ppermute(block, 'virt', [(v, v ^ 1) for v in range(count)])  21.1 us
    ppermute x1, starting transfers between devices, mirror_swap(): lax.ppermute(block, axes, [leg for leg in direct if leg[0] not in detour])  6.57 us
    pallas_call x5, Pallas kernels, sum_slots(): pl.pallas_call(functools.partial(sum_kernel, pairs, slots, acc is not Non...  5.59 us
    unnamed x12, local copies, waits for them, and re-layouts  4 us
    pallas_call x1, Pallas kernels, screened(): pl.pallas_call(functools.partial(screen_kernel, pairs), out_shape=jax.Sha...  3.04 us
    ppermute x7, waiting for transfers between devices, ring_step(): return lax.ppermute(block, 'virt', route)  2.9 us
  transfers between devices with their start and end apart: 18, of which 3 were waited for; matrix products, arithmetic and copies ran while one was open for 1% of the time, Pallas kernels for 8%

profile of v4, /device:TPU:1, one launch (start us, length us, event | category | flops | bytes accessed | tf_op | source)
XLA Modules:
  0.0 126.5 jit_solution(5991391417784534872)
XLA Ops:
  0.0 5.9 %collective-permute-start = (bf16[2,256,512]{2,1,0:T(8,128)(2,1)}, bf16[2,256,512]{2,1,0:T(8,128)(2,1)S(1)}, u32[]{:S(2)}, u32[]{:S(2)}) collective-permute-start(bf16[2,256,512]{2,1,0:T(8,128)(2,1)} %refs_1_.1), channel_id=1, source_target_pairs={{0,2},{2,4},{4,6},{6,8},{8,10},{10,12},{12,14},{14,0},{1,15},{3,1}... | collective-permute-start | bytes 1572872 | tf_op jit(solution)/shard_map/ppermute | solution.py:29
  5.9 2.2 %collective-permute-start.2 = (bf16[2,256,512]{2,1,0:T(8,128)(2,1)}, bf16[2,256,512]{2,1,0:T(8,128)(2,1)S(1)}, u32[]{:S(2)}, u32[]{:S(2)}) collective-permute-start(bf16[2,256,512]{2,1,0:T(8,128)(2,1)} %refs_1_.1), channel_id=1, source_target_pairs={{1,2},{3,4},{5,6},{7,8},{9,10},{11,12},{13,14},{15,0},{0,15},{2,1}... | collective-permute-start | bytes 1572872 | tf_op jit(solution)/shard_map/ppermute | solution.py:29
  8.1 0.8 copy.8
  9.7 1.6 %copy-done = bf16[256,4096]{1,0:T(8,128)(2,1)S(1)} copy-done((bf16[256,4096]{1,0:T(8,128)(2,1)S(1)}, bf16[256,4096]{1,0:T(8,128)(2,1)}, u32[]{:S(2)}) %copy-start) | copy-done | bytes 2097176
  11.3 1.6 %copy-done.1 = bf16[256,4096]{1,0:T(8,128)(2,1)S(1)} copy-done((bf16[256,4096]{1,0:T(8,128)(2,1)S(1)}, bf16[256,4096]{1,0:T(8,128)(2,1)}, u32[]{:S(2)}) %copy-start.1) | copy-done | bytes 2097176
  12.9 3.0 %screened.1.refs_0_ = bf16[2,512,4096]{2,1,0:T(8,128)(2,1)S(1)} custom-call(s32[16]{0:T(128)S(1)} %fusion.2.slot_ref, s32[4,32]{1,0:T(4,128)S(1)} %convert_element_type.12.mask_ref, bf16[256,4096]{1,0:T(8,128)(2,1)S(1)} %copy-done, bf16[256,4096]{1,0:T(8,128)(2,1)S(1)} %copy-done.1), custom_call_target="tpu_custom_call" | custom-call | bytes 4194304 | tf_op jit(solution)/shard_map/screened/pallas_call | solution.py:94
  15.9 14.3 %collective-permute-start.1 = (bf16[2,256,512]{2,1,0:T(8,128)(2,1)S(1)}, bf16[2,256,512]{2,1,0:T(8,128)(2,1)S(1)}, u32[]{:S(2)}, u32[]{:S(2)}) collective-permute-start(bf16[2,256,512]{2,1,0:T(8,128)(2,1)S(1)} %collective-permute-done.refs_2_), channel_id=1, source_target_pairs={{0,2},{2,4},{4,6},{6,8},{8,10},{10,12},{12,14},{14,0},{1,15},{3,1}... | collective-permute-start | bytes 1572872 | tf_op jit(solution)/shard_map/ppermute | solution.py:29
  30.3 3.6 %collective-permute-start.6 = (bf16[2,256,512]{2,1,0:T(8,128)(2,1)S(1)}, bf16[2,256,512]{2,1,0:T(8,128)(2,1)S(1)}, u32[]{:S(2)}, u32[]{:S(2)}) collective-permute-start(bf16[2,256,512]{2,1,0:T(8,128)(2,1)S(1)} %collective-permute-done.2.refs_3_), channel_id=1, source_target_pairs={{0,2},{2,4},{4,6},{6,8},{8,10},{10,12},{12,14},{14,0},{1,15},{3,1}... | collective-permute-start | bytes 1572872 | tf_op jit(solution)/shard_map/ppermute | solution.py:29
  33.9 2.7 %collective-permute-start.4 = (bf16[2,256,512]{2,1,0:T(8,128)(2,1)S(1)}, bf16[2,256,512]{2,1,0:T(8,128)(2,1)S(1)}, u32[]{:S(2)}, u32[]{:S(2)}) collective-permute-start(bf16[2,256,512]{2,1,0:T(8,128)(2,1)S(1)} %collective-permute-done.refs_2_), channel_id=1, source_target_pairs={{0,1},{1,0},{2,3},{3,2},{4,5},{5,4},{6,7},{7,6},{8,9},{9,8},{10,11... | collective-permute-start | bytes 1572872 | tf_op jit(solution)/shard_map/ppermute | solution.py:22
  36.6 1.9 %collective-permute-start.5 = (bf16[2,256,512]{2,1,0:T(8,128)(2,1)S(1)}, bf16[2,256,512]{2,1,0:T(8,128)(2,1)S(1)}, u32[]{:S(2)}, u32[]{:S(2)}) collective-permute-start(bf16[2,256,512]{2,1,0:T(8,128)(2,1)S(1)} %collective-permute-done.2.refs_3_), channel_id=1, source_target_pairs={{0,1},{1,0},{2,3},{3,2},{4,5},{5,4},{6,7},{7,6},{8,9},{9,8},{10,11... | collective-permute-start | bytes 1572872 | tf_op jit(solution)/shard_map/ppermute | solution.py:22
  38.6 1.0 sum_1.1.refs_5_
  39.6 4.9 %collective-permute-start.3 = (bf16[2,256,512]{2,1,0:T(8,128)(2,1)S(1)}, bf16[2,256,512]{2,1,0:T(8,128)(2,1)S(1)}, u32[]{:S(2)}, u32[]{:S(2)}) collective-permute-start(bf16[2,256,512]{2,1,0:T(8,128)(2,1)S(1)} %collective-permute-done.1.refs_3_), channel_id=1, source_target_pairs={{0,2},{2,4},{4,6},{6,8},{8,10},{10,12},{12,14},{14,0},{1,15},{3,1}... | collective-permute-start | bytes 1572872 | tf_op jit(solution)/shard_map/ppermute | solution.py:29
  44.4 2.5 %collective-permute-start.9 = (bf16[2,256,512]{2,1,0:T(8,128)(2,1)S(1)}, bf16[2,256,512]{2,1,0:T(8,128)(2,1)S(1)}, u32[]{:S(2)}, u32[]{:S(2)}) collective-permute-start(bf16[2,256,512]{2,1,0:T(8,128)(2,1)S(1)} %collective-permute-done.1.refs_3_), channel_id=1, source_target_pairs={{0,1},{1,0},{2,3},{3,2},{4,5},{5,4},{6,7},{7,6},{8,9},{9,8},{10,11... | collective-permute-start | bytes 1572872 | tf_op jit(solution)/shard_map/ppermute | solution.py:22
  47.0 3.7 %collective-permute-start.10 = (bf16[2,256,512]{2,1,0:T(8,128)(2,1)S(1)}, bf16[2,256,512]{2,1,0:T(8,128)(2,1)S(1)}, u32[]{:S(2)}, u32[]{:S(2)}) collective-permute-start(bf16[2,256,512]{2,1,0:T(8,128)(2,1)S(1)} %collective-permute-done.6.refs_4_), channel_id=1, source_target_pairs={{0,1},{1,0},{2,3},{3,2},{4,5},{5,4},{6,7},{7,6},{8,9},{9,8},{10,11... | collective-permute-start | bytes 1572872 | tf_op jit(solution)/shard_map/ppermute | solution.py:22
  50.7 3.1 %collective-permute-start.13 = (bf16[2,256,512]{2,1,0:T(8,128)(2,1)S(1)}, bf16[2,256,512]{2,1,0:T(8,128)(2,1)S(1)}, u32[]{:S(2)}, u32[]{:S(2)}) collective-permute-start(bf16[2,256,512]{2,1,0:T(8,128)(2,1)S(1)} %collective-permute-done.6.refs_4_), channel_id=1, source_target_pairs={{0,2},{2,4},{4,6},{6,8},{8,10},{10,12},{12,14},{14,0},{1,15},{3,1}... | collective-permute-start | bytes 1572872 | tf_op jit(solution)/shard_map/ppermute | solution.py:29
  53.8 1.2 sum_2.1.refs_4_
  55.0 1.9 %collective-permute-start.7 = (bf16[2,256,512]{2,1,0:T(8,128)(2,1)S(1)}, bf16[2,256,512]{2,1,0:T(8,128)(2,1)S(1)}, u32[]{:S(2)}, u32[]{:S(2)}) collective-permute-start(bf16[2,256,512]{2,1,0:T(8,128)(2,1)S(1)} %collective-permute-done.3.refs_3_), channel_id=1, source_target_pairs={{0,2},{2,4},{4,6},{6,8},{8,10},{10,12},{12,14},{14,0},{1,15},{3,1}... | collective-permute-start | bytes 1572872 | tf_op jit(solution)/shard_map/ppermute | solution.py:29
  57.0 1.0 sum_3.1.refs_6_
  58.0 2.9 %collective-permute-done.13.refs_4_ = bf16[2,256,512]{2,1,0:T(8,128)(2,1)S(1)} collective-permute-done((bf16[2,256,512]{2,1,0:T(8,128)(2,1)S(1)}, bf16[2,256,512]{2,1,0:T(8,128)(2,1)S(1)}, u32[]{:S(2)}, u32[]{:S(2)}) %collective-permute-start.13) | collective-permute-done | bytes 524320 | tf_op jit(solution)/shard_map/ppermute | solution.py:29
  60.9 4.0 %collective-permute-start.14 = (bf16[2,256,512]{2,1,0:T(8,128)(2,1)S(1)}, bf16[2,256,512]{2,1,0:T(8,128)(2,1)S(1)}, u32[]{:S(2)}, u32[]{:S(2)}) collective-permute-start(bf16[2,256,512]{2,1,0:T(8,128)(2,1)S(1)} %collective-permute-done.13.refs_4_), channel_id=1, source_target_pairs={{0,1},{1,0},{2,3},{3,2},{4,5},{5,4},{6,7},{7,6},{8,9},{9,8},{10,11... | collective-permute-start | bytes 1572872 | tf_op jit(solution)/shard_map/ppermute | solution.py:22
  64.9 1.9 %collective-permute-start.11 = (bf16[2,256,512]{2,1,0:T(8,128)(2,1)S(1)}, bf16[2,256,512]{2,1,0:T(8,128)(2,1)S(1)}, u32[]{:S(2)}, u32[]{:S(2)}) collective-permute-start(bf16[2,256,512]{2,1,0:T(8,128)(2,1)S(1)} %copy-done.2), channel_id=1, source_target_pairs={{0,1},{1,0},{2,3},{3,2},{4,5},{5,4},{6,7},{7,6},{8,9},{9,8},{10,11... | collective-permute-start | bytes 1572872 | tf_op jit(solution)/shard_map/ppermute | solution.py:22
  66.8 2.4 %collective-permute-start.12 = (bf16[2,256,512]{2,1,0:T(8,128)(2,1)S(1)}, bf16[2,256,512]{2,1,0:T(8,128)(2,1)S(1)}, u32[]{:S(2)}, u32[]{:S(2)}) collective-permute-start(bf16[2,256,512]{2,1,0:T(8,128)(2,1)S(1)} %collective-permute-done.3.refs_3_), channel_id=1, source_target_pairs={{0,1},{1,0},{2,3},{3,2},{4,5},{5,4},{6,7},{7,6},{8,9},{9,8},{10,11... | collective-permute-start | bytes 1572872 | tf_op jit(solution)/shard_map/ppermute | solution.py:22
  69.2 1.9 %collective-permute-start.8 = (bf16[2,256,512]{2,1,0:T(8,128)(2,1)S(1)}, bf16[2,256,512]{2,1,0:T(8,128)(2,1)S(1)}, u32[]{:S(2)}, u32[]{:S(2)}) collective-permute-start(bf16[2,256,512]{2,1,0:T(8,128)(2,1)S(1)} %collective-permute-done.7.refs_5_), channel_id=1, source_target_pairs={{0,1},{1,0},{2,3},{3,2},{4,5},{5,4},{6,7},{7,6},{8,9},{9,8},{10,11... | collective-permute-start | bytes 1572872 | tf_op jit(solution)/shard_map/ppermute | solution.py:22
  71.2 1.5 %sum_4.1.refs_2_ = f32[2,512,512]{2,1,0:T(8,128)S(1)} custom-call(bf16[2,512,4096]{2,1,0:T(8,128)(2,1)S(1)} %screened.1.refs_0_, bf16[2,256,512]{2,1,0:T(8,128)(2,1)S(1)} %collective-permute-done.11.refs_1_, bf16[2,256,512]{2,1,0:T(8,128)(2,1)S(1)} %collective-permute-done.12.refs_2_, bf16[2,256,512]{2,1,0:T(8,128)(2,1)S(1)} %collective-permute-done.14.refs_3_, ...), custom_call_target="tpu_custom_call" | custom-call | flops 1342177280 | bytes 1048576 | tf_op jit(solution)/shard_map/sum_4/pallas_call | solution.py:132
  73.0 0.9 sum_5.1.a_ref
  73.9 0.7 collective-permute-start.16
  74.6 6.6 %collective-permute-start.15 = (bf16[2,256,512]{2,1,0:T(8,128)(2,1)S(1)}, bf16[2,256,512]{2,1,0:T(8,128)(2,1)S(1)}, u32[]{:S(2)}, u32[]{:S(2)}) collective-permute-start(bf16[2,256,512]{2,1,0:T(8,128)(2,1)S(1)} %sum_5.1.a_ref), channel_id=1, source_target_pairs={{0,1008},{1,1009},{2,1010},{3,1011},{4,1012},{5,1013},{6,1014},{7,... | collective-permute-start | bytes 1572872 | tf_op jit(solution)/shard_map/ppermute | solution.py:49
  81.2 0.7 collective-permute-start.17
  81.9 39.8 %collective-permute-done.15.b_ref = bf16[2,256,512]{2,1,0:T(8,128)(2,1)S(1)} collective-permute-done((bf16[2,256,512]{2,1,0:T(8,128)(2,1)S(1)}, bf16[2,256,512]{2,1,0:T(8,128)(2,1)S(1)}, u32[]{:S(2)}, u32[]{:S(2)}) %collective-permute-start.15) | collective-permute-done | bytes 524320 | tf_op jit(solution)/shard_map/ppermute | solution.py:49
  121.7 0.8 copy-done.5
  122.5 2.1 %add.44 = bf16[2,256,512]{2,1,0:T(8,128)(2,1)} custom-call(bf16[2,256,512]{2,1,0:T(8,128)(2,1)} %copy-done.4, bf16[2,256,512]{2,1,0:T(8,128)(2,1)} %copy-done.5), custom_call_target="tpu_custom_call" | custom-call | flops 17179869184 | bytes 1048576 | tf_op jit(solution)/shard_map/add/pallas_call | solution.py:59
  124.6 2.0 %add_convert_fusion = bf16[2,256,512]{2,1,0:T(8,128)(2,1)} fusion(bf16[2,256,512]{2,1,0:T(8,128)(2,1)S(1)} %collective-permute-done.17, bf16[2,256,512]{2,1,0:T(8,128)(2,1)} %add.44), kind=kLoop, calls=%fused_computation | loop fusion | flops 1048576 | bytes 1572864 | tf_op jit(solution)/shard_map/convert_element_type | solution.py:172
  (28 shorter events, 1.2 us)
Async XLA Ops:
  0.0 15.9 %collective-permute-start = (bf16[2,256,512]{2,1,0:T(8,128)(2,1)}, bf16[2,256,512]{2,1,0:T(8,128)(2,1)S(1)}, u32[]{:S(2)}, u32[]{:S(2)}) collective-permute-start(bf16[2,256,512]{2,1,0:T(8,128)(2,1)} %refs_1_.1), channel_id=1, source_target_pairs={{0,2},{2,4},{4,6},{6,8},{8,10},{10,12},{12,14},{14,0},{1,15},{3,1}... | collective-permute-start | bytes 1572872 | tf_op jit(solution)/shard_map/ppermute | solution.py:29
  5.9 24.3 %collective-permute-start.2 = (bf16[2,256,512]{2,1,0:T(8,128)(2,1)}, bf16[2,256,512]{2,1,0:T(8,128)(2,1)S(1)}, u32[]{:S(2)}, u32[]{:S(2)}) collective-permute-start(bf16[2,256,512]{2,1,0:T(8,128)(2,1)} %refs_1_.1), channel_id=1, source_target_pairs={{1,2},{3,4},{5,6},{7,8},{9,10},{11,12},{13,14},{15,0},{0,15},{2,1}... | collective-permute-start | bytes 1572872 | tf_op jit(solution)/shard_map/ppermute | solution.py:29
  9.7 1.6 %copy-start = (bf16[256,4096]{1,0:T(8,128)(2,1)S(1)}, bf16[256,4096]{1,0:T(8,128)(2,1)}, u32[]{:S(2)}) copy-start(bf16[256,4096]{1,0:T(8,128)(2,1)} %fock.1) | copy-start | bytes 6291460
  11.3 1.6 %copy-start.1 = (bf16[256,4096]{1,0:T(8,128)(2,1)S(1)}, bf16[256,4096]{1,0:T(8,128)(2,1)}, u32[]{:S(2)}) copy-start(bf16[256,4096]{1,0:T(8,128)(2,1)} %ladder.1) | copy-start | bytes 6291460
  12.9 25.7 %copy-start.2 = (bf16[2,256,512]{2,1,0:T(8,128)(2,1)S(1)}, bf16[2,256,512]{2,1,0:T(8,128)(2,1)}, u32[]{:S(2)}) copy-start(bf16[2,256,512]{2,1,0:T(8,128)(2,1)} %refs_1_.1) | copy-start | bytes 1572868
  15.9 23.6 %collective-permute-start.1 = (bf16[2,256,512]{2,1,0:T(8,128)(2,1)S(1)}, bf16[2,256,512]{2,1,0:T(8,128)(2,1)S(1)}, u32[]{:S(2)}, u32[]{:S(2)}) collective-permute-start(bf16[2,256,512]{2,1,0:T(8,128)(2,1)S(1)} %collective-permute-done.refs_2_), channel_id=1, source_target_pairs={{0,2},{2,4},{4,6},{6,8},{8,10},{10,12},{12,14},{14,0},{1,15},{3,1}... | collective-permute-start | bytes 1572872 | tf_op jit(solution)/shard_map/ppermute | solution.py:29
  30.3 16.7 %collective-permute-start.6 = (bf16[2,256,512]{2,1,0:T(8,128)(2,1)S(1)}, bf16[2,256,512]{2,1,0:T(8,128)(2,1)S(1)}, u32[]{:S(2)}, u32[]{:S(2)}) collective-permute-start(bf16[2,256,512]{2,1,0:T(8,128)(2,1)S(1)} %collective-permute-done.2.refs_3_), channel_id=1, source_target_pairs={{0,2},{2,4},{4,6},{6,8},{8,10},{10,12},{12,14},{14,0},{1,15},{3,1}... | collective-permute-start | bytes 1572872 | tf_op jit(solution)/shard_map/ppermute | solution.py:29
  33.9 16.8 %collective-permute-start.4 = (bf16[2,256,512]{2,1,0:T(8,128)(2,1)S(1)}, bf16[2,256,512]{2,1,0:T(8,128)(2,1)S(1)}, u32[]{:S(2)}, u32[]{:S(2)}) collective-permute-start(bf16[2,256,512]{2,1,0:T(8,128)(2,1)S(1)} %collective-permute-done.refs_2_), channel_id=1, source_target_pairs={{0,1},{1,0},{2,3},{3,2},{4,5},{5,4},{6,7},{7,6},{8,9},{9,8},{10,11... | collective-permute-start | bytes 1572872 | tf_op jit(solution)/shard_map/ppermute | solution.py:22
  36.6 17.1 %collective-permute-start.5 = (bf16[2,256,512]{2,1,0:T(8,128)(2,1)S(1)}, bf16[2,256,512]{2,1,0:T(8,128)(2,1)S(1)}, u32[]{:S(2)}, u32[]{:S(2)}) collective-permute-start(bf16[2,256,512]{2,1,0:T(8,128)(2,1)S(1)} %collective-permute-done.2.refs_3_), channel_id=1, source_target_pairs={{0,1},{1,0},{2,3},{3,2},{4,5},{5,4},{6,7},{7,6},{8,9},{9,8},{10,11... | collective-permute-start | bytes 1572872 | tf_op jit(solution)/shard_map/ppermute | solution.py:22
  39.6 15.5 %collective-permute-start.3 = (bf16[2,256,512]{2,1,0:T(8,128)(2,1)S(1)}, bf16[2,256,512]{2,1,0:T(8,128)(2,1)S(1)}, u32[]{:S(2)}, u32[]{:S(2)}) collective-permute-start(bf16[2,256,512]{2,1,0:T(8,128)(2,1)S(1)} %collective-permute-done.1.refs_3_), channel_id=1, source_target_pairs={{0,2},{2,4},{4,6},{6,8},{8,10},{10,12},{12,14},{14,0},{1,15},{3,1}... | collective-permute-start | bytes 1572872 | tf_op jit(solution)/shard_map/ppermute | solution.py:29
  44.4 12.6 %collective-permute-start.9 = (bf16[2,256,512]{2,1,0:T(8,128)(2,1)S(1)}, bf16[2,256,512]{2,1,0:T(8,128)(2,1)S(1)}, u32[]{:S(2)}, u32[]{:S(2)}) collective-permute-start(bf16[2,256,512]{2,1,0:T(8,128)(2,1)S(1)} %collective-permute-done.1.refs_3_), channel_id=1, source_target_pairs={{0,1},{1,0},{2,3},{3,2},{4,5},{5,4},{6,7},{7,6},{8,9},{9,8},{10,11... | collective-permute-start | bytes 1572872 | tf_op jit(solution)/shard_map/ppermute | solution.py:22
  47.0 10.0 %collective-permute-start.10 = (bf16[2,256,512]{2,1,0:T(8,128)(2,1)S(1)}, bf16[2,256,512]{2,1,0:T(8,128)(2,1)S(1)}, u32[]{:S(2)}, u32[]{:S(2)}) collective-permute-start(bf16[2,256,512]{2,1,0:T(8,128)(2,1)S(1)} %collective-permute-done.6.refs_4_), channel_id=1, source_target_pairs={{0,1},{1,0},{2,3},{3,2},{4,5},{5,4},{6,7},{7,6},{8,9},{9,8},{10,11... | collective-permute-start | bytes 1572872 | tf_op jit(solution)/shard_map/ppermute | solution.py:22
  50.7 10.2 %collective-permute-start.13 = (bf16[2,256,512]{2,1,0:T(8,128)(2,1)S(1)}, bf16[2,256,512]{2,1,0:T(8,128)(2,1)S(1)}, u32[]{:S(2)}, u32[]{:S(2)}) collective-permute-start(bf16[2,256,512]{2,1,0:T(8,128)(2,1)S(1)} %collective-permute-done.6.refs_4_), channel_id=1, source_target_pairs={{0,2},{2,4},{4,6},{6,8},{8,10},{10,12},{12,14},{14,0},{1,15},{3,1}... | collective-permute-start | bytes 1572872 | tf_op jit(solution)/shard_map/ppermute | solution.py:29
  55.0 14.2 %collective-permute-start.7 = (bf16[2,256,512]{2,1,0:T(8,128)(2,1)S(1)}, bf16[2,256,512]{2,1,0:T(8,128)(2,1)S(1)}, u32[]{:S(2)}, u32[]{:S(2)}) collective-permute-start(bf16[2,256,512]{2,1,0:T(8,128)(2,1)S(1)} %collective-permute-done.3.refs_3_), channel_id=1, source_target_pairs={{0,2},{2,4},{4,6},{6,8},{8,10},{10,12},{12,14},{14,0},{1,15},{3,1}... | collective-permute-start | bytes 1572872 | tf_op jit(solution)/shard_map/ppermute | solution.py:29
  58.0 15.0 %copy-start.3 = (bf16[512,512]{1,0:T(8,128)(2,1)S(1)}, bf16[512,512]{1,0:T(8,128)(2,1)}, u32[]{:S(2)}) copy-start(bf16[512,512]{1,0:T(8,128)(2,1)} %refs_3_.1) | copy-start | bytes 1572868
  60.9 10.3 %collective-permute-start.14 = (bf16[2,256,512]{2,1,0:T(8,128)(2,1)S(1)}, bf16[2,256,512]{2,1,0:T(8,128)(2,1)S(1)}, u32[]{:S(2)}, u32[]{:S(2)}) collective-permute-start(bf16[2,256,512]{2,1,0:T(8,128)(2,1)S(1)} %collective-permute-done.13.refs_4_), channel_id=1, source_target_pairs={{0,1},{1,0},{2,3},{3,2},{4,5},{5,4},{6,7},{7,6},{8,9},{9,8},{10,11... | collective-permute-start | bytes 1572872 | tf_op jit(solution)/shard_map/ppermute | solution.py:22
  64.9 6.3 %collective-permute-start.11 = (bf16[2,256,512]{2,1,0:T(8,128)(2,1)S(1)}, bf16[2,256,512]{2,1,0:T(8,128)(2,1)S(1)}, u32[]{:S(2)}, u32[]{:S(2)}) collective-permute-start(bf16[2,256,512]{2,1,0:T(8,128)(2,1)S(1)} %copy-done.2), channel_id=1, source_target_pairs={{0,1},{1,0},{2,3},{3,2},{4,5},{5,4},{6,7},{7,6},{8,9},{9,8},{10,11... | collective-permute-start | bytes 1572872 | tf_op jit(solution)/shard_map/ppermute | solution.py:22
  66.8 4.4 %collective-permute-start.12 = (bf16[2,256,512]{2,1,0:T(8,128)(2,1)S(1)}, bf16[2,256,512]{2,1,0:T(8,128)(2,1)S(1)}, u32[]{:S(2)}, u32[]{:S(2)}) collective-permute-start(bf16[2,256,512]{2,1,0:T(8,128)(2,1)S(1)} %collective-permute-done.3.refs_3_), channel_id=1, source_target_pairs={{0,1},{1,0},{2,3},{3,2},{4,5},{5,4},{6,7},{7,6},{8,9},{9,8},{10,11... | collective-permute-start | bytes 1572872 | tf_op jit(solution)/shard_map/ppermute | solution.py:22
  69.2 3.8 %collective-permute-start.8 = (bf16[2,256,512]{2,1,0:T(8,128)(2,1)S(1)}, bf16[2,256,512]{2,1,0:T(8,128)(2,1)S(1)}, u32[]{:S(2)}, u32[]{:S(2)}) collective-permute-start(bf16[2,256,512]{2,1,0:T(8,128)(2,1)S(1)} %collective-permute-done.7.refs_5_), channel_id=1, source_target_pairs={{0,1},{1,0},{2,3},{3,2},{4,5},{5,4},{6,7},{7,6},{8,9},{9,8},{10,11... | collective-permute-start | bytes 1572872 | tf_op jit(solution)/shard_map/ppermute | solution.py:22
  73.9 47.8 %copy-start.4 = (bf16[2,256,512]{2,1,0:T(8,128)(2,1)}, bf16[2,256,512]{2,1,0:T(8,128)(2,1)S(1)}, u32[]{:S(2)}) copy-start(bf16[2,256,512]{2,1,0:T(8,128)(2,1)S(1)} %sum_5.1.a_ref) | copy-start | bytes 1572868
  73.9 7.3 %collective-permute-start.16 = (bf16[2,256,512]{2,1,0:T(8,128)(2,1)S(1)}, bf16[2,256,512]{2,1,0:T(8,128)(2,1)S(1)}, u32[]{:S(2)}, u32[]{:S(2)}) collective-permute-start(bf16[2,256,512]{2,1,0:T(8,128)(2,1)S(1)} %sum_5.1.a_ref), channel_id=1, source_target_pairs={{48,144},{50,146},{52,148},{54,150},{56,152},{58,154},{60,156},{62... | collective-permute-start | bytes 1572872 | tf_op jit(solution)/shard_map/ppermute | solution.py:48
  74.6 47.0 %collective-permute-start.15 = (bf16[2,256,512]{2,1,0:T(8,128)(2,1)S(1)}, bf16[2,256,512]{2,1,0:T(8,128)(2,1)S(1)}, u32[]{:S(2)}, u32[]{:S(2)}) collective-permute-start(bf16[2,256,512]{2,1,0:T(8,128)(2,1)S(1)} %sum_5.1.a_ref), channel_id=1, source_target_pairs={{0,1008},{1,1009},{2,1010},{3,1011},{4,1012},{5,1013},{6,1014},{7,... | collective-permute-start | bytes 1572872 | tf_op jit(solution)/shard_map/ppermute | solution.py:49
  81.2 43.4 %collective-permute-start.17 = (bf16[2,256,512]{2,1,0:T(8,128)(2,1)S(1)}, bf16[2,256,512]{2,1,0:T(8,128)(2,1)S(1)}, u32[]{:S(2)}, u32[]{:S(2)}) collective-permute-start(bf16[2,256,512]{2,1,0:T(8,128)(2,1)S(1)} %collective-permute-done.16), channel_id=1, source_target_pairs={{144,240},{146,242},{148,244},{150,246},{152,248},{154,250},{156,2... | collective-permute-start | bytes 1572872 | tf_op jit(solution)/shard_map/ppermute | solution.py:50
  121.7 0.8 copy-start.5

commit v5 on v4

--- a/solution.py
+++ b/solution.py
@@ -12,7 +12,6 @@
 SPLIT = HALF // TILE
 VMEM_LIMIT = 24 * 1024 * 1024
 RING = 16
-ADD_FLOPS = 1 << 34
 HOPS = (None, (0, 0), (1, 0), (1, 1), (2, 0), (2, 1), (3, 0), (3, 1), (4, 0))
 ORDER = (1, 2, 3, -2, -3, 4, 5, -4, -5, 6, -1, -6, -7, 7, 8, -8)
 
@@ -48,22 +47,6 @@
     halfway = lax.ppermute(block, axes, [(at(place, v), at(stop, v)) for place, stop, _, v in legs])
     straight = lax.ppermute(block, axes, [leg for leg in direct if leg[0] not in detour])
     return straight, lax.ppermute(halfway, axes, [(at(stop, v), at(end, v)) for _, stop, end, v in legs])
-
-
-def add_kernel(a_ref, b_ref, out_ref):
-    out_ref[...] = (a_ref[...].astype(jnp.float32) + b_ref[...].astype(jnp.float32)).astype(out_ref.dtype)
-
-
-def add(a, b):
-    vmem = pl.BlockSpec(memory_space=pltpu.VMEM)
-    return pl.pallas_call(
-        add_kernel,
-        out_shape=jax.ShapeDtypeStruct(a.shape, a.dtype),
-        in_specs=[vmem, vmem],
-        out_specs=vmem,
-        cost_estimate=pl.CostEstimate(flops=ADD_FLOPS, bytes_accessed=1 << 20, transcendentals=0),
-        name="add",
-    )(a, b)
 
 
 def after(block, *earlier):
@@ -168,8 +151,8 @@
     late = (core_swap(after(x0, acc)), core_swap(x3), core_swap(after(s3, acc)), s3, x4)
     acc = sum_slots("sum_4", mat, late, 10, acc)
     half_term = sum_slots("sum_5", mat, (core_swap(x4),), 15, acc, couple)
-    straight, detoured = mirror_swap(half_term)
-    return (add(half_term, straight).astype(jnp.float32) + detoured.astype(jnp.float32)).astype(jnp.bfloat16)
+    terms = [term.astype(jnp.float32) for term in (half_term, *mirror_swap(half_term))]
+    return (terms[0] + (terms[1] + terms[2])).astype(jnp.bfloat16)
 
 
 def solution(mesh):

time: 127 us -> 123 us (0.969)
  Pallas kernels: 10.7 us -> 8.63 us
    pallas_call x1 -> x0, Pallas kernels: 2.11 us -> none  [add(): pl.pallas_call(add_kernel, out_shape=jax.ShapeDtypeStruct(a.shape, a.dtyp...]
    unnamed x12 -> x8, local copies, waits for them, and re-layouts: 4 us -> 3.19 us
  transfers between devices with their start and end apart: 18 -> 18, of which waited for: 3 -> 3; matrix products, arithmetic and copies ran while one was open for 1% -> 1% of each run, Pallas kernels for 8% -> 6%
where the time goes in v5:
time: 123 us
  starting transfers between devices  64.9 us (53%)
  waiting for transfers between devices  43 us (35%)
  Pallas kernels  8.63 us (7%)
  local copies, waits for them, and re-layouts  3.96 us (3%)
  other arithmetic  1.79 us (1%)
    ppermute x1, waiting for transfers between devices, mirror_swap(): lax.ppermute(block, axes, [leg for leg in direct if leg[0] not in detour])  39.8 us
    ppermute x7, starting transfers between devices, ring_step(): return lax.ppermute(block, 'virt', route)  35.9 us
    ppermute x8, starting transfers between devices, core_swap(): return lax.ppermute(block, 'virt', [(v, v ^ 1) for v in range(count)])  21.1 us
    ppermute x1, starting transfers between devices, mirror_swap(): lax.ppermute(block, axes, [leg for leg in direct if leg[0] not in detour])  6.57 us
    pallas_call x5, Pallas kernels, sum_slots(): pl.pallas_call(functools.partial(sum_kernel, pairs, slots, acc is not Non...  5.59 us
    unnamed x8, local copies, waits for them, and re-layouts  3.19 us
    pallas_call x1, Pallas kernels, screened(): pl.pallas_call(functools.partial(screen_kernel, pairs), out_shape=jax.Sha...  3.04 us
    ppermute x7, waiting for transfers between devices, ring_step(): return lax.ppermute(block, 'virt', route)  2.9 us
  transfers between devices with their start and end apart: 18, of which 3 were waited for; matrix products, arithmetic and copies ran while one was open for 1% of the time, Pallas kernels for 6%

profile of v5, /device:TPU:1, one launch (start us, length us, event | category | flops | bytes accessed | tf_op | source)
XLA Modules:
  0.0 122.6 jit_solution(6208926755557893561)
XLA Ops:
  0.0 5.9 %collective-permute-start = (bf16[2,256,512]{2,1,0:T(8,128)(2,1)}, bf16[2,256,512]{2,1,0:T(8,128)(2,1)S(1)}, u32[]{:S(2)}, u32[]{:S(2)}) collective-permute-start(bf16[2,256,512]{2,1,0:T(8,128)(2,1)} %refs_1_.1), channel_id=1, source_target_pairs={{0,2},{2,4},{4,6},{6,8},{8,10},{10,12},{12,14},{14,0},{1,15},{3,1}... | collective-permute-start | bytes 1572872 | tf_op jit(solution)/shard_map/ppermute | solution.py:28
  5.9 2.2 %collective-permute-start.2 = (bf16[2,256,512]{2,1,0:T(8,128)(2,1)}, bf16[2,256,512]{2,1,0:T(8,128)(2,1)S(1)}, u32[]{:S(2)}, u32[]{:S(2)}) collective-permute-start(bf16[2,256,512]{2,1,0:T(8,128)(2,1)} %refs_1_.1), channel_id=1, source_target_pairs={{1,2},{3,4},{5,6},{7,8},{9,10},{11,12},{13,14},{15,0},{0,15},{2,1}... | collective-permute-start | bytes 1572872 | tf_op jit(solution)/shard_map/ppermute | solution.py:28
  8.1 0.8 copy.8
  9.0 0.7 fusion.2.slot_ref
  9.7 1.6 %copy-done = bf16[256,4096]{1,0:T(8,128)(2,1)S(1)} copy-done((bf16[256,4096]{1,0:T(8,128)(2,1)S(1)}, bf16[256,4096]{1,0:T(8,128)(2,1)}, u32[]{:S(2)}) %copy-start) | copy-done | bytes 2097176
  11.3 1.6 %copy-done.1 = bf16[256,4096]{1,0:T(8,128)(2,1)S(1)} copy-done((bf16[256,4096]{1,0:T(8,128)(2,1)S(1)}, bf16[256,4096]{1,0:T(8,128)(2,1)}, u32[]{:S(2)}) %copy-start.1) | copy-done | bytes 2097176
  12.9 3.0 %screened.1.refs_0_ = bf16[2,512,4096]{2,1,0:T(8,128)(2,1)S(1)} custom-call(s32[16]{0:T(128)S(1)} %fusion.2.slot_ref, s32[4,32]{1,0:T(4,128)S(1)} %convert_element_type.15.mask_ref, bf16[256,4096]{1,0:T(8,128)(2,1)S(1)} %copy-done, bf16[256,4096]{1,0:T(8,128)(2,1)S(1)} %copy-done.1), custom_call_target="tpu_custom_call" | custom-call | bytes 4194304 | tf_op jit(solution)/shard_map/screened/pallas_call | solution.py:77
  15.9 14.3 %collective-permute-start.1 = (bf16[2,256,512]{2,1,0:T(8,128)(2,1)S(1)}, bf16[2,256,512]{2,1,0:T(8,128)(2,1)S(1)}, u32[]{:S(2)}, u32[]{:S(2)}) collective-permute-start(bf16[2,256,512]{2,1,0:T(8,128)(2,1)S(1)} %collective-permute-done.refs_2_), channel_id=1, source_target_pairs={{0,2},{2,4},{4,6},{6,8},{8,10},{10,12},{12,14},{14,0},{1,15},{3,1}... | collective-permute-start | bytes 1572872 | tf_op jit(solution)/shard_map/ppermute | solution.py:28
  30.3 3.6 %collective-permute-start.6 = (bf16[2,256,512]{2,1,0:T(8,128)(2,1)S(1)}, bf16[2,256,512]{2,1,0:T(8,128)(2,1)S(1)}, u32[]{:S(2)}, u32[]{:S(2)}) collective-permute-start(bf16[2,256,512]{2,1,0:T(8,128)(2,1)S(1)} %collective-permute-done.2.refs_3_), channel_id=1, source_target_pairs={{0,2},{2,4},{4,6},{6,8},{8,10},{10,12},{12,14},{14,0},{1,15},{3,1}... | collective-permute-start | bytes 1572872 | tf_op jit(solution)/shard_map/ppermute | solution.py:28
  33.9 2.7 %collective-permute-start.4 = (bf16[2,256,512]{2,1,0:T(8,128)(2,1)S(1)}, bf16[2,256,512]{2,1,0:T(8,128)(2,1)S(1)}, u32[]{:S(2)}, u32[]{:S(2)}) collective-permute-start(bf16[2,256,512]{2,1,0:T(8,128)(2,1)S(1)} %collective-permute-done.refs_2_), channel_id=1, source_target_pairs={{0,1},{1,0},{2,3},{3,2},{4,5},{5,4},{6,7},{7,6},{8,9},{9,8},{10,11... | collective-permute-start | bytes 1572872 | tf_op jit(solution)/shard_map/ppermute | solution.py:21
  36.6 1.9 %collective-permute-start.5 = (bf16[2,256,512]{2,1,0:T(8,128)(2,1)S(1)}, bf16[2,256,512]{2,1,0:T(8,128)(2,1)S(1)}, u32[]{:S(2)}, u32[]{:S(2)}) collective-permute-start(bf16[2,256,512]{2,1,0:T(8,128)(2,1)S(1)} %collective-permute-done.2.refs_3_), channel_id=1, source_target_pairs={{0,1},{1,0},{2,3},{3,2},{4,5},{5,4},{6,7},{7,6},{8,9},{9,8},{10,11... | collective-permute-start | bytes 1572872 | tf_op jit(solution)/shard_map/ppermute | solution.py:21
  38.6 1.0 sum_1.1.refs_5_
  39.6 4.9 %collective-permute-start.3 = (bf16[2,256,512]{2,1,0:T(8,128)(2,1)S(1)}, bf16[2,256,512]{2,1,0:T(8,128)(2,1)S(1)}, u32[]{:S(2)}, u32[]{:S(2)}) collective-permute-start(bf16[2,256,512]{2,1,0:T(8,128)(2,1)S(1)} %collective-permute-done.1.refs_3_), channel_id=1, source_target_pairs={{0,2},{2,4},{4,6},{6,8},{8,10},{10,12},{12,14},{14,0},{1,15},{3,1}... | collective-permute-start | bytes 1572872 | tf_op jit(solution)/shard_map/ppermute | solution.py:28
  44.4 2.5 %collective-permute-start.9 = (bf16[2,256,512]{2,1,0:T(8,128)(2,1)S(1)}, bf16[2,256,512]{2,1,0:T(8,128)(2,1)S(1)}, u32[]{:S(2)}, u32[]{:S(2)}) collective-permute-start(bf16[2,256,512]{2,1,0:T(8,128)(2,1)S(1)} %collective-permute-done.1.refs_3_), channel_id=1, source_target_pairs={{0,1},{1,0},{2,3},{3,2},{4,5},{5,4},{6,7},{7,6},{8,9},{9,8},{10,11... | collective-permute-start | bytes 1572872 | tf_op jit(solution)/shard_map/ppermute | solution.py:21
  47.0 3.7 %collective-permute-start.10 = (bf16[2,256,512]{2,1,0:T(8,128)(2,1)S(1)}, bf16[2,256,512]{2,1,0:T(8,128)(2,1)S(1)}, u32[]{:S(2)}, u32[]{:S(2)}) collective-permute-start(bf16[2,256,512]{2,1,0:T(8,128)(2,1)S(1)} %collective-permute-done.6.refs_4_), channel_id=1, source_target_pairs={{0,1},{1,0},{2,3},{3,2},{4,5},{5,4},{6,7},{7,6},{8,9},{9,8},{10,11... | collective-permute-start | bytes 1572872 | tf_op jit(solution)/shard_map/ppermute | solution.py:21
  50.7 3.1 %collective-permute-start.13 = (bf16[2,256,512]{2,1,0:T(8,128)(2,1)S(1)}, bf16[2,256,512]{2,1,0:T(8,128)(2,1)S(1)}, u32[]{:S(2)}, u32[]{:S(2)}) collective-permute-start(bf16[2,256,512]{2,1,0:T(8,128)(2,1)S(1)} %collective-permute-done.6.refs_4_), channel_id=1, source_target_pairs={{0,2},{2,4},{4,6},{6,8},{8,10},{10,12},{12,14},{14,0},{1,15},{3,1}... | collective-permute-start | bytes 1572872 | tf_op jit(solution)/shard_map/ppermute | solution.py:28
  53.8 1.2 %sum_2.1.refs_4_ = f32[2,512,512]{2,1,0:T(8,128)S(1)} custom-call(bf16[2,512,4096]{2,1,0:T(8,128)(2,1)S(1)} %screened.1.refs_0_, bf16[2,256,512]{2,1,0:T(8,128)(2,1)S(1)} %collective-permute-done.4.refs_1_, bf16[2,256,512]{2,1,0:T(8,128)(2,1)S(1)} %collective-permute-done.5.refs_2_, bf16[2,256,512]{2,1,0:T(8,128)(2,1)S(1)} %collective-permute-done.1.refs_3_, ...), custom_call_target="tpu_custom_call" | custom-call | flops 1073741824 | bytes 1048576 | tf_op jit(solution)/shard_map/sum_2/pallas_call | solution.py:115
  55.0 1.9 %collective-permute-start.7 = (bf16[2,256,512]{2,1,0:T(8,128)(2,1)S(1)}, bf16[2,256,512]{2,1,0:T(8,128)(2,1)S(1)}, u32[]{:S(2)}, u32[]{:S(2)}) collective-permute-start(bf16[2,256,512]{2,1,0:T(8,128)(2,1)S(1)} %collective-permute-done.3.refs_3_), channel_id=1, source_target_pairs={{0,2},{2,4},{4,6},{6,8},{8,10},{10,12},{12,14},{14,0},{1,15},{3,1}... | collective-permute-start | bytes 1572872 | tf_op jit(solution)/shard_map/ppermute | solution.py:28
  57.0 1.0 sum_3.1.refs_6_
  58.0 2.9 %collective-permute-done.13.refs_4_ = bf16[2,256,512]{2,1,0:T(8,128)(2,1)S(1)} collective-permute-done((bf16[2,256,512]{2,1,0:T(8,128)(2,1)S(1)}, bf16[2,256,512]{2,1,0:T(8,128)(2,1)S(1)}, u32[]{:S(2)}, u32[]{:S(2)}) %collective-permute-start.13) | collective-permute-done | bytes 524320 | tf_op jit(solution)/shard_map/ppermute | solution.py:28
  60.9 4.0 %collective-permute-start.14 = (bf16[2,256,512]{2,1,0:T(8,128)(2,1)S(1)}, bf16[2,256,512]{2,1,0:T(8,128)(2,1)S(1)}, u32[]{:S(2)}, u32[]{:S(2)}) collective-permute-start(bf16[2,256,512]{2,1,0:T(8,128)(2,1)S(1)} %collective-permute-done.13.refs_4_), channel_id=1, source_target_pairs={{0,1},{1,0},{2,3},{3,2},{4,5},{5,4},{6,7},{7,6},{8,9},{9,8},{10,11... | collective-permute-start | bytes 1572872 | tf_op jit(solution)/shard_map/ppermute | solution.py:21
  64.9 1.9 %collective-permute-start.11 = (bf16[2,256,512]{2,1,0:T(8,128)(2,1)S(1)}, bf16[2,256,512]{2,1,0:T(8,128)(2,1)S(1)}, u32[]{:S(2)}, u32[]{:S(2)}) collective-permute-start(bf16[2,256,512]{2,1,0:T(8,128)(2,1)S(1)} %copy-done.2), channel_id=1, source_target_pairs={{0,1},{1,0},{2,3},{3,2},{4,5},{5,4},{6,7},{7,6},{8,9},{9,8},{10,11... | collective-permute-start | bytes 1572872 | tf_op jit(solution)/shard_map/ppermute | solution.py:21
  66.8 2.4 %collective-permute-start.12 = (bf16[2,256,512]{2,1,0:T(8,128)(2,1)S(1)}, bf16[2,256,512]{2,1,0:T(8,128)(2,1)S(1)}, u32[]{:S(2)}, u32[]{:S(2)}) collective-permute-start(bf16[2,256,512]{2,1,0:T(8,128)(2,1)S(1)} %collective-permute-done.3.refs_3_), channel_id=1, source_target_pairs={{0,1},{1,0},{2,3},{3,2},{4,5},{5,4},{6,7},{7,6},{8,9},{9,8},{10,11... | collective-permute-start | bytes 1572872 | tf_op jit(solution)/shard_map/ppermute | solution.py:21
  69.2 1.9 %collective-permute-start.8 = (bf16[2,256,512]{2,1,0:T(8,128)(2,1)S(1)}, bf16[2,256,512]{2,1,0:T(8,128)(2,1)S(1)}, u32[]{:S(2)}, u32[]{:S(2)}) collective-permute-start(bf16[2,256,512]{2,1,0:T(8,128)(2,1)S(1)} %collective-permute-done.7.refs_5_), channel_id=1, source_target_pairs={{0,1},{1,0},{2,3},{3,2},{4,5},{5,4},{6,7},{7,6},{8,9},{9,8},{10,11... | collective-permute-start | bytes 1572872 | tf_op jit(solution)/shard_map/ppermute | solution.py:21
  71.2 1.5 %sum_4.1.refs_2_ = f32[2,512,512]{2,1,0:T(8,128)S(1)} custom-call(bf16[2,512,4096]{2,1,0:T(8,128)(2,1)S(1)} %screened.1.refs_0_, bf16[2,256,512]{2,1,0:T(8,128)(2,1)S(1)} %collective-permute-done.11.refs_1_, bf16[2,256,512]{2,1,0:T(8,128)(2,1)S(1)} %collective-permute-done.12.refs_2_, bf16[2,256,512]{2,1,0:T(8,128)(2,1)S(1)} %collective-permute-done.14.refs_3_, ...), custom_call_target="tpu_custom_call" | custom-call | flops 1342177280 | bytes 1048576 | tf_op jit(solution)/shard_map/sum_4/pallas_call | solution.py:115
  72.7 0.3 collective-permute-done.8.refs_1_
  73.0 0.9 sum_5.1
  73.9 0.7 collective-permute-start.16
  74.6 6.6 %collective-permute-start.15 = (bf16[2,256,512]{2,1,0:T(8,128)(2,1)S(1)}, bf16[2,256,512]{2,1,0:T(8,128)(2,1)S(1)}, u32[]{:S(2)}, u32[]{:S(2)}) collective-permute-start(bf16[2,256,512]{2,1,0:T(8,128)(2,1)S(1)} %sum_5.1), channel_id=1, source_target_pairs={{0,1008},{1,1009},{2,1010},{3,1011},{4,1012},{5,1013},{6,1014},{7,... | collective-permute-start | bytes 1572872 | tf_op jit(solution)/shard_map/ppermute | solution.py:48
  81.2 0.7 collective-permute-start.17
  81.9 39.8 %collective-permute-done.15 = bf16[2,256,512]{2,1,0:T(8,128)(2,1)S(1)} collective-permute-done((bf16[2,256,512]{2,1,0:T(8,128)(2,1)S(1)}, bf16[2,256,512]{2,1,0:T(8,128)(2,1)S(1)}, u32[]{:S(2)}, u32[]{:S(2)}) %collective-permute-start.15) | collective-permute-done | bytes 524320 | tf_op jit(solution)/shard_map/ppermute | solution.py:48
  121.6 1.0 add_convert_fusion
  (23 shorter events, 0.1 us)
Async XLA Ops:
  0.0 15.9 %collective-permute-start = (bf16[2,256,512]{2,1,0:T(8,128)(2,1)}, bf16[2,256,512]{2,1,0:T(8,128)(2,1)S(1)}, u32[]{:S(2)}, u32[]{:S(2)}) collective-permute-start(bf16[2,256,512]{2,1,0:T(8,128)(2,1)} %refs_1_.1), channel_id=1, source_target_pairs={{0,2},{2,4},{4,6},{6,8},{8,10},{10,12},{12,14},{14,0},{1,15},{3,1}... | collective-permute-start | bytes 1572872 | tf_op jit(solution)/shard_map/ppermute | solution.py:28
  5.9 24.3 %collective-permute-start.2 = (bf16[2,256,512]{2,1,0:T(8,128)(2,1)}, bf16[2,256,512]{2,1,0:T(8,128)(2,1)S(1)}, u32[]{:S(2)}, u32[]{:S(2)}) collective-permute-start(bf16[2,256,512]{2,1,0:T(8,128)(2,1)} %refs_1_.1), channel_id=1, source_target_pairs={{1,2},{3,4},{5,6},{7,8},{9,10},{11,12},{13,14},{15,0},{0,15},{2,1}... | collective-permute-start | bytes 1572872 | tf_op jit(solution)/shard_map/ppermute | solution.py:28
  9.7 1.6 %copy-start = (bf16[256,4096]{1,0:T(8,128)(2,1)S(1)}, bf16[256,4096]{1,0:T(8,128)(2,1)}, u32[]{:S(2)}) copy-start(bf16[256,4096]{1,0:T(8,128)(2,1)} %fock.1) | copy-start | bytes 6291460
  11.3 1.6 %copy-start.1 = (bf16[256,4096]{1,0:T(8,128)(2,1)S(1)}, bf16[256,4096]{1,0:T(8,128)(2,1)}, u32[]{:S(2)}) copy-start(bf16[256,4096]{1,0:T(8,128)(2,1)} %ladder.1) | copy-start | bytes 6291460
  12.9 25.7 %copy-start.2 = (bf16[2,256,512]{2,1,0:T(8,128)(2,1)S(1)}, bf16[2,256,512]{2,1,0:T(8,128)(2,1)}, u32[]{:S(2)}) copy-start(bf16[2,256,512]{2,1,0:T(8,128)(2,1)} %refs_1_.1) | copy-start | bytes 1572868
  15.9 23.6 %collective-permute-start.1 = (bf16[2,256,512]{2,1,0:T(8,128)(2,1)S(1)}, bf16[2,256,512]{2,1,0:T(8,128)(2,1)S(1)}, u32[]{:S(2)}, u32[]{:S(2)}) collective-permute-start(bf16[2,256,512]{2,1,0:T(8,128)(2,1)S(1)} %collective-permute-done.refs_2_), channel_id=1, source_target_pairs={{0,2},{2,4},{4,6},{6,8},{8,10},{10,12},{12,14},{14,0},{1,15},{3,1}... | collective-permute-start | bytes 1572872 | tf_op jit(solution)/shard_map/ppermute | solution.py:28
  30.3 16.7 %collective-permute-start.6 = (bf16[2,256,512]{2,1,0:T(8,128)(2,1)S(1)}, bf16[2,256,512]{2,1,0:T(8,128)(2,1)S(1)}, u32[]{:S(2)}, u32[]{:S(2)}) collective-permute-start(bf16[2,256,512]{2,1,0:T(8,128)(2,1)S(1)} %collective-permute-done.2.refs_3_), channel_id=1, source_target_pairs={{0,2},{2,4},{4,6},{6,8},{8,10},{10,12},{12,14},{14,0},{1,15},{3,1}... | collective-permute-start | bytes 1572872 | tf_op jit(solution)/shard_map/ppermute | solution.py:28
  33.9 16.8 %collective-permute-start.4 = (bf16[2,256,512]{2,1,0:T(8,128)(2,1)S(1)}, bf16[2,256,512]{2,1,0:T(8,128)(2,1)S(1)}, u32[]{:S(2)}, u32[]{:S(2)}) collective-permute-start(bf16[2,256,512]{2,1,0:T(8,128)(2,1)S(1)} %collective-permute-done.refs_2_), channel_id=1, source_target_pairs={{0,1},{1,0},{2,3},{3,2},{4,5},{5,4},{6,7},{7,6},{8,9},{9,8},{10,11... | collective-permute-start | bytes 1572872 | tf_op jit(solution)/shard_map/ppermute | solution.py:21
  36.6 17.1 %collective-permute-start.5 = (bf16[2,256,512]{2,1,0:T(8,128)(2,1)S(1)}, bf16[2,256,512]{2,1,0:T(8,128)(2,1)S(1)}, u32[]{:S(2)}, u32[]{:S(2)}) collective-permute-start(bf16[2,256,512]{2,1,0:T(8,128)(2,1)S(1)} %collective-permute-done.2.refs_3_), channel_id=1, source_target_pairs={{0,1},{1,0},{2,3},{3,2},{4,5},{5,4},{6,7},{7,6},{8,9},{9,8},{10,11... | collective-permute-start | bytes 1572872 | tf_op jit(solution)/shard_map/ppermute | solution.py:21
  39.6 15.5 %collective-permute-start.3 = (bf16[2,256,512]{2,1,0:T(8,128)(2,1)S(1)}, bf16[2,256,512]{2,1,0:T(8,128)(2,1)S(1)}, u32[]{:S(2)}, u32[]{:S(2)}) collective-permute-start(bf16[2,256,512]{2,1,0:T(8,128)(2,1)S(1)} %collective-permute-done.1.refs_3_), channel_id=1, source_target_pairs={{0,2},{2,4},{4,6},{6,8},{8,10},{10,12},{12,14},{14,0},{1,15},{3,1}... | collective-permute-start | bytes 1572872 | tf_op jit(solution)/shard_map/ppermute | solution.py:28
  44.4 12.6 %collective-permute-start.9 = (bf16[2,256,512]{2,1,0:T(8,128)(2,1)S(1)}, bf16[2,256,512]{2,1,0:T(8,128)(2,1)S(1)}, u32[]{:S(2)}, u32[]{:S(2)}) collective-permute-start(bf16[2,256,512]{2,1,0:T(8,128)(2,1)S(1)} %collective-permute-done.1.refs_3_), channel_id=1, source_target_pairs={{0,1},{1,0},{2,3},{3,2},{4,5},{5,4},{6,7},{7,6},{8,9},{9,8},{10,11... | collective-permute-start | bytes 1572872 | tf_op jit(solution)/shard_map/ppermute | solution.py:21
  47.0 10.0 %collective-permute-start.10 = (bf16[2,256,512]{2,1,0:T(8,128)(2,1)S(1)}, bf16[2,256,512]{2,1,0:T(8,128)(2,1)S(1)}, u32[]{:S(2)}, u32[]{:S(2)}) collective-permute-start(bf16[2,256,512]{2,1,0:T(8,128)(2,1)S(1)} %collective-permute-done.6.refs_4_), channel_id=1, source_target_pairs={{0,1},{1,0},{2,3},{3,2},{4,5},{5,4},{6,7},{7,6},{8,9},{9,8},{10,11... | collective-permute-start | bytes 1572872 | tf_op jit(solution)/shard_map/ppermute | solution.py:21
  50.7 10.2 %collective-permute-start.13 = (bf16[2,256,512]{2,1,0:T(8,128)(2,1)S(1)}, bf16[2,256,512]{2,1,0:T(8,128)(2,1)S(1)}, u32[]{:S(2)}, u32[]{:S(2)}) collective-permute-start(bf16[2,256,512]{2,1,0:T(8,128)(2,1)S(1)} %collective-permute-done.6.refs_4_), channel_id=1, source_target_pairs={{0,2},{2,4},{4,6},{6,8},{8,10},{10,12},{12,14},{14,0},{1,15},{3,1}... | collective-permute-start | bytes 1572872 | tf_op jit(solution)/shard_map/ppermute | solution.py:28
  55.0 14.2 %collective-permute-start.7 = (bf16[2,256,512]{2,1,0:T(8,128)(2,1)S(1)}, bf16[2,256,512]{2,1,0:T(8,128)(2,1)S(1)}, u32[]{:S(2)}, u32[]{:S(2)}) collective-permute-start(bf16[2,256,512]{2,1,0:T(8,128)(2,1)S(1)} %collective-permute-done.3.refs_3_), channel_id=1, source_target_pairs={{0,2},{2,4},{4,6},{6,8},{8,10},{10,12},{12,14},{14,0},{1,15},{3,1}... | collective-permute-start | bytes 1572872 | tf_op jit(solution)/shard_map/ppermute | solution.py:28
  58.0 15.0 %copy-start.3 = (bf16[512,512]{1,0:T(8,128)(2,1)S(1)}, bf16[512,512]{1,0:T(8,128)(2,1)}, u32[]{:S(2)}) copy-start(bf16[512,512]{1,0:T(8,128)(2,1)} %refs_3_.1) | copy-start | bytes 1572868
  60.9 10.3 %collective-permute-start.14 = (bf16[2,256,512]{2,1,0:T(8,128)(2,1)S(1)}, bf16[2,256,512]{2,1,0:T(8,128)(2,1)S(1)}, u32[]{:S(2)}, u32[]{:S(2)}) collective-permute-start(bf16[2,256,512]{2,1,0:T(8,128)(2,1)S(1)} %collective-permute-done.13.refs_4_), channel_id=1, source_target_pairs={{0,1},{1,0},{2,3},{3,2},{4,5},{5,4},{6,7},{7,6},{8,9},{9,8},{10,11... | collective-permute-start | bytes 1572872 | tf_op jit(solution)/shard_map/ppermute | solution.py:21
  64.9 6.3 %collective-permute-start.11 = (bf16[2,256,512]{2,1,0:T(8,128)(2,1)S(1)}, bf16[2,256,512]{2,1,0:T(8,128)(2,1)S(1)}, u32[]{:S(2)}, u32[]{:S(2)}) collective-permute-start(bf16[2,256,512]{2,1,0:T(8,128)(2,1)S(1)} %copy-done.2), channel_id=1, source_target_pairs={{0,1},{1,0},{2,3},{3,2},{4,5},{5,4},{6,7},{7,6},{8,9},{9,8},{10,11... | collective-permute-start | bytes 1572872 | tf_op jit(solution)/shard_map/ppermute | solution.py:21
  66.8 4.4 %collective-permute-start.12 = (bf16[2,256,512]{2,1,0:T(8,128)(2,1)S(1)}, bf16[2,256,512]{2,1,0:T(8,128)(2,1)S(1)}, u32[]{:S(2)}, u32[]{:S(2)}) collective-permute-start(bf16[2,256,512]{2,1,0:T(8,128)(2,1)S(1)} %collective-permute-done.3.refs_3_), channel_id=1, source_target_pairs={{0,1},{1,0},{2,3},{3,2},{4,5},{5,4},{6,7},{7,6},{8,9},{9,8},{10,11... | collective-permute-start | bytes 1572872 | tf_op jit(solution)/shard_map/ppermute | solution.py:21
  69.2 3.8 %collective-permute-start.8 = (bf16[2,256,512]{2,1,0:T(8,128)(2,1)S(1)}, bf16[2,256,512]{2,1,0:T(8,128)(2,1)S(1)}, u32[]{:S(2)}, u32[]{:S(2)}) collective-permute-start(bf16[2,256,512]{2,1,0:T(8,128)(2,1)S(1)} %collective-permute-done.7.refs_5_), channel_id=1, source_target_pairs={{0,1},{1,0},{2,3},{3,2},{4,5},{5,4},{6,7},{7,6},{8,9},{9,8},{10,11... | collective-permute-start | bytes 1572872 | tf_op jit(solution)/shard_map/ppermute | solution.py:21
  73.9 7.3 %collective-permute-start.16 = (bf16[2,256,512]{2,1,0:T(8,128)(2,1)S(1)}, bf16[2,256,512]{2,1,0:T(8,128)(2,1)S(1)}, u32[]{:S(2)}, u32[]{:S(2)}) collective-permute-start(bf16[2,256,512]{2,1,0:T(8,128)(2,1)S(1)} %sum_5.1), channel_id=1, source_target_pairs={{48,144},{50,146},{52,148},{54,150},{56,152},{58,154},{60,156},{62... | collective-permute-start | bytes 1572872 | tf_op jit(solution)/shard_map/ppermute | solution.py:47
  74.6 47.0 %collective-permute-start.15 = (bf16[2,256,512]{2,1,0:T(8,128)(2,1)S(1)}, bf16[2,256,512]{2,1,0:T(8,128)(2,1)S(1)}, u32[]{:S(2)}, u32[]{:S(2)}) collective-permute-start(bf16[2,256,512]{2,1,0:T(8,128)(2,1)S(1)} %sum_5.1), channel_id=1, source_target_pairs={{0,1008},{1,1009},{2,1010},{3,1011},{4,1012},{5,1013},{6,1014},{7,... | collective-permute-start | bytes 1572872 | tf_op jit(solution)/shard_map/ppermute | solution.py:48
  81.2 40.5 %collective-permute-start.17 = (bf16[2,256,512]{2,1,0:T(8,128)(2,1)S(1)}, bf16[2,256,512]{2,1,0:T(8,128)(2,1)S(1)}, u32[]{:S(2)}, u32[]{:S(2)}) collective-permute-start(bf16[2,256,512]{2,1,0:T(8,128)(2,1)S(1)} %collective-permute-done.16), channel_id=1, source_target_pairs={{144,240},{146,242},{148,244},{150,246},{152,248},{154,250},{156,2... | collective-permute-start | bytes 1572872 | tf_op jit(solution)/shard_map/ppermute | solution.py:49

commit v6 on v5

--- a/solution.py
+++ b/solution.py
@@ -33,20 +33,35 @@
     return count - 1 - sum(((place >> b) & 1) << (nbits - 1 - b) for b in range(nbits))
 
 
+def detours(rows):
+    moves = []
+    for x in range(rows):
+        for core in range(2):
+            moves.append(((x, RING // 4 - 1), (x, RING // 2), core))
+            moves.append(((x, RING - RING // 4), (x, RING // 2 - 1), core))
+    for z, row in ((5, 1), (6, 2), (9, 1), (10, 2)):
+        moves.append(((0, z), (row, z), 0))
+        moves.append(((rows - 1, RING - 1 - z), (rows - 1 - row, RING - 1 - z), 1))
+    return [(place[0] * RING + place[1], stop[0] * RING + stop[1], core) for place, stop, core in moves]
+
+
 def mirror_swap(block):
     count, across = lax.axis_size("pair"), lax.axis_size("virt")
-    axes, quarter = ("pair", "virt"), RING // 4
-    stops = {}
-    for row in range(0, count, RING):
-        stops[row + quarter - 1] = row + RING // 2 + 1
-        stops[row + RING - quarter] = row + RING // 2 - 2
-    at = lambda place, v: place * across + v
-    legs = [(place, stop, mirror_of(place, count), v) for place, stop in stops.items() for v in range(0, across, 2)]
-    detour = {at(place, v) for place, _, _, v in legs}
-    direct = [(at(place, v), at(mirror_of(place, count), v)) for place in range(count) for v in range(across)]
-    halfway = lax.ppermute(block, axes, [(at(place, v), at(stop, v)) for place, stop, _, v in legs])
-    straight = lax.ppermute(block, axes, [leg for leg in direct if leg[0] not in detour])
-    return straight, lax.ppermute(halfway, axes, [(at(stop, v), at(end, v)) for _, stop, end, v in legs])
+    axes = ("pair", "virt")
+    first, second, direct = [], [], []
+    moves = {(place, core): stop for place, stop, core in detours(count // RING)}
+    for place in range(count):
+        for v in range(across):
+            here, end = place * across + v, mirror_of(place, count) * across + v
+            if (place, v % 2) in moves:
+                stop = moves[place, v % 2] * across + v
+                first.append((here, stop))
+                second.append((stop, end))
+            else:
+                direct.append((here, end))
+    halfway = lax.ppermute(block, axes, first)
+    straight = lax.ppermute(block, axes, direct)
+    return straight, lax.ppermute(halfway, axes, second)
 
 
 def after(block, *earlier):
@@ -147,9 +162,8 @@
     x3, s3 = ring_step(after(x2, acc)), ring_step(s2)
     acc = sum_slots("sum_2", mat, (core_swap(x1), core_swap(s1), x2, s2), 3, acc)
     x4 = ring_step(after(x3, acc))
-    acc = sum_slots("sum_3", mat, (core_swap(x2), core_swap(s2), x3), 7, acc)
-    late = (core_swap(after(x0, acc)), core_swap(x3), core_swap(after(s3, acc)), s3, x4)
-    acc = sum_slots("sum_4", mat, late, 10, acc)
+    acc = sum_slots("sum_3", mat, (core_swap(x2), core_swap(s2), x3, core_swap(x0)), 7, acc)
+    acc = sum_slots("sum_4", mat, (core_swap(x3), core_swap(s3), s3, x4), 11, acc)
     half_term = sum_slots("sum_5", mat, (core_swap(x4),), 15, acc, couple)
     terms = [term.astype(jnp.float32) for term in (half_term, *mirror_swap(half_term))]
     return (terms[0] + (terms[1] + terms[2])).astype(jnp.bfloat16)

time: 123 us -> 122 us (level)
  the two profiles are of different devices: /device:TPU:1 before, /device:TPU:28 now
where the time goes in v6:
time: 122 us; the launch traced here: 121 us
  starting transfers between devices  65.1 us (53%)
  waiting for transfers between devices  41.7 us (34%)
  Pallas kernels  8.58 us (7%)
  local copies, waits for them, and re-layouts  3.96 us (3%)
  other arithmetic  1.78 us (1%)
    ppermute x1, waiting for transfers between devices, mirror_swap(): straight = lax.ppermute(block, axes, direct)  40.9 us
    ppermute x7, starting transfers between devices, ring_step(): return lax.ppermute(block, 'virt', route)  28 us
    ppermute x1, starting transfers between devices, mirror_swap(): straight = lax.ppermute(block, axes, direct)  18.8 us
    ppermute x8, starting transfers between devices, core_swap(): return lax.ppermute(block, 'virt', [(v, v ^ 1) for v in range(count)])  16.8 us
    pallas_call x5, Pallas kernels, sum_slots(): pl.pallas_call(functools.partial(sum_kernel, pairs, slots, acc is not Non...  5.59 us
    unnamed x8, local copies, waits for them, and re-layouts  3.19 us
    pallas_call x1, Pallas kernels, screened(): pl.pallas_call(functools.partial(screen_kernel, pairs), out_shape=jax.Sha...  2.99 us
  transfers between devices with their start and end apart: 18, of which 2 were waited for; matrix products, arithmetic and copies ran while one was open for 1% of the time, Pallas kernels for 6%

profile of v6, /device:TPU:28, one launch (start us, length us, event | category | flops | bytes accessed | tf_op | source)
XLA Modules:
  0.0 121.5 jit_solution(12504604378533519839)
XLA Ops:
  0.0 4.7 %collective-permute-start = (bf16[2,256,512]{2,1,0:T(8,128)(2,1)}, bf16[2,256,512]{2,1,0:T(8,128)(2,1)S(1)}, u32[]{:S(2)}, u32[]{:S(2)}) collective-permute-start(bf16[2,256,512]{2,1,0:T(8,128)(2,1)} %refs_1_.1), channel_id=1, source_target_pairs={{0,2},{2,4},{4,6},{6,8},{8,10},{10,12},{12,14},{14,0},{1,15},{3,1}... | collective-permute-start | bytes 1572872 | tf_op jit(solution)/shard_map/ppermute | solution.py:28
  4.7 1.9 %collective-permute-start.2 = (bf16[2,256,512]{2,1,0:T(8,128)(2,1)}, bf16[2,256,512]{2,1,0:T(8,128)(2,1)S(1)}, u32[]{:S(2)}, u32[]{:S(2)}) collective-permute-start(bf16[2,256,512]{2,1,0:T(8,128)(2,1)} %refs_1_.1), channel_id=1, source_target_pairs={{1,2},{3,4},{5,6},{7,8},{9,10},{11,12},{13,14},{15,0},{0,15},{2,1}... | collective-permute-start | bytes 1572872 | tf_op jit(solution)/shard_map/ppermute | solution.py:28
  6.6 0.8 copy.8
  7.4 0.7 fusion.2.slot_ref
  8.1 0.1 fusion
  8.2 1.6 %copy-done = bf16[256,4096]{1,0:T(8,128)(2,1)S(1)} copy-done((bf16[256,4096]{1,0:T(8,128)(2,1)S(1)}, bf16[256,4096]{1,0:T(8,128)(2,1)}, u32[]{:S(2)}) %copy-start) | copy-done | bytes 2097176
  9.8 1.6 %copy-done.1 = bf16[256,4096]{1,0:T(8,128)(2,1)S(1)} copy-done((bf16[256,4096]{1,0:T(8,128)(2,1)S(1)}, bf16[256,4096]{1,0:T(8,128)(2,1)}, u32[]{:S(2)}) %copy-start.1) | copy-done | bytes 2097176
  11.4 3.0 %screened.1.refs_0_ = bf16[2,512,4096]{2,1,0:T(8,128)(2,1)S(1)} custom-call(s32[16]{0:T(128)S(1)} %fusion.2.slot_ref, s32[4,32]{1,0:T(4,128)S(1)} %convert_element_type.15.mask_ref, bf16[256,4096]{1,0:T(8,128)(2,1)S(1)} %copy-done, bf16[256,4096]{1,0:T(8,128)(2,1)S(1)} %copy-done.1), custom_call_target="tpu_custom_call" | custom-call | bytes 4194304 | tf_op jit(solution)/shard_map/screened/pallas_call | solution.py:92
  14.4 0.8 collective-permute-done.refs_2_
  15.2 5.5 %collective-permute-start.1 = (bf16[2,256,512]{2,1,0:T(8,128)(2,1)S(1)}, bf16[2,256,512]{2,1,0:T(8,128)(2,1)S(1)}, u32[]{:S(2)}, u32[]{:S(2)}) collective-permute-start(bf16[2,256,512]{2,1,0:T(8,128)(2,1)S(1)} %collective-permute-done.refs_2_), channel_id=1, source_target_pairs={{0,2},{2,4},{4,6},{6,8},{8,10},{10,12},{12,14},{14,0},{1,15},{3,1}... | collective-permute-start | bytes 1572872 | tf_op jit(solution)/shard_map/ppermute | solution.py:28
  20.7 2.1 %collective-permute-start.6 = (bf16[2,256,512]{2,1,0:T(8,128)(2,1)S(1)}, bf16[2,256,512]{2,1,0:T(8,128)(2,1)S(1)}, u32[]{:S(2)}, u32[]{:S(2)}) collective-permute-start(bf16[2,256,512]{2,1,0:T(8,128)(2,1)S(1)} %collective-permute-done.2.refs_3_), channel_id=1, source_target_pairs={{0,2},{2,4},{4,6},{6,8},{8,10},{10,12},{12,14},{14,0},{1,15},{3,1}... | collective-permute-start | bytes 1572872 | tf_op jit(solution)/shard_map/ppermute | solution.py:28
  22.8 1.9 %collective-permute-start.4 = (bf16[2,256,512]{2,1,0:T(8,128)(2,1)S(1)}, bf16[2,256,512]{2,1,0:T(8,128)(2,1)S(1)}, u32[]{:S(2)}, u32[]{:S(2)}) collective-permute-start(bf16[2,256,512]{2,1,0:T(8,128)(2,1)S(1)} %collective-permute-done.refs_2_), channel_id=1, source_target_pairs={{0,1},{1,0},{2,3},{3,2},{4,5},{5,4},{6,7},{7,6},{8,9},{9,8},{10,11... | collective-permute-start | bytes 1572872 | tf_op jit(solution)/shard_map/ppermute | solution.py:21
  24.7 2.4 %collective-permute-start.5 = (bf16[2,256,512]{2,1,0:T(8,128)(2,1)S(1)}, bf16[2,256,512]{2,1,0:T(8,128)(2,1)S(1)}, u32[]{:S(2)}, u32[]{:S(2)}) collective-permute-start(bf16[2,256,512]{2,1,0:T(8,128)(2,1)S(1)} %collective-permute-done.2.refs_3_), channel_id=1, source_target_pairs={{0,1},{1,0},{2,3},{3,2},{4,5},{5,4},{6,7},{7,6},{8,9},{9,8},{10,11... | collective-permute-start | bytes 1572872 | tf_op jit(solution)/shard_map/ppermute | solution.py:21
  27.1 1.0 sum_1.1.refs_5_
  28.1 4.8 %collective-permute-start.3 = (bf16[2,256,512]{2,1,0:T(8,128)(2,1)S(1)}, bf16[2,256,512]{2,1,0:T(8,128)(2,1)S(1)}, u32[]{:S(2)}, u32[]{:S(2)}) collective-permute-start(bf16[2,256,512]{2,1,0:T(8,128)(2,1)S(1)} %collective-permute-done.1.refs_3_), channel_id=1, source_target_pairs={{0,2},{2,4},{4,6},{6,8},{8,10},{10,12},{12,14},{14,0},{1,15},{3,1}... | collective-permute-start | bytes 1572872 | tf_op jit(solution)/shard_map/ppermute | solution.py:28
  33.0 1.9 %collective-permute-start.14 = (bf16[2,256,512]{2,1,0:T(8,128)(2,1)S(1)}, bf16[2,256,512]{2,1,0:T(8,128)(2,1)S(1)}, u32[]{:S(2)}, u32[]{:S(2)}) collective-permute-start(bf16[2,256,512]{2,1,0:T(8,128)(2,1)S(1)} %copy-done.2), channel_id=1, source_target_pairs={{0,1},{1,0},{2,3},{3,2},{4,5},{5,4},{6,7},{7,6},{8,9},{9,8},{10,11... | collective-permute-start | bytes 1572872 | tf_op jit(solution)/shard_map/ppermute | solution.py:21
  34.9 3.7 %collective-permute-start.10 = (bf16[2,256,512]{2,1,0:T(8,128)(2,1)S(1)}, bf16[2,256,512]{2,1,0:T(8,128)(2,1)S(1)}, u32[]{:S(2)}, u32[]{:S(2)}) collective-permute-start(bf16[2,256,512]{2,1,0:T(8,128)(2,1)S(1)} %collective-permute-done.6.refs_4_), channel_id=1, source_target_pairs={{0,2},{2,4},{4,6},{6,8},{8,10},{10,12},{12,14},{14,0},{1,15},{3,1}... | collective-permute-start | bytes 1572872 | tf_op jit(solution)/shard_map/ppermute | solution.py:28
  38.6 1.3 %sum_2.1.refs_5_ = f32[2,512,512]{2,1,0:T(8,128)S(1)} custom-call(bf16[2,512,4096]{2,1,0:T(8,128)(2,1)S(1)} %screened.1.refs_0_, bf16[2,256,512]{2,1,0:T(8,128)(2,1)S(1)} %collective-permute-done.4.refs_1_, bf16[2,256,512]{2,1,0:T(8,128)(2,1)S(1)} %collective-permute-done.5.refs_2_, bf16[2,256,512]{2,1,0:T(8,128)(2,1)S(1)} %collective-permute-done.1.refs_3_, ...), custom_call_target="tpu_custom_call" | custom-call | flops 1073741824 | bytes 1048576 | tf_op jit(solution)/shard_map/sum_2/pallas_call | solution.py:130
  39.9 5.4 %collective-permute-start.7 = (bf16[2,256,512]{2,1,0:T(8,128)(2,1)S(1)}, bf16[2,256,512]{2,1,0:T(8,128)(2,1)S(1)}, u32[]{:S(2)}, u32[]{:S(2)}) collective-permute-start(bf16[2,256,512]{2,1,0:T(8,128)(2,1)S(1)} %collective-permute-done.3.refs_3_), channel_id=1, source_target_pairs={{0,2},{2,4},{4,6},{6,8},{8,10},{10,12},{12,14},{14,0},{1,15},{3,1}... | collective-permute-start | bytes 1572872 | tf_op jit(solution)/shard_map/ppermute | solution.py:28
  45.3 1.9 %collective-permute-start.12 = (bf16[2,256,512]{2,1,0:T(8,128)(2,1)S(1)}, bf16[2,256,512]{2,1,0:T(8,128)(2,1)S(1)}, u32[]{:S(2)}, u32[]{:S(2)}) collective-permute-start(bf16[2,256,512]{2,1,0:T(8,128)(2,1)S(1)} %collective-permute-done.1.refs_3_), channel_id=1, source_target_pairs={{0,1},{1,0},{2,3},{3,2},{4,5},{5,4},{6,7},{7,6},{8,9},{9,8},{10,11... | collective-permute-start | bytes 1572872 | tf_op jit(solution)/shard_map/ppermute | solution.py:21
  47.2 2.4 %collective-permute-start.13 = (bf16[2,256,512]{2,1,0:T(8,128)(2,1)S(1)}, bf16[2,256,512]{2,1,0:T(8,128)(2,1)S(1)}, u32[]{:S(2)}, u32[]{:S(2)}) collective-permute-start(bf16[2,256,512]{2,1,0:T(8,128)(2,1)S(1)} %collective-permute-done.6.refs_4_), channel_id=1, source_target_pairs={{0,1},{1,0},{2,3},{3,2},{4,5},{5,4},{6,7},{7,6},{8,9},{9,8},{10,11... | collective-permute-start | bytes 1572872 | tf_op jit(solution)/shard_map/ppermute | solution.py:21
  49.6 1.9 %collective-permute-start.9 = (bf16[2,256,512]{2,1,0:T(8,128)(2,1)S(1)}, bf16[2,256,512]{2,1,0:T(8,128)(2,1)S(1)}, u32[]{:S(2)}, u32[]{:S(2)}) collective-permute-start(bf16[2,256,512]{2,1,0:T(8,128)(2,1)S(1)} %collective-permute-done.3.refs_3_), channel_id=1, source_target_pairs={{0,1},{1,0},{2,3},{3,2},{4,5},{5,4},{6,7},{7,6},{8,9},{9,8},{10,11... | collective-permute-start | bytes 1572872 | tf_op jit(solution)/shard_map/ppermute | solution.py:21
  51.5 2.4 %collective-permute-start.11 = (bf16[2,256,512]{2,1,0:T(8,128)(2,1)S(1)}, bf16[2,256,512]{2,1,0:T(8,128)(2,1)S(1)}, u32[]{:S(2)}, u32[]{:S(2)}) collective-permute-start(bf16[2,256,512]{2,1,0:T(8,128)(2,1)S(1)} %collective-permute-done.10.refs_3_), channel_id=1, source_target_pairs={{0,1},{1,0},{2,3},{3,2},{4,5},{5,4},{6,7},{7,6},{8,9},{9,8},{10,11... | collective-permute-start | bytes 1572872 | tf_op jit(solution)/shard_map/ppermute | solution.py:21
  54.0 1.9 %collective-permute-start.8 = (bf16[2,256,512]{2,1,0:T(8,128)(2,1)S(1)}, bf16[2,256,512]{2,1,0:T(8,128)(2,1)S(1)}, u32[]{:S(2)}, u32[]{:S(2)}) collective-permute-start(bf16[2,256,512]{2,1,0:T(8,128)(2,1)S(1)} %collective-permute-done.7.refs_4_), channel_id=1, source_target_pairs={{0,1},{1,0},{2,3},{3,2},{4,5},{5,4},{6,7},{7,6},{8,9},{9,8},{10,11... | collective-permute-start | bytes 1572872 | tf_op jit(solution)/shard_map/ppermute | solution.py:21
  55.9 1.2 %sum_3.1.refs_5_ = f32[2,512,512]{2,1,0:T(8,128)S(1)} custom-call(bf16[2,512,4096]{2,1,0:T(8,128)(2,1)S(1)} %screened.1.refs_0_, bf16[2,256,512]{2,1,0:T(8,128)(2,1)S(1)} %collective-permute-done.12.refs_1_, bf16[2,256,512]{2,1,0:T(8,128)(2,1)S(1)} %collective-permute-done.13.refs_2_, bf16[2,256,512]{2,1,0:T(8,128)(2,1)S(1)} %collective-permute-done.3.refs_3_, ...), custom_call_target="tpu_custom_call" | custom-call | flops 1073741824 | bytes 1048576 | tf_op jit(solution)/shard_map/sum_3/pallas_call | solution.py:130
  57.2 1.2 %sum_4.1.refs_2_ = f32[2,512,512]{2,1,0:T(8,128)S(1)} custom-call(bf16[2,512,4096]{2,1,0:T(8,128)(2,1)S(1)} %screened.1.refs_0_, bf16[2,256,512]{2,1,0:T(8,128)(2,1)S(1)} %collective-permute-done.9.refs_1_, bf16[2,256,512]{2,1,0:T(8,128)(2,1)S(1)} %collective-permute-done.11.refs_2_, bf16[2,256,512]{2,1,0:T(8,128)(2,1)S(1)} %collective-permute-done.10.refs_3_, ...), custom_call_target="tpu_custom_call" | custom-call | flops 1073741824 | bytes 1048576 | tf_op jit(solution)/shard_map/sum_4/pallas_call | solution.py:130
  58.5 0.9 sum_5.1
  59.4 0.7 collective-permute-start.16
  60.1 18.8 %collective-permute-start.15 = (bf16[2,256,512]{2,1,0:T(8,128)(2,1)S(1)}, bf16[2,256,512]{2,1,0:T(8,128)(2,1)S(1)}, u32[]{:S(2)}, u32[]{:S(2)}) collective-permute-start(bf16[2,256,512]{2,1,0:T(8,128)(2,1)S(1)} %sum_5.1), channel_id=1, source_target_pairs={{0,1008},{1,1009},{2,1010},{3,1011},{4,1012},{5,1013},{6,1014},{7,... | collective-permute-start | bytes 1572872 | tf_op jit(solution)/shard_map/ppermute | solution.py:63
  78.9 0.7 collective-permute-start.17
  79.6 40.9 %collective-permute-done.15 = bf16[2,256,512]{2,1,0:T(8,128)(2,1)S(1)} collective-permute-done((bf16[2,256,512]{2,1,0:T(8,128)(2,1)S(1)}, bf16[2,256,512]{2,1,0:T(8,128)(2,1)S(1)}, u32[]{:S(2)}, u32[]{:S(2)}) %collective-permute-start.15) | collective-permute-done | bytes 524320 | tf_op jit(solution)/shard_map/ppermute | solution.py:63
  120.5 1.0 add_convert_fusion
  (23 shorter events, 0.1 us)
Async XLA Ops:
  0.0 15.2 %collective-permute-start = (bf16[2,256,512]{2,1,0:T(8,128)(2,1)}, bf16[2,256,512]{2,1,0:T(8,128)(2,1)S(1)}, u32[]{:S(2)}, u32[]{:S(2)}) collective-permute-start(bf16[2,256,512]{2,1,0:T(8,128)(2,1)} %refs_1_.1), channel_id=1, source_target_pairs={{0,2},{2,4},{4,6},{6,8},{8,10},{10,12},{12,14},{14,0},{1,15},{3,1}... | collective-permute-start | bytes 1572872 | tf_op jit(solution)/shard_map/ppermute | solution.py:28
  4.7 16.0 %collective-permute-start.2 = (bf16[2,256,512]{2,1,0:T(8,128)(2,1)}, bf16[2,256,512]{2,1,0:T(8,128)(2,1)S(1)}, u32[]{:S(2)}, u32[]{:S(2)}) collective-permute-start(bf16[2,256,512]{2,1,0:T(8,128)(2,1)} %refs_1_.1), channel_id=1, source_target_pairs={{1,2},{3,4},{5,6},{7,8},{9,10},{11,12},{13,14},{15,0},{0,15},{2,1}... | collective-permute-start | bytes 1572872 | tf_op jit(solution)/shard_map/ppermute | solution.py:28
  8.2 1.6 %copy-start = (bf16[256,4096]{1,0:T(8,128)(2,1)S(1)}, bf16[256,4096]{1,0:T(8,128)(2,1)}, u32[]{:S(2)}) copy-start(bf16[256,4096]{1,0:T(8,128)(2,1)} %fock.1) | copy-start | bytes 6291460
  9.8 1.6 %copy-start.1 = (bf16[256,4096]{1,0:T(8,128)(2,1)S(1)}, bf16[256,4096]{1,0:T(8,128)(2,1)}, u32[]{:S(2)}) copy-start(bf16[256,4096]{1,0:T(8,128)(2,1)} %ladder.1) | copy-start | bytes 6291460
  11.4 15.7 %copy-start.2 = (bf16[2,256,512]{2,1,0:T(8,128)(2,1)S(1)}, bf16[2,256,512]{2,1,0:T(8,128)(2,1)}, u32[]{:S(2)}) copy-start(bf16[2,256,512]{2,1,0:T(8,128)(2,1)} %refs_1_.1) | copy-start | bytes 1572868
  15.2 12.9 %collective-permute-start.1 = (bf16[2,256,512]{2,1,0:T(8,128)(2,1)S(1)}, bf16[2,256,512]{2,1,0:T(8,128)(2,1)S(1)}, u32[]{:S(2)}, u32[]{:S(2)}) collective-permute-start(bf16[2,256,512]{2,1,0:T(8,128)(2,1)S(1)} %collective-permute-done.refs_2_), channel_id=1, source_target_pairs={{0,2},{2,4},{4,6},{6,8},{8,10},{10,12},{12,14},{14,0},{1,15},{3,1}... | collective-permute-start | bytes 1572872 | tf_op jit(solution)/shard_map/ppermute | solution.py:28
  20.7 14.2 %collective-permute-start.6 = (bf16[2,256,512]{2,1,0:T(8,128)(2,1)S(1)}, bf16[2,256,512]{2,1,0:T(8,128)(2,1)S(1)}, u32[]{:S(2)}, u32[]{:S(2)}) collective-permute-start(bf16[2,256,512]{2,1,0:T(8,128)(2,1)S(1)} %collective-permute-done.2.refs_3_), channel_id=1, source_target_pairs={{0,2},{2,4},{4,6},{6,8},{8,10},{10,12},{12,14},{14,0},{1,15},{3,1}... | collective-permute-start | bytes 1572872 | tf_op jit(solution)/shard_map/ppermute | solution.py:28
  22.8 15.8 %collective-permute-start.4 = (bf16[2,256,512]{2,1,0:T(8,128)(2,1)S(1)}, bf16[2,256,512]{2,1,0:T(8,128)(2,1)S(1)}, u32[]{:S(2)}, u32[]{:S(2)}) collective-permute-start(bf16[2,256,512]{2,1,0:T(8,128)(2,1)S(1)} %collective-permute-done.refs_2_), channel_id=1, source_target_pairs={{0,1},{1,0},{2,3},{3,2},{4,5},{5,4},{6,7},{7,6},{8,9},{9,8},{10,11... | collective-permute-start | bytes 1572872 | tf_op jit(solution)/shard_map/ppermute | solution.py:21
  24.7 13.9 %collective-permute-start.5 = (bf16[2,256,512]{2,1,0:T(8,128)(2,1)S(1)}, bf16[2,256,512]{2,1,0:T(8,128)(2,1)S(1)}, u32[]{:S(2)}, u32[]{:S(2)}) collective-permute-start(bf16[2,256,512]{2,1,0:T(8,128)(2,1)S(1)} %collective-permute-done.2.refs_3_), channel_id=1, source_target_pairs={{0,1},{1,0},{2,3},{3,2},{4,5},{5,4},{6,7},{7,6},{8,9},{9,8},{10,11... | collective-permute-start | bytes 1572872 | tf_op jit(solution)/shard_map/ppermute | solution.py:21
  28.1 11.7 %collective-permute-start.3 = (bf16[2,256,512]{2,1,0:T(8,128)(2,1)S(1)}, bf16[2,256,512]{2,1,0:T(8,128)(2,1)S(1)}, u32[]{:S(2)}, u32[]{:S(2)}) collective-permute-start(bf16[2,256,512]{2,1,0:T(8,128)(2,1)S(1)} %collective-permute-done.1.refs_3_), channel_id=1, source_target_pairs={{0,2},{2,4},{4,6},{6,8},{8,10},{10,12},{12,14},{14,0},{1,15},{3,1}... | collective-permute-start | bytes 1572872 | tf_op jit(solution)/shard_map/ppermute | solution.py:28
  33.0 16.6 %collective-permute-start.14 = (bf16[2,256,512]{2,1,0:T(8,128)(2,1)S(1)}, bf16[2,256,512]{2,1,0:T(8,128)(2,1)S(1)}, u32[]{:S(2)}, u32[]{:S(2)}) collective-permute-start(bf16[2,256,512]{2,1,0:T(8,128)(2,1)S(1)} %copy-done.2), channel_id=1, source_target_pairs={{0,1},{1,0},{2,3},{3,2},{4,5},{5,4},{6,7},{7,6},{8,9},{9,8},{10,11... | collective-permute-start | bytes 1572872 | tf_op jit(solution)/shard_map/ppermute | solution.py:21
  34.9 16.6 %collective-permute-start.10 = (bf16[2,256,512]{2,1,0:T(8,128)(2,1)S(1)}, bf16[2,256,512]{2,1,0:T(8,128)(2,1)S(1)}, u32[]{:S(2)}, u32[]{:S(2)}) collective-permute-start(bf16[2,256,512]{2,1,0:T(8,128)(2,1)S(1)} %collective-permute-done.6.refs_4_), channel_id=1, source_target_pairs={{0,2},{2,4},{4,6},{6,8},{8,10},{10,12},{12,14},{14,0},{1,15},{3,1}... | collective-permute-start | bytes 1572872 | tf_op jit(solution)/shard_map/ppermute | solution.py:28
  39.9 14.1 %collective-permute-start.7 = (bf16[2,256,512]{2,1,0:T(8,128)(2,1)S(1)}, bf16[2,256,512]{2,1,0:T(8,128)(2,1)S(1)}, u32[]{:S(2)}, u32[]{:S(2)}) collective-permute-start(bf16[2,256,512]{2,1,0:T(8,128)(2,1)S(1)} %collective-permute-done.3.refs_3_), channel_id=1, source_target_pairs={{0,2},{2,4},{4,6},{6,8},{8,10},{10,12},{12,14},{14,0},{1,15},{3,1}... | collective-permute-start | bytes 1572872 | tf_op jit(solution)/shard_map/ppermute | solution.py:28
  45.3 10.6 %collective-permute-start.12 = (bf16[2,256,512]{2,1,0:T(8,128)(2,1)S(1)}, bf16[2,256,512]{2,1,0:T(8,128)(2,1)S(1)}, u32[]{:S(2)}, u32[]{:S(2)}) collective-permute-start(bf16[2,256,512]{2,1,0:T(8,128)(2,1)S(1)} %collective-permute-done.1.refs_3_), channel_id=1, source_target_pairs={{0,1},{1,0},{2,3},{3,2},{4,5},{5,4},{6,7},{7,6},{8,9},{9,8},{10,11... | collective-permute-start | bytes 1572872 | tf_op jit(solution)/shard_map/ppermute | solution.py:21
  47.2 8.7 %collective-permute-start.13 = (bf16[2,256,512]{2,1,0:T(8,128)(2,1)S(1)}, bf16[2,256,512]{2,1,0:T(8,128)(2,1)S(1)}, u32[]{:S(2)}, u32[]{:S(2)}) collective-permute-start(bf16[2,256,512]{2,1,0:T(8,128)(2,1)S(1)} %collective-permute-done.6.refs_4_), channel_id=1, source_target_pairs={{0,1},{1,0},{2,3},{3,2},{4,5},{5,4},{6,7},{7,6},{8,9},{9,8},{10,11... | collective-permute-start | bytes 1572872 | tf_op jit(solution)/shard_map/ppermute | solution.py:21
  49.6 7.6 %collective-permute-start.9 = (bf16[2,256,512]{2,1,0:T(8,128)(2,1)S(1)}, bf16[2,256,512]{2,1,0:T(8,128)(2,1)S(1)}, u32[]{:S(2)}, u32[]{:S(2)}) collective-permute-start(bf16[2,256,512]{2,1,0:T(8,128)(2,1)S(1)} %collective-permute-done.3.refs_3_), channel_id=1, source_target_pairs={{0,1},{1,0},{2,3},{3,2},{4,5},{5,4},{6,7},{7,6},{8,9},{9,8},{10,11... | collective-permute-start | bytes 1572872 | tf_op jit(solution)/shard_map/ppermute | solution.py:21
  51.5 5.7 %collective-permute-start.11 = (bf16[2,256,512]{2,1,0:T(8,128)(2,1)S(1)}, bf16[2,256,512]{2,1,0:T(8,128)(2,1)S(1)}, u32[]{:S(2)}, u32[]{:S(2)}) collective-permute-start(bf16[2,256,512]{2,1,0:T(8,128)(2,1)S(1)} %collective-permute-done.10.refs_3_), channel_id=1, source_target_pairs={{0,1},{1,0},{2,3},{3,2},{4,5},{5,4},{6,7},{7,6},{8,9},{9,8},{10,11... | collective-permute-start | bytes 1572872 | tf_op jit(solution)/shard_map/ppermute | solution.py:21
  54.0 4.5 %collective-permute-start.8 = (bf16[2,256,512]{2,1,0:T(8,128)(2,1)S(1)}, bf16[2,256,512]{2,1,0:T(8,128)(2,1)S(1)}, u32[]{:S(2)}, u32[]{:S(2)}) collective-permute-start(bf16[2,256,512]{2,1,0:T(8,128)(2,1)S(1)} %collective-permute-done.7.refs_4_), channel_id=1, source_target_pairs={{0,1},{1,0},{2,3},{3,2},{4,5},{5,4},{6,7},{7,6},{8,9},{9,8},{10,11... | collective-permute-start | bytes 1572872 | tf_op jit(solution)/shard_map/ppermute | solution.py:21
  57.2 1.3 %copy-start.3 = (bf16[512,512]{1,0:T(8,128)(2,1)S(1)}, bf16[512,512]{1,0:T(8,128)(2,1)}, u32[]{:S(2)}) copy-start(bf16[512,512]{1,0:T(8,128)(2,1)} %refs_3_.1) | copy-start | bytes 1572868
  59.4 19.6 %collective-permute-start.16 = (bf16[2,256,512]{2,1,0:T(8,128)(2,1)S(1)}, bf16[2,256,512]{2,1,0:T(8,128)(2,1)S(1)}, u32[]{:S(2)}, u32[]{:S(2)}) collective-permute-start(bf16[2,256,512]{2,1,0:T(8,128)(2,1)S(1)} %sum_5.1), channel_id=1, source_target_pairs={{48,128},{49,129},{50,130},{51,131},{52,132},{53,133},{54,134},{55... | collective-permute-start | bytes 1572872 | tf_op jit(solution)/shard_map/ppermute | solution.py:62
  60.1 60.4 %collective-permute-start.15 = (bf16[2,256,512]{2,1,0:T(8,128)(2,1)S(1)}, bf16[2,256,512]{2,1,0:T(8,128)(2,1)S(1)}, u32[]{:S(2)}, u32[]{:S(2)}) collective-permute-start(bf16[2,256,512]{2,1,0:T(8,128)(2,1)S(1)} %sum_5.1), channel_id=1, source_target_pairs={{0,1008},{1,1009},{2,1010},{3,1011},{4,1012},{5,1013},{6,1014},{7,... | collective-permute-start | bytes 1572872 | tf_op jit(solution)/shard_map/ppermute | solution.py:63
  78.9 41.6 %collective-permute-start.17 = (bf16[2,256,512]{2,1,0:T(8,128)(2,1)S(1)}, bf16[2,256,512]{2,1,0:T(8,128)(2,1)S(1)}, u32[]{:S(2)}, u32[]{:S(2)}) collective-permute-start(bf16[2,256,512]{2,1,0:T(8,128)(2,1)S(1)} %collective-permute-done.16), channel_id=1, source_target_pairs={{128,240},{129,241},{130,242},{131,243},{132,244},{133,245},{134,2... | collective-permute-start | bytes 1572872 | tf_op jit(solution)/shard_map/ppermute | solution.py:64

commit v7 on v6

--- a/solution.py
+++ b/solution.py
@@ -12,6 +12,7 @@
 SPLIT = HALF // TILE
 VMEM_LIMIT = 24 * 1024 * 1024
 RING = 16
+MARK_FLOPS = 1 << 33
 HOPS = (None, (0, 0), (1, 0), (1, 1), (2, 0), (2, 1), (3, 0), (3, 1), (4, 0))
 ORDER = (1, 2, 3, -2, -3, 4, 5, -4, -5, 6, -1, -6, -7, 7, 8, -8)
 
@@ -66,6 +67,27 @@
 
 def after(block, *earlier):
     return lax.optimization_barrier((block, *earlier))[0]
+
+
+def mark_kernel(list_ref, out_ref):
+    listed = list_ref[...]
+    columns = lax.broadcasted_iota(jnp.int32, out_ref.shape, 1)
+    hit = columns == listed[:, 0:1]
+    for n in range(1, listed.shape[1]):
+        hit = hit | (columns == listed[:, n : n + 1])
+    out_ref[...] = hit.astype(jnp.int32)
+
+
+def marks(listed, total_tiles):
+    vmem = pl.BlockSpec(memory_space=pltpu.VMEM)
+    return pl.pallas_call(
+        mark_kernel,
+        out_shape=jax.ShapeDtypeStruct((listed.shape[0], total_tiles), jnp.int32),
+        in_specs=[vmem],
+        out_specs=vmem,
+        cost_estimate=pl.CostEstimate(flops=MARK_FLOPS, bytes_accessed=1 << 12, transcendentals=0),
+        name="marks",
+    )(listed)
 
 
 def screen_kernel(pairs, slot_ref, mask_ref, fock, ladder, out_ref):
@@ -151,8 +173,7 @@
     way = jnp.where(core == 0, -1, 1)
     half_of = jnp.where(other == 1, 1 - core, core)
     slot_tiles = ((chip + way * hops + chips) % chips * 2 * SPLIT + half_of * SPLIT).astype(jnp.int32)
-    columns = jnp.arange(total_tiles, dtype=jnp.int32)
-    masks = jnp.any(tile_list.reshape(pairs * SPLIT, nnz)[:, :, None] == columns, axis=1).astype(jnp.int32)
+    masks = marks(tile_list.reshape(pairs * SPLIT, nnz), total_tiles)
 
     x0 = amps
     x1, s1 = ring_step(x0), ring_step(x0, cross=1)

time: 122 us -> 122 us (level)
  local copies, waits for them, and re-layouts: 3.96 us -> 2.39 us
  Pallas kernels: 8.58 us -> 10.1 us
    pallas_call x0 -> x1, Pallas kernels: none -> 1.5 us  [marks(): pl.pallas_call(mark_kernel, out_shape=jax.ShapeDtypeStruct((listed.shape[...]
    unnamed x8 -> x14, local copies, waits for them, and re-layouts: 3.19 us -> 2.39 us
  transfers between devices with their start and end apart: 18 -> 18, of which waited for: 2 -> 2; matrix products, arithmetic and copies ran while one was open for 1% -> 0% of each run, Pallas kernels for 6% -> 8%
where the time goes in v7:
time: 122 us; the launch traced here: 121 us
  starting transfers between devices  65.1 us (53%)
  waiting for transfers between devices  42.6 us (35%)
  Pallas kernels  10.1 us (8%)
  local copies, waits for them, and re-layouts  2.39 us (2%)
    ppermute x1, waiting for transfers between devices, mirror_swap(): straight = lax.ppermute(block, axes, direct)  40.9 us
    ppermute x7, starting transfers between devices, ring_step(): return lax.ppermute(block, 'virt', route)  28 us
    ppermute x1, starting transfers between devices, mirror_swap(): straight = lax.ppermute(block, axes, direct)  18.8 us
    ppermute x8, starting transfers between devices, core_swap(): return lax.ppermute(block, 'virt', [(v, v ^ 1) for v in range(count)])  16.8 us
    pallas_call x5, Pallas kernels, sum_slots(): pl.pallas_call(functools.partial(sum_kernel, pairs, slots, acc is not Non...  5.59 us
    pallas_call x1, Pallas kernels, screened(): pl.pallas_call(functools.partial(screen_kernel, pairs), out_shape=jax.Sha...  3.01 us
  transfers between devices with their start and end apart: 18, of which 2 were waited for; matrix products, arithmetic and copies ran while one was open for 0% of the time, Pallas kernels for 8%

profile of v7, /device:TPU:28, one launch (start us, length us, event | category | flops | bytes accessed | tf_op | source)
XLA Modules:
  0.0 121.5 jit_solution(5432058968174521403)
XLA Ops:
  0.0 4.7 %collective-permute-start = (bf16[2,256,512]{2,1,0:T(8,128)(2,1)}, bf16[2,256,512]{2,1,0:T(8,128)(2,1)S(1)}, u32[]{:S(2)}, u32[]{:S(2)}) collective-permute-start(bf16[2,256,512]{2,1,0:T(8,128)(2,1)} %refs_1_.1), channel_id=1, source_target_pairs={{0,2},{2,4},{4,6},{6,8},{8,10},{10,12},{12,14},{14,0},{1,15},{3,1}... | collective-permute-start | bytes 1572872 | tf_op jit(solution)/shard_map/ppermute | solution.py:29
  4.7 1.9 %collective-permute-start.2 = (bf16[2,256,512]{2,1,0:T(8,128)(2,1)}, bf16[2,256,512]{2,1,0:T(8,128)(2,1)S(1)}, u32[]{:S(2)}, u32[]{:S(2)}) collective-permute-start(bf16[2,256,512]{2,1,0:T(8,128)(2,1)} %refs_1_.1), channel_id=1, source_target_pairs={{1,2},{3,4},{5,6},{7,8},{9,10},{11,12},{13,14},{15,0},{0,15},{2,1}... | collective-permute-start | bytes 1572872 | tf_op jit(solution)/shard_map/ppermute | solution.py:29
  6.6 0.0 copy-start.6
  6.7 1.5 %marks.1.mask_ref = s32[4,32]{1,0:T(4,128)} custom-call(s32[4,12]{1,0:T(4,128)} %bitcast.1), custom_call_target="tpu_custom_call" | custom-call | flops 8589934592 | bytes 4096 | tf_op jit(solution)/shard_map/marks/pallas_call | solution.py:83
  8.2 0.1 copy-done
  8.3 1.6 %copy-done.1 = bf16[256,4096]{1,0:T(8,128)(2,1)S(1)} copy-done((bf16[256,4096]{1,0:T(8,128)(2,1)S(1)}, bf16[256,4096]{1,0:T(8,128)(2,1)}, u32[]{:S(2)}) %copy-start.1) | copy-done | bytes 2097176
  9.9 0.7 copy-done.4
  10.5 3.0 %screened.1.refs_0_ = bf16[2,512,4096]{2,1,0:T(8,128)(2,1)S(1)} custom-call(s32[16]{0:T(128)S(1)} %fusion.1.slot_ref, s32[4,32]{1,0:T(4,128)S(1)} %copy-done.4, bf16[256,4096]{1,0:T(8,128)(2,1)S(1)} %copy-done, bf16[256,4096]{1,0:T(8,128)(2,1)S(1)} %copy-done.1), custom_call_target="tpu_custom_call" | custom-call | bytes 4194304 | tf_op jit(solution)/shard_map/screened/pallas_call | solution.py:114
  13.6 1.7 %collective-permute-done.refs_2_ = bf16[2,256,512]{2,1,0:T(8,128)(2,1)S(1)} collective-permute-done((bf16[2,256,512]{2,1,0:T(8,128)(2,1)}, bf16[2,256,512]{2,1,0:T(8,128)(2,1)S(1)}, u32[]{:S(2)}, u32[]{:S(2)}) %collective-permute-start) | collective-permute-done | bytes 524320 | tf_op jit(solution)/shard_map/ppermute | solution.py:29
  15.2 5.5 %collective-permute-start.1 = (bf16[2,256,512]{2,1,0:T(8,128)(2,1)S(1)}, bf16[2,256,512]{2,1,0:T(8,128)(2,1)S(1)}, u32[]{:S(2)}, u32[]{:S(2)}) collective-permute-start(bf16[2,256,512]{2,1,0:T(8,128)(2,1)S(1)} %collective-permute-done.refs_2_), channel_id=1, source_target_pairs={{0,2},{2,4},{4,6},{6,8},{8,10},{10,12},{12,14},{14,0},{1,15},{3,1}... | collective-permute-start | bytes 1572872 | tf_op jit(solution)/shard_map/ppermute | solution.py:29
  20.7 2.1 %collective-permute-start.6 = (bf16[2,256,512]{2,1,0:T(8,128)(2,1)S(1)}, bf16[2,256,512]{2,1,0:T(8,128)(2,1)S(1)}, u32[]{:S(2)}, u32[]{:S(2)}) collective-permute-start(bf16[2,256,512]{2,1,0:T(8,128)(2,1)S(1)} %collective-permute-done.2.refs_3_), channel_id=1, source_target_pairs={{0,2},{2,4},{4,6},{6,8},{8,10},{10,12},{12,14},{14,0},{1,15},{3,1}... | collective-permute-start | bytes 1572872 | tf_op jit(solution)/shard_map/ppermute | solution.py:29
  22.8 1.9 %collective-permute-start.4 = (bf16[2,256,512]{2,1,0:T(8,128)(2,1)S(1)}, bf16[2,256,512]{2,1,0:T(8,128)(2,1)S(1)}, u32[]{:S(2)}, u32[]{:S(2)}) collective-permute-start(bf16[2,256,512]{2,1,0:T(8,128)(2,1)S(1)} %collective-permute-done.refs_2_), channel_id=1, source_target_pairs={{0,1},{1,0},{2,3},{3,2},{4,5},{5,4},{6,7},{7,6},{8,9},{9,8},{10,11... | collective-permute-start | bytes 1572872 | tf_op jit(solution)/shard_map/ppermute | solution.py:22
  24.7 2.4 %collective-permute-start.5 = (bf16[2,256,512]{2,1,0:T(8,128)(2,1)S(1)}, bf16[2,256,512]{2,1,0:T(8,128)(2,1)S(1)}, u32[]{:S(2)}, u32[]{:S(2)}) collective-permute-start(bf16[2,256,512]{2,1,0:T(8,128)(2,1)S(1)} %collective-permute-done.2.refs_3_), channel_id=1, source_target_pairs={{0,1},{1,0},{2,3},{3,2},{4,5},{5,4},{6,7},{7,6},{8,9},{9,8},{10,11... | collective-permute-start | bytes 1572872 | tf_op jit(solution)/shard_map/ppermute | solution.py:22
  27.1 1.0 sum_1.1.refs_5_
  28.1 4.8 %collective-permute-start.3 = (bf16[2,256,512]{2,1,0:T(8,128)(2,1)S(1)}, bf16[2,256,512]{2,1,0:T(8,128)(2,1)S(1)}, u32[]{:S(2)}, u32[]{:S(2)}) collective-permute-start(bf16[2,256,512]{2,1,0:T(8,128)(2,1)S(1)} %collective-permute-done.1.refs_3_), channel_id=1, source_target_pairs={{0,2},{2,4},{4,6},{6,8},{8,10},{10,12},{12,14},{14,0},{1,15},{3,1}... | collective-permute-start | bytes 1572872 | tf_op jit(solution)/shard_map/ppermute | solution.py:29
  33.0 1.9 %collective-permute-start.14 = (bf16[2,256,512]{2,1,0:T(8,128)(2,1)S(1)}, bf16[2,256,512]{2,1,0:T(8,128)(2,1)S(1)}, u32[]{:S(2)}, u32[]{:S(2)}) collective-permute-start(bf16[2,256,512]{2,1,0:T(8,128)(2,1)S(1)} %copy-done.2), channel_id=1, source_target_pairs={{0,1},{1,0},{2,3},{3,2},{4,5},{5,4},{6,7},{7,6},{8,9},{9,8},{10,11... | collective-permute-start | bytes 1572872 | tf_op jit(solution)/shard_map/ppermute | solution.py:22
  34.9 3.7 %collective-permute-start.10 = (bf16[2,256,512]{2,1,0:T(8,128)(2,1)S(1)}, bf16[2,256,512]{2,1,0:T(8,128)(2,1)S(1)}, u32[]{:S(2)}, u32[]{:S(2)}) collective-permute-start(bf16[2,256,512]{2,1,0:T(8,128)(2,1)S(1)} %collective-permute-done.6.refs_4_), channel_id=1, source_target_pairs={{0,2},{2,4},{4,6},{6,8},{8,10},{10,12},{12,14},{14,0},{1,15},{3,1}... | collective-permute-start | bytes 1572872 | tf_op jit(solution)/shard_map/ppermute | solution.py:29
  38.6 1.3 %sum_2.1.refs_5_ = f32[2,512,512]{2,1,0:T(8,128)S(1)} custom-call(bf16[2,512,4096]{2,1,0:T(8,128)(2,1)S(1)} %screened.1.refs_0_, bf16[2,256,512]{2,1,0:T(8,128)(2,1)S(1)} %collective-permute-done.4.refs_1_, bf16[2,256,512]{2,1,0:T(8,128)(2,1)S(1)} %collective-permute-done.5.refs_2_, bf16[2,256,512]{2,1,0:T(8,128)(2,1)S(1)} %collective-permute-done.1.refs_3_, ...), custom_call_target="tpu_custom_call" | custom-call | flops 1073741824 | bytes 1048576 | tf_op jit(solution)/shard_map/sum_2/pallas_call | solution.py:152
  39.9 5.4 %collective-permute-start.7 = (bf16[2,256,512]{2,1,0:T(8,128)(2,1)S(1)}, bf16[2,256,512]{2,1,0:T(8,128)(2,1)S(1)}, u32[]{:S(2)}, u32[]{:S(2)}) collective-permute-start(bf16[2,256,512]{2,1,0:T(8,128)(2,1)S(1)} %collective-permute-done.3.refs_3_), channel_id=1, source_target_pairs={{0,2},{2,4},{4,6},{6,8},{8,10},{10,12},{12,14},{14,0},{1,15},{3,1}... | collective-permute-start | bytes 1572872 | tf_op jit(solution)/shard_map/ppermute | solution.py:29
  45.3 1.9 %collective-permute-start.12 = (bf16[2,256,512]{2,1,0:T(8,128)(2,1)S(1)}, bf16[2,256,512]{2,1,0:T(8,128)(2,1)S(1)}, u32[]{:S(2)}, u32[]{:S(2)}) collective-permute-start(bf16[2,256,512]{2,1,0:T(8,128)(2,1)S(1)} %collective-permute-done.1.refs_3_), channel_id=1, source_target_pairs={{0,1},{1,0},{2,3},{3,2},{4,5},{5,4},{6,7},{7,6},{8,9},{9,8},{10,11... | collective-permute-start | bytes 1572872 | tf_op jit(solution)/shard_map/ppermute | solution.py:22
  47.2 2.4 %collective-permute-start.13 = (bf16[2,256,512]{2,1,0:T(8,128)(2,1)S(1)}, bf16[2,256,512]{2,1,0:T(8,128)(2,1)S(1)}, u32[]{:S(2)}, u32[]{:S(2)}) collective-permute-start(bf16[2,256,512]{2,1,0:T(8,128)(2,1)S(1)} %collective-permute-done.6.refs_4_), channel_id=1, source_target_pairs={{0,1},{1,0},{2,3},{3,2},{4,5},{5,4},{6,7},{7,6},{8,9},{9,8},{10,11... | collective-permute-start | bytes 1572872 | tf_op jit(solution)/shard_map/ppermute | solution.py:22
  49.6 1.9 %collective-permute-start.9 = (bf16[2,256,512]{2,1,0:T(8,128)(2,1)S(1)}, bf16[2,256,512]{2,1,0:T(8,128)(2,1)S(1)}, u32[]{:S(2)}, u32[]{:S(2)}) collective-permute-start(bf16[2,256,512]{2,1,0:T(8,128)(2,1)S(1)} %collective-permute-done.3.refs_3_), channel_id=1, source_target_pairs={{0,1},{1,0},{2,3},{3,2},{4,5},{5,4},{6,7},{7,6},{8,9},{9,8},{10,11... | collective-permute-start | bytes 1572872 | tf_op jit(solution)/shard_map/ppermute | solution.py:22
  51.5 2.4 %collective-permute-start.11 = (bf16[2,256,512]{2,1,0:T(8,128)(2,1)S(1)}, bf16[2,256,512]{2,1,0:T(8,128)(2,1)S(1)}, u32[]{:S(2)}, u32[]{:S(2)}) collective-permute-start(bf16[2,256,512]{2,1,0:T(8,128)(2,1)S(1)} %collective-permute-done.10.refs_3_), channel_id=1, source_target_pairs={{0,1},{1,0},{2,3},{3,2},{4,5},{5,4},{6,7},{7,6},{8,9},{9,8},{10,11... | collective-permute-start | bytes 1572872 | tf_op jit(solution)/shard_map/ppermute | solution.py:22
  54.0 1.9 %collective-permute-start.8 = (bf16[2,256,512]{2,1,0:T(8,128)(2,1)S(1)}, bf16[2,256,512]{2,1,0:T(8,128)(2,1)S(1)}, u32[]{:S(2)}, u32[]{:S(2)}) collective-permute-start(bf16[2,256,512]{2,1,0:T(8,128)(2,1)S(1)} %collective-permute-done.7.refs_4_), channel_id=1, source_target_pairs={{0,1},{1,0},{2,3},{3,2},{4,5},{5,4},{6,7},{7,6},{8,9},{9,8},{10,11... | collective-permute-start | bytes 1572872 | tf_op jit(solution)/shard_map/ppermute | solution.py:22
  55.9 1.2 %sum_3.1.refs_5_ = f32[2,512,512]{2,1,0:T(8,128)S(1)} custom-call(bf16[2,512,4096]{2,1,0:T(8,128)(2,1)S(1)} %screened.1.refs_0_, bf16[2,256,512]{2,1,0:T(8,128)(2,1)S(1)} %collective-permute-done.12.refs_1_, bf16[2,256,512]{2,1,0:T(8,128)(2,1)S(1)} %collective-permute-done.13.refs_2_, bf16[2,256,512]{2,1,0:T(8,128)(2,1)S(1)} %collective-permute-done.3.refs_3_, ...), custom_call_target="tpu_custom_call" | custom-call | flops 1073741824 | bytes 1048576 | tf_op jit(solution)/shard_map/sum_3/pallas_call | solution.py:152
  57.2 1.2 %sum_4.1.refs_2_ = f32[2,512,512]{2,1,0:T(8,128)S(1)} custom-call(bf16[2,512,4096]{2,1,0:T(8,128)(2,1)S(1)} %screened.1.refs_0_, bf16[2,256,512]{2,1,0:T(8,128)(2,1)S(1)} %collective-permute-done.9.refs_1_, bf16[2,256,512]{2,1,0:T(8,128)(2,1)S(1)} %collective-permute-done.11.refs_2_, bf16[2,256,512]{2,1,0:T(8,128)(2,1)S(1)} %collective-permute-done.10.refs_3_, ...), custom_call_target="tpu_custom_call" | custom-call | flops 1073741824 | bytes 1048576 | tf_op jit(solution)/shard_map/sum_4/pallas_call | solution.py:152
  58.5 0.9 sum_5.1
  59.4 0.7 collective-permute-start.16
  60.1 18.8 %collective-permute-start.15 = (bf16[2,256,512]{2,1,0:T(8,128)(2,1)S(1)}, bf16[2,256,512]{2,1,0:T(8,128)(2,1)S(1)}, u32[]{:S(2)}, u32[]{:S(2)}) collective-permute-start(bf16[2,256,512]{2,1,0:T(8,128)(2,1)S(1)} %sum_5.1), channel_id=1, source_target_pairs={{0,1008},{1,1009},{2,1010},{3,1011},{4,1012},{5,1013},{6,1014},{7,... | collective-permute-start | bytes 1572872 | tf_op jit(solution)/shard_map/ppermute | solution.py:64
  78.9 0.7 collective-permute-start.17
  79.6 40.9 %collective-permute-done.15 = bf16[2,256,512]{2,1,0:T(8,128)(2,1)S(1)} collective-permute-done((bf16[2,256,512]{2,1,0:T(8,128)(2,1)S(1)}, bf16[2,256,512]{2,1,0:T(8,128)(2,1)S(1)}, u32[]{:S(2)}, u32[]{:S(2)}) %collective-permute-start.15) | collective-permute-done | bytes 524320 | tf_op jit(solution)/shard_map/ppermute | solution.py:64
  120.5 1.0 add_convert_fusion
  (27 shorter events, 0.1 us)
Async XLA Ops:
  0.0 15.2 %collective-permute-start = (bf16[2,256,512]{2,1,0:T(8,128)(2,1)}, bf16[2,256,512]{2,1,0:T(8,128)(2,1)S(1)}, u32[]{:S(2)}, u32[]{:S(2)}) collective-permute-start(bf16[2,256,512]{2,1,0:T(8,128)(2,1)} %refs_1_.1), channel_id=1, source_target_pairs={{0,2},{2,4},{4,6},{6,8},{8,10},{10,12},{12,14},{14,0},{1,15},{3,1}... | collective-permute-start | bytes 1572872 | tf_op jit(solution)/shard_map/ppermute | solution.py:29
  4.7 16.0 %collective-permute-start.2 = (bf16[2,256,512]{2,1,0:T(8,128)(2,1)}, bf16[2,256,512]{2,1,0:T(8,128)(2,1)S(1)}, u32[]{:S(2)}, u32[]{:S(2)}) collective-permute-start(bf16[2,256,512]{2,1,0:T(8,128)(2,1)} %refs_1_.1), channel_id=1, source_target_pairs={{1,2},{3,4},{5,6},{7,8},{9,10},{11,12},{13,14},{15,0},{0,15},{2,1}... | collective-permute-start | bytes 1572872 | tf_op jit(solution)/shard_map/ppermute | solution.py:29
  6.6 1.5 %copy-start.5 = (s32[16]{0:T(128)S(1)}, s32[16]{0:T(128)}, u32[]{:S(2)}) copy-start(s32[16]{0:T(128)} %constant.54.clone) | copy-start | bytes 196
  6.6 1.5 %copy-start.6 = (pred[16]{0:T(512)(128)(4,1)S(1)}, pred[16]{0:T(512)(128)(4,1)}, u32[]{:S(2)}) copy-start(pred[16]{0:T(512)(128)(4,1)} %constant.58) | copy-start | bytes 52
  6.6 1.6 %copy-start = (bf16[256,4096]{1,0:T(8,128)(2,1)S(1)}, bf16[256,4096]{1,0:T(8,128)(2,1)}, u32[]{:S(2)}) copy-start(bf16[256,4096]{1,0:T(8,128)(2,1)} %fock.1) | copy-start | bytes 6291460
  8.3 1.6 %copy-start.1 = (bf16[256,4096]{1,0:T(8,128)(2,1)S(1)}, bf16[256,4096]{1,0:T(8,128)(2,1)}, u32[]{:S(2)}) copy-start(bf16[256,4096]{1,0:T(8,128)(2,1)} %ladder.1) | copy-start | bytes 6291460
  9.9 0.7 copy-start.4
  10.5 16.6 %copy-start.2 = (bf16[2,256,512]{2,1,0:T(8,128)(2,1)S(1)}, bf16[2,256,512]{2,1,0:T(8,128)(2,1)}, u32[]{:S(2)}) copy-start(bf16[2,256,512]{2,1,0:T(8,128)(2,1)} %refs_1_.1) | copy-start | bytes 1572868
  15.2 12.9 %collective-permute-start.1 = (bf16[2,256,512]{2,1,0:T(8,128)(2,1)S(1)}, bf16[2,256,512]{2,1,0:T(8,128)(2,1)S(1)}, u32[]{:S(2)}, u32[]{:S(2)}) collective-permute-start(bf16[2,256,512]{2,1,0:T(8,128)(2,1)S(1)} %collective-permute-done.refs_2_), channel_id=1, source_target_pairs={{0,2},{2,4},{4,6},{6,8},{8,10},{10,12},{12,14},{14,0},{1,15},{3,1}... | collective-permute-start | bytes 1572872 | tf_op jit(solution)/shard_map/ppermute | solution.py:29
  20.7 14.2 %collective-permute-start.6 = (bf16[2,256,512]{2,1,0:T(8,128)(2,1)S(1)}, bf16[2,256,512]{2,1,0:T(8,128)(2,1)S(1)}, u32[]{:S(2)}, u32[]{:S(2)}) collective-permute-start(bf16[2,256,512]{2,1,0:T(8,128)(2,1)S(1)} %collective-permute-done.2.refs_3_), channel_id=1, source_target_pairs={{0,2},{2,4},{4,6},{6,8},{8,10},{10,12},{12,14},{14,0},{1,15},{3,1}... | collective-permute-start | bytes 1572872 | tf_op jit(solution)/shard_map/ppermute | solution.py:29
  22.8 15.8 %collective-permute-start.4 = (bf16[2,256,512]{2,1,0:T(8,128)(2,1)S(1)}, bf16[2,256,512]{2,1,0:T(8,128)(2,1)S(1)}, u32[]{:S(2)}, u32[]{:S(2)}) collective-permute-start(bf16[2,256,512]{2,1,0:T(8,128)(2,1)S(1)} %collective-permute-done.refs_2_), channel_id=1, source_target_pairs={{0,1},{1,0},{2,3},{3,2},{4,5},{5,4},{6,7},{7,6},{8,9},{9,8},{10,11... | collective-permute-start | bytes 1572872 | tf_op jit(solution)/shard_map/ppermute | solution.py:22
  24.7 13.9 %collective-permute-start.5 = (bf16[2,256,512]{2,1,0:T(8,128)(2,1)S(1)}, bf16[2,256,512]{2,1,0:T(8,128)(2,1)S(1)}, u32[]{:S(2)}, u32[]{:S(2)}) collective-permute-start(bf16[2,256,512]{2,1,0:T(8,128)(2,1)S(1)} %collective-permute-done.2.refs_3_), channel_id=1, source_target_pairs={{0,1},{1,0},{2,3},{3,2},{4,5},{5,4},{6,7},{7,6},{8,9},{9,8},{10,11... | collective-permute-start | bytes 1572872 | tf_op jit(solution)/shard_map/ppermute | solution.py:22
  28.1 11.7 %collective-permute-start.3 = (bf16[2,256,512]{2,1,0:T(8,128)(2,1)S(1)}, bf16[2,256,512]{2,1,0:T(8,128)(2,1)S(1)}, u32[]{:S(2)}, u32[]{:S(2)}) collective-permute-start(bf16[2,256,512]{2,1,0:T(8,128)(2,1)S(1)} %collective-permute-done.1.refs_3_), channel_id=1, source_target_pairs={{0,2},{2,4},{4,6},{6,8},{8,10},{10,12},{12,14},{14,0},{1,15},{3,1}... | collective-permute-start | bytes 1572872 | tf_op jit(solution)/shard_map/ppermute | solution.py:29
  33.0 16.6 %collective-permute-start.14 = (bf16[2,256,512]{2,1,0:T(8,128)(2,1)S(1)}, bf16[2,256,512]{2,1,0:T(8,128)(2,1)S(1)}, u32[]{:S(2)}, u32[]{:S(2)}) collective-permute-start(bf16[2,256,512]{2,1,0:T(8,128)(2,1)S(1)} %copy-done.2), channel_id=1, source_target_pairs={{0,1},{1,0},{2,3},{3,2},{4,5},{5,4},{6,7},{7,6},{8,9},{9,8},{10,11... | collective-permute-start | bytes 1572872 | tf_op jit(solution)/shard_map/ppermute | solution.py:22
  34.9 16.6 %collective-permute-start.10 = (bf16[2,256,512]{2,1,0:T(8,128)(2,1)S(1)}, bf16[2,256,512]{2,1,0:T(8,128)(2,1)S(1)}, u32[]{:S(2)}, u32[]{:S(2)}) collective-permute-start(bf16[2,256,512]{2,1,0:T(8,128)(2,1)S(1)} %collective-permute-done.6.refs_4_), channel_id=1, source_target_pairs={{0,2},{2,4},{4,6},{6,8},{8,10},{10,12},{12,14},{14,0},{1,15},{3,1}... | collective-permute-start | bytes 1572872 | tf_op jit(solution)/shard_map/ppermute | solution.py:29
  39.9 14.1 %collective-permute-start.7 = (bf16[2,256,512]{2,1,0:T(8,128)(2,1)S(1)}, bf16[2,256,512]{2,1,0:T(8,128)(2,1)S(1)}, u32[]{:S(2)}, u32[]{:S(2)}) collective-permute-start(bf16[2,256,512]{2,1,0:T(8,128)(2,1)S(1)} %collective-permute-done.3.refs_3_), channel_id=1, source_target_pairs={{0,2},{2,4},{4,6},{6,8},{8,10},{10,12},{12,14},{14,0},{1,15},{3,1}... | collective-permute-start | bytes 1572872 | tf_op jit(solution)/shard_map/ppermute | solution.py:29
  45.3 10.6 %collective-permute-start.12 = (bf16[2,256,512]{2,1,0:T(8,128)(2,1)S(1)}, bf16[2,256,512]{2,1,0:T(8,128)(2,1)S(1)}, u32[]{:S(2)}, u32[]{:S(2)}) collective-permute-start(bf16[2,256,512]{2,1,0:T(8,128)(2,1)S(1)} %collective-permute-done.1.refs_3_), channel_id=1, source_target_pairs={{0,1},{1,0},{2,3},{3,2},{4,5},{5,4},{6,7},{7,6},{8,9},{9,8},{10,11... | collective-permute-start | bytes 1572872 | tf_op jit(solution)/shard_map/ppermute | solution.py:22
  47.2 8.7 %collective-permute-start.13 = (bf16[2,256,512]{2,1,0:T(8,128)(2,1)S(1)}, bf16[2,256,512]{2,1,0:T(8,128)(2,1)S(1)}, u32[]{:S(2)}, u32[]{:S(2)}) collective-permute-start(bf16[2,256,512]{2,1,0:T(8,128)(2,1)S(1)} %collective-permute-done.6.refs_4_), channel_id=1, source_target_pairs={{0,1},{1,0},{2,3},{3,2},{4,5},{5,4},{6,7},{7,6},{8,9},{9,8},{10,11... | collective-permute-start | bytes 1572872 | tf_op jit(solution)/shard_map/ppermute | solution.py:22
  49.6 7.6 %collective-permute-start.9 = (bf16[2,256,512]{2,1,0:T(8,128)(2,1)S(1)}, bf16[2,256,512]{2,1,0:T(8,128)(2,1)S(1)}, u32[]{:S(2)}, u32[]{:S(2)}) collective-permute-start(bf16[2,256,512]{2,1,0:T(8,128)(2,1)S(1)} %collective-permute-done.3.refs_3_), channel_id=1, source_target_pairs={{0,1},{1,0},{2,3},{3,2},{4,5},{5,4},{6,7},{7,6},{8,9},{9,8},{10,11... | collective-permute-start | bytes 1572872 | tf_op jit(solution)/shard_map/ppermute | solution.py:22
  51.5 5.7 %collective-permute-start.11 = (bf16[2,256,512]{2,1,0:T(8,128)(2,1)S(1)}, bf16[2,256,512]{2,1,0:T(8,128)(2,1)S(1)}, u32[]{:S(2)}, u32[]{:S(2)}) collective-permute-start(bf16[2,256,512]{2,1,0:T(8,128)(2,1)S(1)} %collective-permute-done.10.refs_3_), channel_id=1, source_target_pairs={{0,1},{1,0},{2,3},{3,2},{4,5},{5,4},{6,7},{7,6},{8,9},{9,8},{10,11... | collective-permute-start | bytes 1572872 | tf_op jit(solution)/shard_map/ppermute | solution.py:22
  54.0 4.5 %collective-permute-start.8 = (bf16[2,256,512]{2,1,0:T(8,128)(2,1)S(1)}, bf16[2,256,512]{2,1,0:T(8,128)(2,1)S(1)}, u32[]{:S(2)}, u32[]{:S(2)}) collective-permute-start(bf16[2,256,512]{2,1,0:T(8,128)(2,1)S(1)} %collective-permute-done.7.refs_4_), channel_id=1, source_target_pairs={{0,1},{1,0},{2,3},{3,2},{4,5},{5,4},{6,7},{7,6},{8,9},{9,8},{10,11... | collective-permute-start | bytes 1572872 | tf_op jit(solution)/shard_map/ppermute | solution.py:22
  57.2 1.3 %copy-start.3 = (bf16[512,512]{1,0:T(8,128)(2,1)S(1)}, bf16[512,512]{1,0:T(8,128)(2,1)}, u32[]{:S(2)}) copy-start(bf16[512,512]{1,0:T(8,128)(2,1)} %refs_3_.1) | copy-start | bytes 1572868
  59.4 19.6 %collective-permute-start.16 = (bf16[2,256,512]{2,1,0:T(8,128)(2,1)S(1)}, bf16[2,256,512]{2,1,0:T(8,128)(2,1)S(1)}, u32[]{:S(2)}, u32[]{:S(2)}) collective-permute-start(bf16[2,256,512]{2,1,0:T(8,128)(2,1)S(1)} %sum_5.1), channel_id=1, source_target_pairs={{48,128},{49,129},{50,130},{51,131},{52,132},{53,133},{54,134},{55... | collective-permute-start | bytes 1572872 | tf_op jit(solution)/shard_map/ppermute | solution.py:63
  60.1 60.4 %collective-permute-start.15 = (bf16[2,256,512]{2,1,0:T(8,128)(2,1)S(1)}, bf16[2,256,512]{2,1,0:T(8,128)(2,1)S(1)}, u32[]{:S(2)}, u32[]{:S(2)}) collective-permute-start(bf16[2,256,512]{2,1,0:T(8,128)(2,1)S(1)} %sum_5.1), channel_id=1, source_target_pairs={{0,1008},{1,1009},{2,1010},{3,1011},{4,1012},{5,1013},{6,1014},{7,... | collective-permute-start | bytes 1572872 | tf_op jit(solution)/shard_map/ppermute | solution.py:64
  78.9 41.6 %collective-permute-start.17 = (bf16[2,256,512]{2,1,0:T(8,128)(2,1)S(1)}, bf16[2,256,512]{2,1,0:T(8,128)(2,1)S(1)}, u32[]{:S(2)}, u32[]{:S(2)}) collective-permute-start(bf16[2,256,512]{2,1,0:T(8,128)(2,1)S(1)} %collective-permute-done.16), channel_id=1, source_target_pairs={{128,240},{129,241},{130,242},{131,243},{132,244},{133,245},{134,2... | collective-permute-start | bytes 1572872 | tf_op jit(solution)/shard_map/ppermute | solution.py:65

commit v8 on v6

--- a/solution.py
+++ b/solution.py
@@ -35,10 +35,10 @@
 
 def detours(rows):
     moves = []
-    for x in range(rows):
+    for x, z in enumerate((3, 1, 2, 3)):
         for core in range(2):
-            moves.append(((x, RING // 4 - 1), (x, RING // 2), core))
-            moves.append(((x, RING - RING // 4), (x, RING // 2 - 1), core))
+            moves.append(((x, z), (x, RING // 2), core))
+            moves.append(((rows - 1 - x, RING - 1 - z), (rows - 1 - x, RING // 2 - 1), core))
     for z, row in ((5, 1), (6, 2), (9, 1), (10, 2)):
         moves.append(((0, z), (row, z), 0))
         moves.append(((rows - 1, RING - 1 - z), (rows - 1 - row, RING - 1 - z), 1))

time: 122 us -> 117 us (0.959)
  the two profiles are of different devices: /device:TPU:28 before, /device:TPU:1 now
where the time goes in v8:
time: 117 us; the launch traced here: 116 us
  starting transfers between devices  67.1 us (57%)
  waiting for transfers between devices  34.2 us (29%)
  Pallas kernels  8.63 us (7%)
  local copies, waits for them, and re-layouts  3.96 us (3%)
  other arithmetic  1.78 us (2%)
    ppermute x7, starting transfers between devices, ring_step(): return lax.ppermute(block, 'virt', route)  38.1 us
    ppermute x1, waiting for transfers between devices, mirror_swap(): straight = lax.ppermute(block, axes, direct)  34.2 us
    ppermute x8, starting transfers between devices, core_swap(): return lax.ppermute(block, 'virt', [(v, v ^ 1) for v in range(count)])  21.2 us
    ppermute x1, starting transfers between devices, mirror_swap(): straight = lax.ppermute(block, axes, direct)  6.44 us
    pallas_call x5, Pallas kernels, sum_slots(): pl.pallas_call(functools.partial(sum_kernel, pairs, slots, acc is not Non...  5.6 us
    unnamed x8, local copies, waits for them, and re-layouts  3.19 us
    pallas_call x1, Pallas kernels, screened(): pl.pallas_call(functools.partial(screen_kernel, pairs), out_shape=jax.Sha...  3.04 us
  transfers between devices with their start and end apart: 18, of which 1 were waited for; matrix products, arithmetic and copies ran while one was open for 1% of the time, Pallas kernels for 7%

profile of v8, /device:TPU:1, one launch (start us, length us, event | category | flops | bytes accessed | tf_op | source)
XLA Modules:
  0.0 116.1 jit_solution(16168154255332716875)
XLA Ops:
  0.0 5.9 %collective-permute-start = (bf16[2,256,512]{2,1,0:T(8,128)(2,1)}, bf16[2,256,512]{2,1,0:T(8,128)(2,1)S(1)}, u32[]{:S(2)}, u32[]{:S(2)}) collective-permute-start(bf16[2,256,512]{2,1,0:T(8,128)(2,1)} %refs_1_.1), channel_id=1, source_target_pairs={{0,2},{2,4},{4,6},{6,8},{8,10},{10,12},{12,14},{14,0},{1,15},{3,1}... | collective-permute-start | bytes 1572872 | tf_op jit(solution)/shard_map/ppermute | solution.py:28
  5.9 2.2 %collective-permute-start.2 = (bf16[2,256,512]{2,1,0:T(8,128)(2,1)}, bf16[2,256,512]{2,1,0:T(8,128)(2,1)S(1)}, u32[]{:S(2)}, u32[]{:S(2)}) collective-permute-start(bf16[2,256,512]{2,1,0:T(8,128)(2,1)} %refs_1_.1), channel_id=1, source_target_pairs={{1,2},{3,4},{5,6},{7,8},{9,10},{11,12},{13,14},{15,0},{0,15},{2,1}... | collective-permute-start | bytes 1572872 | tf_op jit(solution)/shard_map/ppermute | solution.py:28
  8.1 0.8 copy.8
  8.9 0.7 fusion.2.slot_ref
  9.6 0.1 fusion
  9.7 0.0 copy-start
  9.7 1.6 %copy-done = bf16[256,4096]{1,0:T(8,128)(2,1)S(1)} copy-done((bf16[256,4096]{1,0:T(8,128)(2,1)S(1)}, bf16[256,4096]{1,0:T(8,128)(2,1)}, u32[]{:S(2)}) %copy-start) | copy-done | bytes 2097176
  11.3 1.6 %copy-done.1 = bf16[256,4096]{1,0:T(8,128)(2,1)S(1)} copy-done((bf16[256,4096]{1,0:T(8,128)(2,1)S(1)}, bf16[256,4096]{1,0:T(8,128)(2,1)}, u32[]{:S(2)}) %copy-start.1) | copy-done | bytes 2097176
  12.9 3.0 %screened.1.refs_0_ = bf16[2,512,4096]{2,1,0:T(8,128)(2,1)S(1)} custom-call(s32[16]{0:T(128)S(1)} %fusion.2.slot_ref, s32[4,32]{1,0:T(4,128)S(1)} %convert_element_type.15.mask_ref, bf16[256,4096]{1,0:T(8,128)(2,1)S(1)} %copy-done, bf16[256,4096]{1,0:T(8,128)(2,1)S(1)} %copy-done.1), custom_call_target="tpu_custom_call" | custom-call | bytes 4194304 | tf_op jit(solution)/shard_map/screened/pallas_call | solution.py:92
  15.9 14.3 %collective-permute-start.1 = (bf16[2,256,512]{2,1,0:T(8,128)(2,1)S(1)}, bf16[2,256,512]{2,1,0:T(8,128)(2,1)S(1)}, u32[]{:S(2)}, u32[]{:S(2)}) collective-permute-start(bf16[2,256,512]{2,1,0:T(8,128)(2,1)S(1)} %collective-permute-done.refs_2_), channel_id=1, source_target_pairs={{0,2},{2,4},{4,6},{6,8},{8,10},{10,12},{12,14},{14,0},{1,15},{3,1}... | collective-permute-start | bytes 1572872 | tf_op jit(solution)/shard_map/ppermute | solution.py:28
  30.3 3.6 %collective-permute-start.6 = (bf16[2,256,512]{2,1,0:T(8,128)(2,1)S(1)}, bf16[2,256,512]{2,1,0:T(8,128)(2,1)S(1)}, u32[]{:S(2)}, u32[]{:S(2)}) collective-permute-start(bf16[2,256,512]{2,1,0:T(8,128)(2,1)S(1)} %collective-permute-done.2.refs_3_), channel_id=1, source_target_pairs={{0,2},{2,4},{4,6},{6,8},{8,10},{10,12},{12,14},{14,0},{1,15},{3,1}... | collective-permute-start | bytes 1572872 | tf_op jit(solution)/shard_map/ppermute | solution.py:28
  33.9 2.7 %collective-permute-start.4 = (bf16[2,256,512]{2,1,0:T(8,128)(2,1)S(1)}, bf16[2,256,512]{2,1,0:T(8,128)(2,1)S(1)}, u32[]{:S(2)}, u32[]{:S(2)}) collective-permute-start(bf16[2,256,512]{2,1,0:T(8,128)(2,1)S(1)} %collective-permute-done.refs_2_), channel_id=1, source_target_pairs={{0,1},{1,0},{2,3},{3,2},{4,5},{5,4},{6,7},{7,6},{8,9},{9,8},{10,11... | collective-permute-start | bytes 1572872 | tf_op jit(solution)/shard_map/ppermute | solution.py:21
  36.6 1.9 %collective-permute-start.5 = (bf16[2,256,512]{2,1,0:T(8,128)(2,1)S(1)}, bf16[2,256,512]{2,1,0:T(8,128)(2,1)S(1)}, u32[]{:S(2)}, u32[]{:S(2)}) collective-permute-start(bf16[2,256,512]{2,1,0:T(8,128)(2,1)S(1)} %collective-permute-done.2.refs_3_), channel_id=1, source_target_pairs={{0,1},{1,0},{2,3},{3,2},{4,5},{5,4},{6,7},{7,6},{8,9},{9,8},{10,11... | collective-permute-start | bytes 1572872 | tf_op jit(solution)/shard_map/ppermute | solution.py:21
  38.6 1.0 sum_1.1.refs_5_
  39.6 4.9 %collective-permute-start.3 = (bf16[2,256,512]{2,1,0:T(8,128)(2,1)S(1)}, bf16[2,256,512]{2,1,0:T(8,128)(2,1)S(1)}, u32[]{:S(2)}, u32[]{:S(2)}) collective-permute-start(bf16[2,256,512]{2,1,0:T(8,128)(2,1)S(1)} %collective-permute-done.1.refs_3_), channel_id=1, source_target_pairs={{0,2},{2,4},{4,6},{6,8},{8,10},{10,12},{12,14},{14,0},{1,15},{3,1}... | collective-permute-start | bytes 1572872 | tf_op jit(solution)/shard_map/ppermute | solution.py:28
  44.4 2.5 %collective-permute-start.14 = (bf16[2,256,512]{2,1,0:T(8,128)(2,1)S(1)}, bf16[2,256,512]{2,1,0:T(8,128)(2,1)S(1)}, u32[]{:S(2)}, u32[]{:S(2)}) collective-permute-start(bf16[2,256,512]{2,1,0:T(8,128)(2,1)S(1)} %copy-done.2), channel_id=1, source_target_pairs={{0,1},{1,0},{2,3},{3,2},{4,5},{5,4},{6,7},{7,6},{8,9},{9,8},{10,11... | collective-permute-start | bytes 1572872 | tf_op jit(solution)/shard_map/ppermute | solution.py:21
  47.0 4.9 %collective-permute-start.10 = (bf16[2,256,512]{2,1,0:T(8,128)(2,1)S(1)}, bf16[2,256,512]{2,1,0:T(8,128)(2,1)S(1)}, u32[]{:S(2)}, u32[]{:S(2)}) collective-permute-start(bf16[2,256,512]{2,1,0:T(8,128)(2,1)S(1)} %collective-permute-done.6.refs_4_), channel_id=1, source_target_pairs={{0,2},{2,4},{4,6},{6,8},{8,10},{10,12},{12,14},{14,0},{1,15},{3,1}... | collective-permute-start | bytes 1572872 | tf_op jit(solution)/shard_map/ppermute | solution.py:28
  51.8 1.2 %sum_2.1.refs_5_ = f32[2,512,512]{2,1,0:T(8,128)S(1)} custom-call(bf16[2,512,4096]{2,1,0:T(8,128)(2,1)S(1)} %screened.1.refs_0_, bf16[2,256,512]{2,1,0:T(8,128)(2,1)S(1)} %collective-permute-done.4.refs_1_, bf16[2,256,512]{2,1,0:T(8,128)(2,1)S(1)} %collective-permute-done.5.refs_2_, bf16[2,256,512]{2,1,0:T(8,128)(2,1)S(1)} %collective-permute-done.1.refs_3_, ...), custom_call_target="tpu_custom_call" | custom-call | flops 1073741824 | bytes 1048576 | tf_op jit(solution)/shard_map/sum_2/pallas_call | solution.py:130
  53.1 2.4 %collective-permute-start.7 = (bf16[2,256,512]{2,1,0:T(8,128)(2,1)S(1)}, bf16[2,256,512]{2,1,0:T(8,128)(2,1)S(1)}, u32[]{:S(2)}, u32[]{:S(2)}) collective-permute-start(bf16[2,256,512]{2,1,0:T(8,128)(2,1)S(1)} %collective-permute-done.3.refs_3_), channel_id=1, source_target_pairs={{0,2},{2,4},{4,6},{6,8},{8,10},{10,12},{12,14},{14,0},{1,15},{3,1}... | collective-permute-start | bytes 1572872 | tf_op jit(solution)/shard_map/ppermute | solution.py:28
  55.5 3.7 %collective-permute-start.12 = (bf16[2,256,512]{2,1,0:T(8,128)(2,1)S(1)}, bf16[2,256,512]{2,1,0:T(8,128)(2,1)S(1)}, u32[]{:S(2)}, u32[]{:S(2)}) collective-permute-start(bf16[2,256,512]{2,1,0:T(8,128)(2,1)S(1)} %collective-permute-done.1.refs_3_), channel_id=1, source_target_pairs={{0,1},{1,0},{2,3},{3,2},{4,5},{5,4},{6,7},{7,6},{8,9},{9,8},{10,11... | collective-permute-start | bytes 1572872 | tf_op jit(solution)/shard_map/ppermute | solution.py:21
  59.2 1.9 %collective-permute-start.13 = (bf16[2,256,512]{2,1,0:T(8,128)(2,1)S(1)}, bf16[2,256,512]{2,1,0:T(8,128)(2,1)S(1)}, u32[]{:S(2)}, u32[]{:S(2)}) collective-permute-start(bf16[2,256,512]{2,1,0:T(8,128)(2,1)S(1)} %collective-permute-done.6.refs_4_), channel_id=1, source_target_pairs={{0,1},{1,0},{2,3},{3,2},{4,5},{5,4},{6,7},{7,6},{8,9},{9,8},{10,11... | collective-permute-start | bytes 1572872 | tf_op jit(solution)/shard_map/ppermute | solution.py:21
  61.2 2.4 %collective-permute-start.9 = (bf16[2,256,512]{2,1,0:T(8,128)(2,1)S(1)}, bf16[2,256,512]{2,1,0:T(8,128)(2,1)S(1)}, u32[]{:S(2)}, u32[]{:S(2)}) collective-permute-start(bf16[2,256,512]{2,1,0:T(8,128)(2,1)S(1)} %collective-permute-done.3.refs_3_), channel_id=1, source_target_pairs={{0,1},{1,0},{2,3},{3,2},{4,5},{5,4},{6,7},{7,6},{8,9},{9,8},{10,11... | collective-permute-start | bytes 1572872 | tf_op jit(solution)/shard_map/ppermute | solution.py:21
  63.6 1.9 %collective-permute-start.11 = (bf16[2,256,512]{2,1,0:T(8,128)(2,1)S(1)}, bf16[2,256,512]{2,1,0:T(8,128)(2,1)S(1)}, u32[]{:S(2)}, u32[]{:S(2)}) collective-permute-start(bf16[2,256,512]{2,1,0:T(8,128)(2,1)S(1)} %collective-permute-done.10.refs_3_), channel_id=1, source_target_pairs={{0,1},{1,0},{2,3},{3,2},{4,5},{5,4},{6,7},{7,6},{8,9},{9,8},{10,11... | collective-permute-start | bytes 1572872 | tf_op jit(solution)/shard_map/ppermute | solution.py:21
  65.5 4.0 %collective-permute-start.8 = (bf16[2,256,512]{2,1,0:T(8,128)(2,1)S(1)}, bf16[2,256,512]{2,1,0:T(8,128)(2,1)S(1)}, u32[]{:S(2)}, u32[]{:S(2)}) collective-permute-start(bf16[2,256,512]{2,1,0:T(8,128)(2,1)S(1)} %collective-permute-done.7.refs_4_), channel_id=1, source_target_pairs={{0,1},{1,0},{2,3},{3,2},{4,5},{5,4},{6,7},{7,6},{8,9},{9,8},{10,11... | collective-permute-start | bytes 1572872 | tf_op jit(solution)/shard_map/ppermute | solution.py:21
  69.6 1.2 %sum_3.1.refs_5_ = f32[2,512,512]{2,1,0:T(8,128)S(1)} custom-call(bf16[2,512,4096]{2,1,0:T(8,128)(2,1)S(1)} %screened.1.refs_0_, bf16[2,256,512]{2,1,0:T(8,128)(2,1)S(1)} %collective-permute-done.12.refs_1_, bf16[2,256,512]{2,1,0:T(8,128)(2,1)S(1)} %collective-permute-done.13.refs_2_, bf16[2,256,512]{2,1,0:T(8,128)(2,1)S(1)} %collective-permute-done.3.refs_3_, ...), custom_call_target="tpu_custom_call" | custom-call | flops 1073741824 | bytes 1048576 | tf_op jit(solution)/shard_map/sum_3/pallas_call | solution.py:130
  70.9 1.2 %sum_4.1.refs_2_ = f32[2,512,512]{2,1,0:T(8,128)S(1)} custom-call(bf16[2,512,4096]{2,1,0:T(8,128)(2,1)S(1)} %screened.1.refs_0_, bf16[2,256,512]{2,1,0:T(8,128)(2,1)S(1)} %collective-permute-done.9.refs_1_, bf16[2,256,512]{2,1,0:T(8,128)(2,1)S(1)} %collective-permute-done.11.refs_2_, bf16[2,256,512]{2,1,0:T(8,128)(2,1)S(1)} %collective-permute-done.10.refs_3_, ...), custom_call_target="tpu_custom_call" | custom-call | flops 1073741824 | bytes 1048576 | tf_op jit(solution)/shard_map/sum_4/pallas_call | solution.py:130
  72.2 0.9 sum_5.1
  73.0 0.7 collective-permute-start.16
  73.7 6.4 %collective-permute-start.15 = (bf16[2,256,512]{2,1,0:T(8,128)(2,1)S(1)}, bf16[2,256,512]{2,1,0:T(8,128)(2,1)S(1)}, u32[]{:S(2)}, u32[]{:S(2)}) collective-permute-start(bf16[2,256,512]{2,1,0:T(8,128)(2,1)S(1)} %sum_5.1), channel_id=1, source_target_pairs={{0,1008},{1,1009},{2,1010},{3,1011},{4,1012},{5,1013},{6,1014},{7,... | collective-permute-start | bytes 1572872 | tf_op jit(solution)/shard_map/ppermute | solution.py:63
  80.2 0.7 collective-permute-start.17
  80.9 34.2 %collective-permute-done.15 = bf16[2,256,512]{2,1,0:T(8,128)(2,1)S(1)} collective-permute-done((bf16[2,256,512]{2,1,0:T(8,128)(2,1)S(1)}, bf16[2,256,512]{2,1,0:T(8,128)(2,1)S(1)}, u32[]{:S(2)}, u32[]{:S(2)}) %collective-permute-start.15) | collective-permute-done | bytes 524320 | tf_op jit(solution)/shard_map/ppermute | solution.py:63
  115.1 1.0 add_convert_fusion
  (23 shorter events, 0.1 us)
Async XLA Ops:
  0.0 15.9 %collective-permute-start = (bf16[2,256,512]{2,1,0:T(8,128)(2,1)}, bf16[2,256,512]{2,1,0:T(8,128)(2,1)S(1)}, u32[]{:S(2)}, u32[]{:S(2)}) collective-permute-start(bf16[2,256,512]{2,1,0:T(8,128)(2,1)} %refs_1_.1), channel_id=1, source_target_pairs={{0,2},{2,4},{4,6},{6,8},{8,10},{10,12},{12,14},{14,0},{1,15},{3,1}... | collective-permute-start | bytes 1572872 | tf_op jit(solution)/shard_map/ppermute | solution.py:28
  5.9 24.3 %collective-permute-start.2 = (bf16[2,256,512]{2,1,0:T(8,128)(2,1)}, bf16[2,256,512]{2,1,0:T(8,128)(2,1)S(1)}, u32[]{:S(2)}, u32[]{:S(2)}) collective-permute-start(bf16[2,256,512]{2,1,0:T(8,128)(2,1)} %refs_1_.1), channel_id=1, source_target_pairs={{1,2},{3,4},{5,6},{7,8},{9,10},{11,12},{13,14},{15,0},{0,15},{2,1}... | collective-permute-start | bytes 1572872 | tf_op jit(solution)/shard_map/ppermute | solution.py:28
  9.7 1.6 %copy-start = (bf16[256,4096]{1,0:T(8,128)(2,1)S(1)}, bf16[256,4096]{1,0:T(8,128)(2,1)}, u32[]{:S(2)}) copy-start(bf16[256,4096]{1,0:T(8,128)(2,1)} %fock.1) | copy-start | bytes 6291460
  11.3 1.6 %copy-start.1 = (bf16[256,4096]{1,0:T(8,128)(2,1)S(1)}, bf16[256,4096]{1,0:T(8,128)(2,1)}, u32[]{:S(2)}) copy-start(bf16[256,4096]{1,0:T(8,128)(2,1)} %ladder.1) | copy-start | bytes 6291460
  12.9 25.7 %copy-start.2 = (bf16[2,256,512]{2,1,0:T(8,128)(2,1)S(1)}, bf16[2,256,512]{2,1,0:T(8,128)(2,1)}, u32[]{:S(2)}) copy-start(bf16[2,256,512]{2,1,0:T(8,128)(2,1)} %refs_1_.1) | copy-start | bytes 1572868
  15.9 23.6 %collective-permute-start.1 = (bf16[2,256,512]{2,1,0:T(8,128)(2,1)S(1)}, bf16[2,256,512]{2,1,0:T(8,128)(2,1)S(1)}, u32[]{:S(2)}, u32[]{:S(2)}) collective-permute-start(bf16[2,256,512]{2,1,0:T(8,128)(2,1)S(1)} %collective-permute-done.refs_2_), channel_id=1, source_target_pairs={{0,2},{2,4},{4,6},{6,8},{8,10},{10,12},{12,14},{14,0},{1,15},{3,1}... | collective-permute-start | bytes 1572872 | tf_op jit(solution)/shard_map/ppermute | solution.py:28
  30.3 16.7 %collective-permute-start.6 = (bf16[2,256,512]{2,1,0:T(8,128)(2,1)S(1)}, bf16[2,256,512]{2,1,0:T(8,128)(2,1)S(1)}, u32[]{:S(2)}, u32[]{:S(2)}) collective-permute-start(bf16[2,256,512]{2,1,0:T(8,128)(2,1)S(1)} %collective-permute-done.2.refs_3_), channel_id=1, source_target_pairs={{0,2},{2,4},{4,6},{6,8},{8,10},{10,12},{12,14},{14,0},{1,15},{3,1}... | collective-permute-start | bytes 1572872 | tf_op jit(solution)/shard_map/ppermute | solution.py:28
  33.9 18.0 %collective-permute-start.4 = (bf16[2,256,512]{2,1,0:T(8,128)(2,1)S(1)}, bf16[2,256,512]{2,1,0:T(8,128)(2,1)S(1)}, u32[]{:S(2)}, u32[]{:S(2)}) collective-permute-start(bf16[2,256,512]{2,1,0:T(8,128)(2,1)S(1)} %collective-permute-done.refs_2_), channel_id=1, source_target_pairs={{0,1},{1,0},{2,3},{3,2},{4,5},{5,4},{6,7},{7,6},{8,9},{9,8},{10,11... | collective-permute-start | bytes 1572872 | tf_op jit(solution)/shard_map/ppermute | solution.py:21
  36.6 15.2 %collective-permute-start.5 = (bf16[2,256,512]{2,1,0:T(8,128)(2,1)S(1)}, bf16[2,256,512]{2,1,0:T(8,128)(2,1)S(1)}, u32[]{:S(2)}, u32[]{:S(2)}) collective-permute-start(bf16[2,256,512]{2,1,0:T(8,128)(2,1)S(1)} %collective-permute-done.2.refs_3_), channel_id=1, source_target_pairs={{0,1},{1,0},{2,3},{3,2},{4,5},{5,4},{6,7},{7,6},{8,9},{9,8},{10,11... | collective-permute-start | bytes 1572872 | tf_op jit(solution)/shard_map/ppermute | solution.py:21
  39.6 13.6 %collective-permute-start.3 = (bf16[2,256,512]{2,1,0:T(8,128)(2,1)S(1)}, bf16[2,256,512]{2,1,0:T(8,128)(2,1)S(1)}, u32[]{:S(2)}, u32[]{:S(2)}) collective-permute-start(bf16[2,256,512]{2,1,0:T(8,128)(2,1)S(1)} %collective-permute-done.1.refs_3_), channel_id=1, source_target_pairs={{0,2},{2,4},{4,6},{6,8},{8,10},{10,12},{12,14},{14,0},{1,15},{3,1}... | collective-permute-start | bytes 1572872 | tf_op jit(solution)/shard_map/ppermute | solution.py:28
  44.4 16.8 %collective-permute-start.14 = (bf16[2,256,512]{2,1,0:T(8,128)(2,1)S(1)}, bf16[2,256,512]{2,1,0:T(8,128)(2,1)S(1)}, u32[]{:S(2)}, u32[]{:S(2)}) collective-permute-start(bf16[2,256,512]{2,1,0:T(8,128)(2,1)S(1)} %copy-done.2), channel_id=1, source_target_pairs={{0,1},{1,0},{2,3},{3,2},{4,5},{5,4},{6,7},{7,6},{8,9},{9,8},{10,11... | collective-permute-start | bytes 1572872 | tf_op jit(solution)/shard_map/ppermute | solution.py:21
  47.0 16.6 %collective-permute-start.10 = (bf16[2,256,512]{2,1,0:T(8,128)(2,1)S(1)}, bf16[2,256,512]{2,1,0:T(8,128)(2,1)S(1)}, u32[]{:S(2)}, u32[]{:S(2)}) collective-permute-start(bf16[2,256,512]{2,1,0:T(8,128)(2,1)S(1)} %collective-permute-done.6.refs_4_), channel_id=1, source_target_pairs={{0,2},{2,4},{4,6},{6,8},{8,10},{10,12},{12,14},{14,0},{1,15},{3,1}... | collective-permute-start | bytes 1572872 | tf_op jit(solution)/shard_map/ppermute | solution.py:28
  53.1 12.4 %collective-permute-start.7 = (bf16[2,256,512]{2,1,0:T(8,128)(2,1)S(1)}, bf16[2,256,512]{2,1,0:T(8,128)(2,1)S(1)}, u32[]{:S(2)}, u32[]{:S(2)}) collective-permute-start(bf16[2,256,512]{2,1,0:T(8,128)(2,1)S(1)} %collective-permute-done.3.refs_3_), channel_id=1, source_target_pairs={{0,2},{2,4},{4,6},{6,8},{8,10},{10,12},{12,14},{14,0},{1,15},{3,1}... | collective-permute-start | bytes 1572872 | tf_op jit(solution)/shard_map/ppermute | solution.py:28
  55.5 14.0 %collective-permute-start.12 = (bf16[2,256,512]{2,1,0:T(8,128)(2,1)S(1)}, bf16[2,256,512]{2,1,0:T(8,128)(2,1)S(1)}, u32[]{:S(2)}, u32[]{:S(2)}) collective-permute-start(bf16[2,256,512]{2,1,0:T(8,128)(2,1)S(1)} %collective-permute-done.1.refs_3_), channel_id=1, source_target_pairs={{0,1},{1,0},{2,3},{3,2},{4,5},{5,4},{6,7},{7,6},{8,9},{9,8},{10,11... | collective-permute-start | bytes 1572872 | tf_op jit(solution)/shard_map/ppermute | solution.py:21
  59.2 10.4 %collective-permute-start.13 = (bf16[2,256,512]{2,1,0:T(8,128)(2,1)S(1)}, bf16[2,256,512]{2,1,0:T(8,128)(2,1)S(1)}, u32[]{:S(2)}, u32[]{:S(2)}) collective-permute-start(bf16[2,256,512]{2,1,0:T(8,128)(2,1)S(1)} %collective-permute-done.6.refs_4_), channel_id=1, source_target_pairs={{0,1},{1,0},{2,3},{3,2},{4,5},{5,4},{6,7},{7,6},{8,9},{9,8},{10,11... | collective-permute-start | bytes 1572872 | tf_op jit(solution)/shard_map/ppermute | solution.py:21
  61.2 9.7 %collective-permute-start.9 = (bf16[2,256,512]{2,1,0:T(8,128)(2,1)S(1)}, bf16[2,256,512]{2,1,0:T(8,128)(2,1)S(1)}, u32[]{:S(2)}, u32[]{:S(2)}) collective-permute-start(bf16[2,256,512]{2,1,0:T(8,128)(2,1)S(1)} %collective-permute-done.3.refs_3_), channel_id=1, source_target_pairs={{0,1},{1,0},{2,3},{3,2},{4,5},{5,4},{6,7},{7,6},{8,9},{9,8},{10,11... | collective-permute-start | bytes 1572872 | tf_op jit(solution)/shard_map/ppermute | solution.py:21
  63.6 7.3 %collective-permute-start.11 = (bf16[2,256,512]{2,1,0:T(8,128)(2,1)S(1)}, bf16[2,256,512]{2,1,0:T(8,128)(2,1)S(1)}, u32[]{:S(2)}, u32[]{:S(2)}) collective-permute-start(bf16[2,256,512]{2,1,0:T(8,128)(2,1)S(1)} %collective-permute-done.10.refs_3_), channel_id=1, source_target_pairs={{0,1},{1,0},{2,3},{3,2},{4,5},{5,4},{6,7},{7,6},{8,9},{9,8},{10,11... | collective-permute-start | bytes 1572872 | tf_op jit(solution)/shard_map/ppermute | solution.py:21
  65.5 6.6 %collective-permute-start.8 = (bf16[2,256,512]{2,1,0:T(8,128)(2,1)S(1)}, bf16[2,256,512]{2,1,0:T(8,128)(2,1)S(1)}, u32[]{:S(2)}, u32[]{:S(2)}) collective-permute-start(bf16[2,256,512]{2,1,0:T(8,128)(2,1)S(1)} %collective-permute-done.7.refs_4_), channel_id=1, source_target_pairs={{0,1},{1,0},{2,3},{3,2},{4,5},{5,4},{6,7},{7,6},{8,9},{9,8},{10,11... | collective-permute-start | bytes 1572872 | tf_op jit(solution)/shard_map/ppermute | solution.py:21
  70.9 1.3 %copy-start.3 = (bf16[512,512]{1,0:T(8,128)(2,1)S(1)}, bf16[512,512]{1,0:T(8,128)(2,1)}, u32[]{:S(2)}) copy-start(bf16[512,512]{1,0:T(8,128)(2,1)} %refs_3_.1) | copy-start | bytes 1572868
  73.0 7.1 %collective-permute-start.16 = (bf16[2,256,512]{2,1,0:T(8,128)(2,1)S(1)}, bf16[2,256,512]{2,1,0:T(8,128)(2,1)S(1)}, u32[]{:S(2)}, u32[]{:S(2)}) collective-permute-start(bf16[2,256,512]{2,1,0:T(8,128)(2,1)S(1)} %sum_5.1), channel_id=1, source_target_pairs={{48,128},{49,129},{50,130},{51,131},{52,132},{53,133},{54,134},{55... | collective-permute-start | bytes 1572872 | tf_op jit(solution)/shard_map/ppermute | solution.py:62
  73.7 41.3 %collective-permute-start.15 = (bf16[2,256,512]{2,1,0:T(8,128)(2,1)S(1)}, bf16[2,256,512]{2,1,0:T(8,128)(2,1)S(1)}, u32[]{:S(2)}, u32[]{:S(2)}) collective-permute-start(bf16[2,256,512]{2,1,0:T(8,128)(2,1)S(1)} %sum_5.1), channel_id=1, source_target_pairs={{0,1008},{1,1009},{2,1010},{3,1011},{4,1012},{5,1013},{6,1014},{7,... | collective-permute-start | bytes 1572872 | tf_op jit(solution)/shard_map/ppermute | solution.py:63
  80.2 34.9 %collective-permute-start.17 = (bf16[2,256,512]{2,1,0:T(8,128)(2,1)S(1)}, bf16[2,256,512]{2,1,0:T(8,128)(2,1)S(1)}, u32[]{:S(2)}, u32[]{:S(2)}) collective-permute-start(bf16[2,256,512]{2,1,0:T(8,128)(2,1)S(1)} %collective-permute-done.16), channel_id=1, source_target_pairs={{128,240},{129,241},{130,242},{131,243},{132,244},{133,245},{134,2... | collective-permute-start | bytes 1572872 | tf_op jit(solution)/shard_map/ppermute | solution.py:64

commit v9 on v8

--- a/solution.py
+++ b/solution.py
@@ -13,7 +13,7 @@
 VMEM_LIMIT = 24 * 1024 * 1024
 RING = 16
 HOPS = (None, (0, 0), (1, 0), (1, 1), (2, 0), (2, 1), (3, 0), (3, 1), (4, 0))
-ORDER = (1, 2, 3, -2, -3, 4, 5, -4, -5, 6, -1, -6, -7, 7, 8, -8)
+ORDER = (1, 2, 3, -2, -3, 4, 5, -4, -1, -5, 6, -6, -7, 7, 8, -8)
 
 
 def core_swap(block):
@@ -100,17 +100,18 @@
     )(slot_tiles, masks, fock, ladder)
 
 
-def sum_kernel(pairs, slots, has_acc, finish, *refs):
+def sum_kernel(pairs, slots, block_count, has_acc, finish, *refs):
     refs = list(refs)
     take = lambda n: [refs.pop(0) for _ in range(n)]
-    mat, blocks = take(1)[0], take(len(slots))
+    mat, blocks = take(1)[0], take(block_count)
     acc_in = take(1)[0] if has_acc else None
     couple_ref = take(1)[0] if finish else None
     out, a_buf = refs
     lo, depth = slots[0] * HALF, len(slots) * HALF
     for p in range(pairs):
-        for n, block in enumerate(blocks):
-            a_buf[n * HALF : (n + 1) * HALF, :] = block[p]
+        held = [block.at[k + p] for block in blocks for k in range(0, block.shape[0], pairs)]
+        for n, block in enumerate(held):
+            a_buf[n * HALF : (n + 1) * HALF, :] = block[...]
         acc = jnp.dot(mat[p, :, lo : lo + depth], a_buf[...], preferred_element_type=jnp.float32)
         if has_acc:
             acc = acc_in[p] + acc
@@ -121,14 +122,15 @@
 
 
 def sum_slots(name, mat, blocks, first, acc=None, couple=None):
-    pairs, _, width = blocks[0].shape
-    slots, finish = tuple(range(first, first + len(blocks))), couple is not None
+    pairs, width = mat.shape[0], blocks[0].shape[2]
+    held = sum(block.shape[0] for block in blocks) // pairs
+    slots, finish = tuple(range(first, first + held)), couple is not None
     vmem = pl.BlockSpec(memory_space=pltpu.VMEM)
     operands = [mat, *blocks] + ([acc] if acc is not None else []) + ([couple] if finish else [])
     out_shape = jax.ShapeDtypeStruct((pairs, HALF if finish else 2 * HALF, width), jnp.bfloat16 if finish else jnp.float32)
     flops = 2 * pairs * 2 * HALF * width * (len(slots) * HALF + (width // 2 if finish else 0))
     return pl.pallas_call(
-        functools.partial(sum_kernel, pairs, slots, acc is not None, finish),
+        functools.partial(sum_kernel, pairs, slots, len(blocks), acc is not None, finish),
         out_shape=out_shape,
         in_specs=[vmem] * len(operands),
         out_specs=vmem,
@@ -162,9 +164,10 @@
     x3, s3 = ring_step(after(x2, acc)), ring_step(s2)
     acc = sum_slots("sum_2", mat, (core_swap(x1), core_swap(s1), x2, s2), 3, acc)
     x4 = ring_step(after(x3, acc))
-    acc = sum_slots("sum_3", mat, (core_swap(x2), core_swap(s2), x3, core_swap(x0)), 7, acc)
+    acc = sum_slots("sum_3", mat, (core_swap(jnp.concatenate([x2, x0])), core_swap(s2), x3), 7, acc)
     acc = sum_slots("sum_4", mat, (core_swap(x3), core_swap(s3), s3, x4), 11, acc)
-    half_term = sum_slots("sum_5", mat, (core_swap(x4),), 15, acc, couple)
+    x4_other = core_swap(x4)
+    half_term = sum_slots("sum_5", mat, (x4_other,), 15, acc, couple)
     terms = [term.astype(jnp.float32) for term in (half_term, *mirror_swap(half_term))]
     return (terms[0] + (terms[1] + terms[2])).astype(jnp.bfloat16)
 

time: 117 us -> 117 us (level)
    ppermute x8 -> x7, starting transfers between devices: 21.2 us -> 21.1 us  [core_swap(): return lax.ppermute(block, 'virt', [(v, v ^ 1) for v in range(count)])]
  transfers between devices with their start and end apart: 18 -> 17, of which waited for: 1 -> 2; matrix products, arithmetic and copies ran while one was open for 1% -> 1% of each run, Pallas kernels for 7% -> 7%
where the time goes in v9:
time: 117 us; the launch traced here: 116 us
  starting transfers between devices  67 us (57%)
  waiting for transfers between devices  34.3 us (29%)
  Pallas kernels  8.58 us (7%)
  local copies, waits for them, and re-layouts  3.96 us (3%)
  other arithmetic  1.87 us (2%)
    ppermute x7, starting transfers between devices, ring_step(): return lax.ppermute(block, 'virt', route)  38.1 us
    ppermute x1, waiting for transfers between devices, mirror_swap(): straight = lax.ppermute(block, axes, direct)  34.2 us
    ppermute x7, starting transfers between devices, core_swap(): return lax.ppermute(block, 'virt', [(v, v ^ 1) for v in range(count)])  21.1 us
    ppermute x1, starting transfers between devices, mirror_swap(): straight = lax.ppermute(block, axes, direct)  6.43 us
    pallas_call x5, Pallas kernels, sum_slots(): pl.pallas_call(functools.partial(sum_kernel, pairs, slots, len(blocks), a...  5.59 us
    unnamed x8, local copies, waits for them, and re-layouts  3.19 us
    pallas_call x1, Pallas kernels, screened(): pl.pallas_call(functools.partial(screen_kernel, pairs), out_shape=jax.Sha...  2.99 us
  transfers between devices with their start and end apart: 17, of which 2 were waited for; matrix products, arithmetic and copies ran while one was open for 1% of the time, Pallas kernels for 7%

profile of v9, /device:TPU:1, one launch (start us, length us, event | category | flops | bytes accessed | tf_op | source)
XLA Modules:
  0.0 116.0 jit_solution(16341556260826095664)
XLA Ops:
  0.0 5.9 %collective-permute-start = (bf16[2,256,512]{2,1,0:T(8,128)(2,1)}, bf16[2,256,512]{2,1,0:T(8,128)(2,1)S(1)}, u32[]{:S(2)}, u32[]{:S(2)}) collective-permute-start(bf16[2,256,512]{2,1,0:T(8,128)(2,1)} %refs_1_.1), channel_id=1, source_target_pairs={{0,2},{2,4},{4,6},{6,8},{8,10},{10,12},{12,14},{14,0},{1,15},{3,1}... | collective-permute-start | bytes 1572872 | tf_op jit(solution)/shard_map/ppermute | solution.py:28
  5.9 2.2 %collective-permute-start.2 = (bf16[2,256,512]{2,1,0:T(8,128)(2,1)}, bf16[2,256,512]{2,1,0:T(8,128)(2,1)S(1)}, u32[]{:S(2)}, u32[]{:S(2)}) collective-permute-start(bf16[2,256,512]{2,1,0:T(8,128)(2,1)} %refs_1_.1), channel_id=1, source_target_pairs={{1,2},{3,4},{5,6},{7,8},{9,10},{11,12},{13,14},{15,0},{0,15},{2,1}... | collective-permute-start | bytes 1572872 | tf_op jit(solution)/shard_map/ppermute | solution.py:28
  8.1 0.8 copy.8
  8.9 0.7 fusion.2.slot_ref
  9.6 0.1 fusion
  9.7 1.6 %copy-done.1 = bf16[256,4096]{1,0:T(8,128)(2,1)S(1)} copy-done((bf16[256,4096]{1,0:T(8,128)(2,1)S(1)}, bf16[256,4096]{1,0:T(8,128)(2,1)}, u32[]{:S(2)}) %copy-start.1) | copy-done | bytes 2097176
  11.3 1.6 %copy-done.2 = bf16[256,4096]{1,0:T(8,128)(2,1)S(1)} copy-done((bf16[256,4096]{1,0:T(8,128)(2,1)S(1)}, bf16[256,4096]{1,0:T(8,128)(2,1)}, u32[]{:S(2)}) %copy-start.2) | copy-done | bytes 2097176
  12.9 3.0 %screened.1.refs_0_ = bf16[2,512,4096]{2,1,0:T(8,128)(2,1)S(1)} custom-call(s32[16]{0:T(128)S(1)} %fusion.2.slot_ref, s32[4,32]{1,0:T(4,128)S(1)} %convert_element_type.15.mask_ref, bf16[256,4096]{1,0:T(8,128)(2,1)S(1)} %copy-done.1, bf16[256,4096]{1,0:T(8,128)(2,1)S(1)} %copy-done.2), custom_call_target="tpu_custom_call" | custom-call | bytes 4194304 | tf_op jit(solution)/shard_map/screened/pallas_call | solution.py:92
  15.9 14.4 %collective-permute-start.1 = (bf16[2,256,512]{2,1,0:T(8,128)(2,1)S(1)}, bf16[2,256,512]{2,1,0:T(8,128)(2,1)S(1)}, u32[]{:S(2)}, u32[]{:S(2)}) collective-permute-start(bf16[2,256,512]{2,1,0:T(8,128)(2,1)S(1)} %collective-permute-done.refs_2_), channel_id=1, source_target_pairs={{0,2},{2,4},{4,6},{6,8},{8,10},{10,12},{12,14},{14,0},{1,15},{3,1}... | collective-permute-start | bytes 1572872 | tf_op jit(solution)/shard_map/ppermute | solution.py:28
  30.2 3.6 %collective-permute-start.6 = (bf16[2,256,512]{2,1,0:T(8,128)(2,1)S(1)}, bf16[2,256,512]{2,1,0:T(8,128)(2,1)S(1)}, u32[]{:S(2)}, u32[]{:S(2)}) collective-permute-start(bf16[2,256,512]{2,1,0:T(8,128)(2,1)S(1)} %collective-permute-done.2.refs_3_), channel_id=1, source_target_pairs={{0,2},{2,4},{4,6},{6,8},{8,10},{10,12},{12,14},{14,0},{1,15},{3,1}... | collective-permute-start | bytes 1572872 | tf_op jit(solution)/shard_map/ppermute | solution.py:28
  33.9 2.7 %collective-permute-start.4 = (bf16[2,256,512]{2,1,0:T(8,128)(2,1)S(1)}, bf16[2,256,512]{2,1,0:T(8,128)(2,1)S(1)}, u32[]{:S(2)}, u32[]{:S(2)}) collective-permute-start(bf16[2,256,512]{2,1,0:T(8,128)(2,1)S(1)} %collective-permute-done.refs_2_), channel_id=1, source_target_pairs={{0,1},{1,0},{2,3},{3,2},{4,5},{5,4},{6,7},{7,6},{8,9},{9,8},{10,11... | collective-permute-start | bytes 1572872 | tf_op jit(solution)/shard_map/ppermute | solution.py:21
  36.6 1.9 %collective-permute-start.5 = (bf16[2,256,512]{2,1,0:T(8,128)(2,1)S(1)}, bf16[2,256,512]{2,1,0:T(8,128)(2,1)S(1)}, u32[]{:S(2)}, u32[]{:S(2)}) collective-permute-start(bf16[2,256,512]{2,1,0:T(8,128)(2,1)S(1)} %collective-permute-done.2.refs_3_), channel_id=1, source_target_pairs={{0,1},{1,0},{2,3},{3,2},{4,5},{5,4},{6,7},{7,6},{8,9},{9,8},{10,11... | collective-permute-start | bytes 1572872 | tf_op jit(solution)/shard_map/ppermute | solution.py:21
  38.6 1.0 sum_1.1.refs_5_
  39.6 4.9 %collective-permute-start.3 = (bf16[2,256,512]{2,1,0:T(8,128)(2,1)S(1)}, bf16[2,256,512]{2,1,0:T(8,128)(2,1)S(1)}, u32[]{:S(2)}, u32[]{:S(2)}) collective-permute-start(bf16[2,256,512]{2,1,0:T(8,128)(2,1)S(1)} %collective-permute-done.1.refs_3_), channel_id=1, source_target_pairs={{0,2},{2,4},{4,6},{6,8},{8,10},{10,12},{12,14},{14,0},{1,15},{3,1}... | collective-permute-start | bytes 1572872 | tf_op jit(solution)/shard_map/ppermute | solution.py:28
  44.4 0.1 pad_maximum_fusion
  44.5 2.5 %collective-permute-start.12 = (bf16[4,256,512]{2,1,0:T(8,128)(2,1)S(1)}, bf16[4,256,512]{2,1,0:T(8,128)(2,1)S(1)}, u32[]{:S(2)}, u32[]{:S(2)}) collective-permute-start(bf16[4,256,512]{2,1,0:T(8,128)(2,1)S(1)} %pad_maximum_fusion), channel_id=1, source_target_pairs={{0,1},{1,0},{2,3},{3,2},{4,5},{5,4},{6,7},{7,6},{8,9},{9,8},{10,11... | collective-permute-start | bytes 3145736 | tf_op jit(solution)/shard_map/ppermute | solution.py:21
  47.1 4.9 %collective-permute-start.10 = (bf16[2,256,512]{2,1,0:T(8,128)(2,1)S(1)}, bf16[2,256,512]{2,1,0:T(8,128)(2,1)S(1)}, u32[]{:S(2)}, u32[]{:S(2)}) collective-permute-start(bf16[2,256,512]{2,1,0:T(8,128)(2,1)S(1)} %collective-permute-done.6.refs_4_), channel_id=1, source_target_pairs={{0,2},{2,4},{4,6},{6,8},{8,10},{10,12},{12,14},{14,0},{1,15},{3,1}... | collective-permute-start | bytes 1572872 | tf_op jit(solution)/shard_map/ppermute | solution.py:28
  52.0 1.2 %sum_2.1.refs_4_ = f32[2,512,512]{2,1,0:T(8,128)S(1)} custom-call(bf16[2,512,4096]{2,1,0:T(8,128)(2,1)S(1)} %screened.1.refs_0_, bf16[2,256,512]{2,1,0:T(8,128)(2,1)S(1)} %collective-permute-done.4.refs_1_, bf16[2,256,512]{2,1,0:T(8,128)(2,1)S(1)} %collective-permute-done.5.refs_2_, bf16[2,256,512]{2,1,0:T(8,128)(2,1)S(1)} %collective-permute-done.1.refs_3_, ...), custom_call_target="tpu_custom_call" | custom-call | flops 1073741824 | bytes 1048576 | tf_op jit(solution)/shard_map/sum_2/pallas_call | solution.py:132
  53.2 2.3 %collective-permute-start.7 = (bf16[2,256,512]{2,1,0:T(8,128)(2,1)S(1)}, bf16[2,256,512]{2,1,0:T(8,128)(2,1)S(1)}, u32[]{:S(2)}, u32[]{:S(2)}) collective-permute-start(bf16[2,256,512]{2,1,0:T(8,128)(2,1)S(1)} %collective-permute-done.3.refs_3_), channel_id=1, source_target_pairs={{0,2},{2,4},{4,6},{6,8},{8,10},{10,12},{12,14},{14,0},{1,15},{3,1}... | collective-permute-start | bytes 1572872 | tf_op jit(solution)/shard_map/ppermute | solution.py:28
  55.5 3.7 %collective-permute-start.13 = (bf16[2,256,512]{2,1,0:T(8,128)(2,1)S(1)}, bf16[2,256,512]{2,1,0:T(8,128)(2,1)S(1)}, u32[]{:S(2)}, u32[]{:S(2)}) collective-permute-start(bf16[2,256,512]{2,1,0:T(8,128)(2,1)S(1)} %collective-permute-done.6.refs_4_), channel_id=1, source_target_pairs={{0,1},{1,0},{2,3},{3,2},{4,5},{5,4},{6,7},{7,6},{8,9},{9,8},{10,11... | collective-permute-start | bytes 1572872 | tf_op jit(solution)/shard_map/ppermute | solution.py:21
  59.2 1.9 %collective-permute-start.9 = (bf16[2,256,512]{2,1,0:T(8,128)(2,1)S(1)}, bf16[2,256,512]{2,1,0:T(8,128)(2,1)S(1)}, u32[]{:S(2)}, u32[]{:S(2)}) collective-permute-start(bf16[2,256,512]{2,1,0:T(8,128)(2,1)S(1)} %collective-permute-done.3.refs_3_), channel_id=1, source_target_pairs={{0,1},{1,0},{2,3},{3,2},{4,5},{5,4},{6,7},{7,6},{8,9},{9,8},{10,11... | collective-permute-start | bytes 1572872 | tf_op jit(solution)/shard_map/ppermute | solution.py:21
  61.2 2.4 %collective-permute-start.11 = (bf16[2,256,512]{2,1,0:T(8,128)(2,1)S(1)}, bf16[2,256,512]{2,1,0:T(8,128)(2,1)S(1)}, u32[]{:S(2)}, u32[]{:S(2)}) collective-permute-start(bf16[2,256,512]{2,1,0:T(8,128)(2,1)S(1)} %collective-permute-done.10.refs_3_), channel_id=1, source_target_pairs={{0,1},{1,0},{2,3},{3,2},{4,5},{5,4},{6,7},{7,6},{8,9},{9,8},{10,11... | collective-permute-start | bytes 1572872 | tf_op jit(solution)/shard_map/ppermute | solution.py:21
  63.6 0.1 collective-permute-done.7.refs_4_
  63.7 5.9 %collective-permute-start.8 = (bf16[2,256,512]{2,1,0:T(8,128)(2,1)S(1)}, bf16[2,256,512]{2,1,0:T(8,128)(2,1)S(1)}, u32[]{:S(2)}, u32[]{:S(2)}) collective-permute-start(bf16[2,256,512]{2,1,0:T(8,128)(2,1)S(1)} %collective-permute-done.7.refs_4_), channel_id=1, source_target_pairs={{0,1},{1,0},{2,3},{3,2},{4,5},{5,4},{6,7},{7,6},{8,9},{9,8},{10,11... | collective-permute-start | bytes 1572872 | tf_op jit(solution)/shard_map/ppermute | solution.py:21
  69.6 1.2 %sum_3.1.refs_5_ = f32[2,512,512]{2,1,0:T(8,128)S(1)} custom-call(bf16[2,512,4096]{2,1,0:T(8,128)(2,1)S(1)} %screened.1.refs_0_, bf16[4,256,512]{2,1,0:T(8,128)(2,1)S(1)} %collective-permute-done.12.refs_1_, bf16[2,256,512]{2,1,0:T(8,128)(2,1)S(1)} %collective-permute-done.13.refs_2_, bf16[2,256,512]{2,1,0:T(8,128)(2,1)S(1)} %collective-permute-done.3.refs_3_, ...), custom_call_target="tpu_custom_call" | custom-call | flops 1073741824 | bytes 1048576 | tf_op jit(solution)/shard_map/sum_3/pallas_call | solution.py:132
  70.9 1.2 %sum_4.1.refs_2_ = f32[2,512,512]{2,1,0:T(8,128)S(1)} custom-call(bf16[2,512,4096]{2,1,0:T(8,128)(2,1)S(1)} %screened.1.refs_0_, bf16[2,256,512]{2,1,0:T(8,128)(2,1)S(1)} %collective-permute-done.9.refs_1_, bf16[2,256,512]{2,1,0:T(8,128)(2,1)S(1)} %collective-permute-done.11.refs_2_, bf16[2,256,512]{2,1,0:T(8,128)(2,1)S(1)} %collective-permute-done.10.refs_3_, ...), custom_call_target="tpu_custom_call" | custom-call | flops 1073741824 | bytes 1048576 | tf_op jit(solution)/shard_map/sum_4/pallas_call | solution.py:132
  72.2 0.9 sum_5.1
  73.0 0.7 collective-permute-start.15
  73.7 6.4 %collective-permute-start.14 = (bf16[2,256,512]{2,1,0:T(8,128)(2,1)S(1)}, bf16[2,256,512]{2,1,0:T(8,128)(2,1)S(1)}, u32[]{:S(2)}, u32[]{:S(2)}) collective-permute-start(bf16[2,256,512]{2,1,0:T(8,128)(2,1)S(1)} %sum_5.1), channel_id=1, source_target_pairs={{0,1008},{1,1009},{2,1010},{3,1011},{4,1012},{5,1013},{6,1014},{7,... | collective-permute-start | bytes 1572872 | tf_op jit(solution)/shard_map/ppermute | solution.py:63
  80.2 0.7 collective-permute-start.16
  80.9 34.2 %collective-permute-done.14 = bf16[2,256,512]{2,1,0:T(8,128)(2,1)S(1)} collective-permute-done((bf16[2,256,512]{2,1,0:T(8,128)(2,1)S(1)}, bf16[2,256,512]{2,1,0:T(8,128)(2,1)S(1)}, u32[]{:S(2)}, u32[]{:S(2)}) %collective-permute-start.14) | collective-permute-done | bytes 524320 | tf_op jit(solution)/shard_map/ppermute | solution.py:63
  115.0 1.0 add_convert_fusion
  (22 shorter events, 0.1 us)
Async XLA Ops:
  0.0 15.9 %collective-permute-start = (bf16[2,256,512]{2,1,0:T(8,128)(2,1)}, bf16[2,256,512]{2,1,0:T(8,128)(2,1)S(1)}, u32[]{:S(2)}, u32[]{:S(2)}) collective-permute-start(bf16[2,256,512]{2,1,0:T(8,128)(2,1)} %refs_1_.1), channel_id=1, source_target_pairs={{0,2},{2,4},{4,6},{6,8},{8,10},{10,12},{12,14},{14,0},{1,15},{3,1}... | collective-permute-start | bytes 1572872 | tf_op jit(solution)/shard_map/ppermute | solution.py:28
  5.9 24.3 %collective-permute-start.2 = (bf16[2,256,512]{2,1,0:T(8,128)(2,1)}, bf16[2,256,512]{2,1,0:T(8,128)(2,1)S(1)}, u32[]{:S(2)}, u32[]{:S(2)}) collective-permute-start(bf16[2,256,512]{2,1,0:T(8,128)(2,1)} %refs_1_.1), channel_id=1, source_target_pairs={{1,2},{3,4},{5,6},{7,8},{9,10},{11,12},{13,14},{15,0},{0,15},{2,1}... | collective-permute-start | bytes 1572872 | tf_op jit(solution)/shard_map/ppermute | solution.py:28
  9.7 1.6 %copy-start.1 = (bf16[256,4096]{1,0:T(8,128)(2,1)S(1)}, bf16[256,4096]{1,0:T(8,128)(2,1)}, u32[]{:S(2)}) copy-start(bf16[256,4096]{1,0:T(8,128)(2,1)} %fock.1) | copy-start | bytes 6291460
  11.3 1.6 %copy-start.2 = (bf16[256,4096]{1,0:T(8,128)(2,1)S(1)}, bf16[256,4096]{1,0:T(8,128)(2,1)}, u32[]{:S(2)}) copy-start(bf16[256,4096]{1,0:T(8,128)(2,1)} %ladder.1) | copy-start | bytes 6291460
  12.9 25.7 %copy-start = (bf16[2,256,512]{2,1,0:T(8,128)(2,1)S(1)}, bf16[2,256,512]{2,1,0:T(8,128)(2,1)}, u32[]{:S(2)}) copy-start(bf16[2,256,512]{2,1,0:T(8,128)(2,1)} %refs_1_.1) | copy-start | bytes 1572868
  15.9 23.7 %collective-permute-start.1 = (bf16[2,256,512]{2,1,0:T(8,128)(2,1)S(1)}, bf16[2,256,512]{2,1,0:T(8,128)(2,1)S(1)}, u32[]{:S(2)}, u32[]{:S(2)}) collective-permute-start(bf16[2,256,512]{2,1,0:T(8,128)(2,1)S(1)} %collective-permute-done.refs_2_), channel_id=1, source_target_pairs={{0,2},{2,4},{4,6},{6,8},{8,10},{10,12},{12,14},{14,0},{1,15},{3,1}... | collective-permute-start | bytes 1572872 | tf_op jit(solution)/shard_map/ppermute | solution.py:28
  30.2 16.8 %collective-permute-start.6 = (bf16[2,256,512]{2,1,0:T(8,128)(2,1)S(1)}, bf16[2,256,512]{2,1,0:T(8,128)(2,1)S(1)}, u32[]{:S(2)}, u32[]{:S(2)}) collective-permute-start(bf16[2,256,512]{2,1,0:T(8,128)(2,1)S(1)} %collective-permute-done.2.refs_3_), channel_id=1, source_target_pairs={{0,2},{2,4},{4,6},{6,8},{8,10},{10,12},{12,14},{14,0},{1,15},{3,1}... | collective-permute-start | bytes 1572872 | tf_op jit(solution)/shard_map/ppermute | solution.py:28
  33.9 18.1 %collective-permute-start.4 = (bf16[2,256,512]{2,1,0:T(8,128)(2,1)S(1)}, bf16[2,256,512]{2,1,0:T(8,128)(2,1)S(1)}, u32[]{:S(2)}, u32[]{:S(2)}) collective-permute-start(bf16[2,256,512]{2,1,0:T(8,128)(2,1)S(1)} %collective-permute-done.refs_2_), channel_id=1, source_target_pairs={{0,1},{1,0},{2,3},{3,2},{4,5},{5,4},{6,7},{7,6},{8,9},{9,8},{10,11... | collective-permute-start | bytes 1572872 | tf_op jit(solution)/shard_map/ppermute | solution.py:21
  36.6 15.3 %collective-permute-start.5 = (bf16[2,256,512]{2,1,0:T(8,128)(2,1)S(1)}, bf16[2,256,512]{2,1,0:T(8,128)(2,1)S(1)}, u32[]{:S(2)}, u32[]{:S(2)}) collective-permute-start(bf16[2,256,512]{2,1,0:T(8,128)(2,1)S(1)} %collective-permute-done.2.refs_3_), channel_id=1, source_target_pairs={{0,1},{1,0},{2,3},{3,2},{4,5},{5,4},{6,7},{7,6},{8,9},{9,8},{10,11... | collective-permute-start | bytes 1572872 | tf_op jit(solution)/shard_map/ppermute | solution.py:21
  39.6 13.7 %collective-permute-start.3 = (bf16[2,256,512]{2,1,0:T(8,128)(2,1)S(1)}, bf16[2,256,512]{2,1,0:T(8,128)(2,1)S(1)}, u32[]{:S(2)}, u32[]{:S(2)}) collective-permute-start(bf16[2,256,512]{2,1,0:T(8,128)(2,1)S(1)} %collective-permute-done.1.refs_3_), channel_id=1, source_target_pairs={{0,2},{2,4},{4,6},{6,8},{8,10},{10,12},{12,14},{14,0},{1,15},{3,1}... | collective-permute-start | bytes 1572872 | tf_op jit(solution)/shard_map/ppermute | solution.py:28
  44.5 25.1 %collective-permute-start.12 = (bf16[4,256,512]{2,1,0:T(8,128)(2,1)S(1)}, bf16[4,256,512]{2,1,0:T(8,128)(2,1)S(1)}, u32[]{:S(2)}, u32[]{:S(2)}) collective-permute-start(bf16[4,256,512]{2,1,0:T(8,128)(2,1)S(1)} %pad_maximum_fusion), channel_id=1, source_target_pairs={{0,1},{1,0},{2,3},{3,2},{4,5},{5,4},{6,7},{7,6},{8,9},{9,8},{10,11... | collective-permute-start | bytes 3145736 | tf_op jit(solution)/shard_map/ppermute | solution.py:21
  47.1 14.1 %collective-permute-start.10 = (bf16[2,256,512]{2,1,0:T(8,128)(2,1)S(1)}, bf16[2,256,512]{2,1,0:T(8,128)(2,1)S(1)}, u32[]{:S(2)}, u32[]{:S(2)}) collective-permute-start(bf16[2,256,512]{2,1,0:T(8,128)(2,1)S(1)} %collective-permute-done.6.refs_4_), channel_id=1, source_target_pairs={{0,2},{2,4},{4,6},{6,8},{8,10},{10,12},{12,14},{14,0},{1,15},{3,1}... | collective-permute-start | bytes 1572872 | tf_op jit(solution)/shard_map/ppermute | solution.py:28
  53.2 10.4 %collective-permute-start.7 = (bf16[2,256,512]{2,1,0:T(8,128)(2,1)S(1)}, bf16[2,256,512]{2,1,0:T(8,128)(2,1)S(1)}, u32[]{:S(2)}, u32[]{:S(2)}) collective-permute-start(bf16[2,256,512]{2,1,0:T(8,128)(2,1)S(1)} %collective-permute-done.3.refs_3_), channel_id=1, source_target_pairs={{0,2},{2,4},{4,6},{6,8},{8,10},{10,12},{12,14},{14,0},{1,15},{3,1}... | collective-permute-start | bytes 1572872 | tf_op jit(solution)/shard_map/ppermute | solution.py:28
  55.5 14.0 %collective-permute-start.13 = (bf16[2,256,512]{2,1,0:T(8,128)(2,1)S(1)}, bf16[2,256,512]{2,1,0:T(8,128)(2,1)S(1)}, u32[]{:S(2)}, u32[]{:S(2)}) collective-permute-start(bf16[2,256,512]{2,1,0:T(8,128)(2,1)S(1)} %collective-permute-done.6.refs_4_), channel_id=1, source_target_pairs={{0,1},{1,0},{2,3},{3,2},{4,5},{5,4},{6,7},{7,6},{8,9},{9,8},{10,11... | collective-permute-start | bytes 1572872 | tf_op jit(solution)/shard_map/ppermute | solution.py:21
  59.2 11.6 %collective-permute-start.9 = (bf16[2,256,512]{2,1,0:T(8,128)(2,1)S(1)}, bf16[2,256,512]{2,1,0:T(8,128)(2,1)S(1)}, u32[]{:S(2)}, u32[]{:S(2)}) collective-permute-start(bf16[2,256,512]{2,1,0:T(8,128)(2,1)S(1)} %collective-permute-done.3.refs_3_), channel_id=1, source_target_pairs={{0,1},{1,0},{2,3},{3,2},{4,5},{5,4},{6,7},{7,6},{8,9},{9,8},{10,11... | collective-permute-start | bytes 1572872 | tf_op jit(solution)/shard_map/ppermute | solution.py:21
  61.2 9.7 %collective-permute-start.11 = (bf16[2,256,512]{2,1,0:T(8,128)(2,1)S(1)}, bf16[2,256,512]{2,1,0:T(8,128)(2,1)S(1)}, u32[]{:S(2)}, u32[]{:S(2)}) collective-permute-start(bf16[2,256,512]{2,1,0:T(8,128)(2,1)S(1)} %collective-permute-done.10.refs_3_), channel_id=1, source_target_pairs={{0,1},{1,0},{2,3},{3,2},{4,5},{5,4},{6,7},{7,6},{8,9},{9,8},{10,11... | collective-permute-start | bytes 1572872 | tf_op jit(solution)/shard_map/ppermute | solution.py:21
  63.7 8.5 %collective-permute-start.8 = (bf16[2,256,512]{2,1,0:T(8,128)(2,1)S(1)}, bf16[2,256,512]{2,1,0:T(8,128)(2,1)S(1)}, u32[]{:S(2)}, u32[]{:S(2)}) collective-permute-start(bf16[2,256,512]{2,1,0:T(8,128)(2,1)S(1)} %collective-permute-done.7.refs_4_), channel_id=1, source_target_pairs={{0,1},{1,0},{2,3},{3,2},{4,5},{5,4},{6,7},{7,6},{8,9},{9,8},{10,11... | collective-permute-start | bytes 1572872 | tf_op jit(solution)/shard_map/ppermute | solution.py:21
  70.9 1.3 %copy-start.3 = (bf16[512,512]{1,0:T(8,128)(2,1)S(1)}, bf16[512,512]{1,0:T(8,128)(2,1)}, u32[]{:S(2)}) copy-start(bf16[512,512]{1,0:T(8,128)(2,1)} %refs_3_.1) | copy-start | bytes 1572868
  73.0 7.1 %collective-permute-start.15 = (bf16[2,256,512]{2,1,0:T(8,128)(2,1)S(1)}, bf16[2,256,512]{2,1,0:T(8,128)(2,1)S(1)}, u32[]{:S(2)}, u32[]{:S(2)}) collective-permute-start(bf16[2,256,512]{2,1,0:T(8,128)(2,1)S(1)} %sum_5.1), channel_id=1, source_target_pairs={{48,128},{49,129},{50,130},{51,131},{52,132},{53,133},{54,134},{55... | collective-permute-start | bytes 1572872 | tf_op jit(solution)/shard_map/ppermute | solution.py:62
  73.7 41.3 %collective-permute-start.14 = (bf16[2,256,512]{2,1,0:T(8,128)(2,1)S(1)}, bf16[2,256,512]{2,1,0:T(8,128)(2,1)S(1)}, u32[]{:S(2)}, u32[]{:S(2)}) collective-permute-start(bf16[2,256,512]{2,1,0:T(8,128)(2,1)S(1)} %sum_5.1), channel_id=1, source_target_pairs={{0,1008},{1,1009},{2,1010},{3,1011},{4,1012},{5,1013},{6,1014},{7,... | collective-permute-start | bytes 1572872 | tf_op jit(solution)/shard_map/ppermute | solution.py:63
  80.2 34.9 %collective-permute-start.16 = (bf16[2,256,512]{2,1,0:T(8,128)(2,1)S(1)}, bf16[2,256,512]{2,1,0:T(8,128)(2,1)S(1)}, u32[]{:S(2)}, u32[]{:S(2)}) collective-permute-start(bf16[2,256,512]{2,1,0:T(8,128)(2,1)S(1)} %collective-permute-done.15), channel_id=1, source_target_pairs={{128,240},{129,241},{130,242},{131,243},{132,244},{133,245},{134,2... | collective-permute-start | bytes 1572872 | tf_op jit(solution)/shard_map/ppermute | solution.py:64

commit v10 on v9

--- a/solution.py
+++ b/solution.py
@@ -160,12 +160,11 @@
     x1, s1 = ring_step(x0), ring_step(x0, cross=1)
     mat = screened(slot_tiles, masks, fock, ladder, pairs)
     x2, s2 = ring_step(after(x1, mat)), ring_step(s1)
-    acc = sum_slots("sum_1", mat, (x0, x1, s1), 0)
-    x3, s3 = ring_step(after(x2, acc)), ring_step(s2)
-    acc = sum_slots("sum_2", mat, (core_swap(x1), core_swap(s1), x2, s2), 3, acc)
+    x3, s3 = ring_step(x2), ring_step(s2)
+    acc = sum_slots("sum_1", mat, (x0, x1, s1, core_swap(x1), core_swap(s1), x2, s2), 0)
     x4 = ring_step(after(x3, acc))
-    acc = sum_slots("sum_3", mat, (core_swap(jnp.concatenate([x2, x0])), core_swap(s2), x3), 7, acc)
-    acc = sum_slots("sum_4", mat, (core_swap(x3), core_swap(s3), s3, x4), 11, acc)
+    early = (core_swap(jnp.concatenate([x2, x0])), core_swap(s2), x3)
+    acc = sum_slots("sum_3", mat, (*early, core_swap(x3), core_swap(s3), s3, x4), 7, acc)
     x4_other = core_swap(x4)
     half_term = sum_slots("sum_5", mat, (x4_other,), 15, acc, couple)
     terms = [term.astype(jnp.float32) for term in (half_term, *mirror_swap(half_term))]

time: 117 us -> 117 us (level)
    pallas_call x5 -> x3, Pallas kernels: 5.59 us -> 5.25 us  [sum_slots(): pl.pallas_call(functools.partial(sum_kernel, pairs, slots, len(blocks), a...]
  transfers between devices with their start and end apart: 17 -> 17, of which waited for: 2 -> 2; matrix products, arithmetic and copies ran while one was open for 1% -> 1% of each run, Pallas kernels for 7% -> 6%
where the time goes in v10:
time: 117 us; the launch traced here: 116 us
  starting transfers between devices  66.5 us (57%)
  waiting for transfers between devices  35 us (30%)
  Pallas kernels  8.19 us (7%)
  local copies, waits for them, and re-layouts  3.96 us (3%)
  other arithmetic  1.88 us (2%)
    ppermute x7, starting transfers between devices, ring_step(): return lax.ppermute(block, 'virt', route)  37.9 us
    ppermute x1, waiting for transfers between devices, mirror_swap(): straight = lax.ppermute(block, axes, direct)  34.2 us
    ppermute x7, starting transfers between devices, core_swap(): return lax.ppermute(block, 'virt', [(v, v ^ 1) for v in range(count)])  20.8 us
    ppermute x1, starting transfers between devices, mirror_swap(): straight = lax.ppermute(block, axes, direct)  6.45 us
    pallas_call x3, Pallas kernels, sum_slots(): pl.pallas_call(functools.partial(sum_kernel, pairs, slots, len(blocks), a...  5.25 us
    unnamed x8, local copies, waits for them, and re-layouts  3.19 us
    pallas_call x1, Pallas kernels, screened(): pl.pallas_call(functools.partial(screen_kernel, pairs), out_shape=jax.Sha...  2.94 us
  transfers between devices with their start and end apart: 17, of which 2 were waited for; matrix products, arithmetic and copies ran while one was open for 1% of the time, Pallas kernels for 6%

profile of v10, /device:TPU:1, one launch (start us, length us, event | category | flops | bytes accessed | tf_op | source)
XLA Modules:
  0.0 115.9 jit_solution(11706307690435919586)
XLA Ops:
  0.0 5.9 %collective-permute-start = (bf16[2,256,512]{2,1,0:T(8,128)(2,1)}, bf16[2,256,512]{2,1,0:T(8,128)(2,1)S(1)}, u32[]{:S(2)}, u32[]{:S(2)}) collective-permute-start(bf16[2,256,512]{2,1,0:T(8,128)(2,1)} %refs_1_.1), channel_id=1, source_target_pairs={{0,2},{2,4},{4,6},{6,8},{8,10},{10,12},{12,14},{14,0},{1,15},{3,1}... | collective-permute-start | bytes 1572872 | tf_op jit(solution)/shard_map/ppermute | solution.py:28
  5.9 2.2 %collective-permute-start.3 = (bf16[2,256,512]{2,1,0:T(8,128)(2,1)}, bf16[2,256,512]{2,1,0:T(8,128)(2,1)S(1)}, u32[]{:S(2)}, u32[]{:S(2)}) collective-permute-start(bf16[2,256,512]{2,1,0:T(8,128)(2,1)} %refs_1_.1), channel_id=1, source_target_pairs={{1,2},{3,4},{5,6},{7,8},{9,10},{11,12},{13,14},{15,0},{0,15},{2,1}... | collective-permute-start | bytes 1572872 | tf_op jit(solution)/shard_map/ppermute | solution.py:28
  8.1 0.8 copy.8
  8.9 0.1 fusion
  9.0 0.7 fusion.2.slot_ref
  9.7 0.0 copy-start.1
  9.7 1.6 %copy-done.1 = bf16[256,4096]{1,0:T(8,128)(2,1)S(1)} copy-done((bf16[256,4096]{1,0:T(8,128)(2,1)S(1)}, bf16[256,4096]{1,0:T(8,128)(2,1)}, u32[]{:S(2)}) %copy-start.1) | copy-done | bytes 2097176
  11.3 1.6 %copy-done.2 = bf16[256,4096]{1,0:T(8,128)(2,1)S(1)} copy-done((bf16[256,4096]{1,0:T(8,128)(2,1)S(1)}, bf16[256,4096]{1,0:T(8,128)(2,1)}, u32[]{:S(2)}) %copy-start.2) | copy-done | bytes 2097176
  12.9 2.9 %screened.1.refs_0_ = bf16[2,512,4096]{2,1,0:T(8,128)(2,1)S(1)} custom-call(s32[16]{0:T(128)S(1)} %fusion.2.slot_ref, s32[4,32]{1,0:T(4,128)S(1)} %convert_element_type.15.mask_ref, bf16[256,4096]{1,0:T(8,128)(2,1)S(1)} %copy-done.1, bf16[256,4096]{1,0:T(8,128)(2,1)S(1)} %copy-done.2), custom_call_target="tpu_custom_call" | custom-call | bytes 4194304 | tf_op jit(solution)/shard_map/screened/pallas_call | solution.py:92
  15.8 14.5 %collective-permute-start.1 = (bf16[2,256,512]{2,1,0:T(8,128)(2,1)S(1)}, bf16[2,256,512]{2,1,0:T(8,128)(2,1)S(1)}, u32[]{:S(2)}, u32[]{:S(2)}) collective-permute-start(bf16[2,256,512]{2,1,0:T(8,128)(2,1)S(1)} %collective-permute-done.refs_2_), channel_id=1, source_target_pairs={{0,2},{2,4},{4,6},{6,8},{8,10},{10,12},{12,14},{14,0},{1,15},{3,1}... | collective-permute-start | bytes 1572872 | tf_op jit(solution)/shard_map/ppermute | solution.py:28
  30.3 3.6 %collective-permute-start.6 = (bf16[2,256,512]{2,1,0:T(8,128)(2,1)S(1)}, bf16[2,256,512]{2,1,0:T(8,128)(2,1)S(1)}, u32[]{:S(2)}, u32[]{:S(2)}) collective-permute-start(bf16[2,256,512]{2,1,0:T(8,128)(2,1)S(1)} %collective-permute-done.3.refs_3_), channel_id=1, source_target_pairs={{0,2},{2,4},{4,6},{6,8},{8,10},{10,12},{12,14},{14,0},{1,15},{3,1}... | collective-permute-start | bytes 1572872 | tf_op jit(solution)/shard_map/ppermute | solution.py:28
  33.9 2.7 %collective-permute-start.4 = (bf16[2,256,512]{2,1,0:T(8,128)(2,1)S(1)}, bf16[2,256,512]{2,1,0:T(8,128)(2,1)S(1)}, u32[]{:S(2)}, u32[]{:S(2)}) collective-permute-start(bf16[2,256,512]{2,1,0:T(8,128)(2,1)S(1)} %collective-permute-done.refs_2_), channel_id=1, source_target_pairs={{0,1},{1,0},{2,3},{3,2},{4,5},{5,4},{6,7},{7,6},{8,9},{9,8},{10,11... | collective-permute-start | bytes 1572872 | tf_op jit(solution)/shard_map/ppermute | solution.py:21
  36.6 1.9 %collective-permute-start.5 = (bf16[2,256,512]{2,1,0:T(8,128)(2,1)S(1)}, bf16[2,256,512]{2,1,0:T(8,128)(2,1)S(1)}, u32[]{:S(2)}, u32[]{:S(2)}) collective-permute-start(bf16[2,256,512]{2,1,0:T(8,128)(2,1)S(1)} %collective-permute-done.3.refs_3_), channel_id=1, source_target_pairs={{0,1},{1,0},{2,3},{3,2},{4,5},{5,4},{6,7},{7,6},{8,9},{9,8},{10,11... | collective-permute-start | bytes 1572872 | tf_op jit(solution)/shard_map/ppermute | solution.py:21
  38.6 4.9 %collective-permute-start.2 = (bf16[2,256,512]{2,1,0:T(8,128)(2,1)S(1)}, bf16[2,256,512]{2,1,0:T(8,128)(2,1)S(1)}, u32[]{:S(2)}, u32[]{:S(2)}) collective-permute-start(bf16[2,256,512]{2,1,0:T(8,128)(2,1)S(1)} %collective-permute-done.1.refs_6_), channel_id=1, source_target_pairs={{0,2},{2,4},{4,6},{6,8},{8,10},{10,12},{12,14},{14,0},{1,15},{3,1}... | collective-permute-start | bytes 1572872 | tf_op jit(solution)/shard_map/ppermute | solution.py:28
  43.4 0.1 pad_maximum_fusion
  43.5 3.5 %collective-permute-start.9 = (bf16[4,256,512]{2,1,0:T(8,128)(2,1)S(1)}, bf16[4,256,512]{2,1,0:T(8,128)(2,1)S(1)}, u32[]{:S(2)}, u32[]{:S(2)}) collective-permute-start(bf16[4,256,512]{2,1,0:T(8,128)(2,1)S(1)} %pad_maximum_fusion), channel_id=1, source_target_pairs={{0,1},{1,0},{2,3},{3,2},{4,5},{5,4},{6,7},{7,6},{8,9},{9,8},{10,11... | collective-permute-start | bytes 3145736 | tf_op jit(solution)/shard_map/ppermute | solution.py:21
  47.1 4.9 %collective-permute-start.12 = (bf16[2,256,512]{2,1,0:T(8,128)(2,1)S(1)}, bf16[2,256,512]{2,1,0:T(8,128)(2,1)S(1)}, u32[]{:S(2)}, u32[]{:S(2)}) collective-permute-start(bf16[2,256,512]{2,1,0:T(8,128)(2,1)S(1)} %collective-permute-done.6.refs_7_), channel_id=1, source_target_pairs={{0,2},{2,4},{4,6},{6,8},{8,10},{10,12},{12,14},{14,0},{1,15},{3,1}... | collective-permute-start | bytes 1572872 | tf_op jit(solution)/shard_map/ppermute | solution.py:28
  52.0 2.1 %sum_1.1.refs_8_ = f32[2,512,512]{2,1,0:T(8,128)S(1)} custom-call(bf16[2,512,4096]{2,1,0:T(8,128)(2,1)S(1)} %screened.1.refs_0_, bf16[2,256,512]{2,1,0:T(8,128)(2,1)S(1)} %copy-done, bf16[2,256,512]{2,1,0:T(8,128)(2,1)S(1)} %collective-permute-done.refs_2_, bf16[2,256,512]{2,1,0:T(8,128)(2,1)S(1)} %collective-permute-done.3.refs_3_, ...), custom_call_target="tpu_custom_call" | custom-call | flops 1879048192 | bytes 1048576 | tf_op jit(solution)/shard_map/sum_1/pallas_call | solution.py:132
  54.0 0.0 copy-start.3
  54.0 2.1 %collective-permute-start.7 = (bf16[2,256,512]{2,1,0:T(8,128)(2,1)S(1)}, bf16[2,256,512]{2,1,0:T(8,128)(2,1)S(1)}, u32[]{:S(2)}, u32[]{:S(2)}) collective-permute-start(bf16[2,256,512]{2,1,0:T(8,128)(2,1)S(1)} %collective-permute-done.2.refs_3_), channel_id=1, source_target_pairs={{0,2},{2,4},{4,6},{6,8},{8,10},{10,12},{12,14},{14,0},{1,15},{3,1}... | collective-permute-start | bytes 1572872 | tf_op jit(solution)/shard_map/ppermute | solution.py:28
  56.1 3.1 %collective-permute-start.10 = (bf16[2,256,512]{2,1,0:T(8,128)(2,1)S(1)}, bf16[2,256,512]{2,1,0:T(8,128)(2,1)S(1)}, u32[]{:S(2)}, u32[]{:S(2)}) collective-permute-start(bf16[2,256,512]{2,1,0:T(8,128)(2,1)S(1)} %collective-permute-done.6.refs_7_), channel_id=1, source_target_pairs={{0,1},{1,0},{2,3},{3,2},{4,5},{5,4},{6,7},{7,6},{8,9},{9,8},{10,11... | collective-permute-start | bytes 1572872 | tf_op jit(solution)/shard_map/ppermute | solution.py:21
  59.2 1.9 %collective-permute-start.11 = (bf16[2,256,512]{2,1,0:T(8,128)(2,1)S(1)}, bf16[2,256,512]{2,1,0:T(8,128)(2,1)S(1)}, u32[]{:S(2)}, u32[]{:S(2)}) collective-permute-start(bf16[2,256,512]{2,1,0:T(8,128)(2,1)S(1)} %collective-permute-done.2.refs_3_), channel_id=1, source_target_pairs={{0,1},{1,0},{2,3},{3,2},{4,5},{5,4},{6,7},{7,6},{8,9},{9,8},{10,11... | collective-permute-start | bytes 1572872 | tf_op jit(solution)/shard_map/ppermute | solution.py:21
  61.2 2.4 %collective-permute-start.13 = (bf16[2,256,512]{2,1,0:T(8,128)(2,1)S(1)}, bf16[2,256,512]{2,1,0:T(8,128)(2,1)S(1)}, u32[]{:S(2)}, u32[]{:S(2)}) collective-permute-start(bf16[2,256,512]{2,1,0:T(8,128)(2,1)S(1)} %collective-permute-done.12.refs_6_), channel_id=1, source_target_pairs={{0,1},{1,0},{2,3},{3,2},{4,5},{5,4},{6,7},{7,6},{8,9},{9,8},{10,11... | collective-permute-start | bytes 1572872 | tf_op jit(solution)/shard_map/ppermute | solution.py:21
  63.6 0.8 collective-permute-done.7.refs_7_
  64.4 5.2 %collective-permute-start.8 = (bf16[2,256,512]{2,1,0:T(8,128)(2,1)S(1)}, bf16[2,256,512]{2,1,0:T(8,128)(2,1)S(1)}, u32[]{:S(2)}, u32[]{:S(2)}) collective-permute-start(bf16[2,256,512]{2,1,0:T(8,128)(2,1)S(1)} %collective-permute-done.7.refs_7_), channel_id=1, source_target_pairs={{0,1},{1,0},{2,3},{3,2},{4,5},{5,4},{6,7},{7,6},{8,9},{9,8},{10,11... | collective-permute-start | bytes 1572872 | tf_op jit(solution)/shard_map/ppermute | solution.py:21
  69.6 2.3 %sum_3.1.refs_2_ = f32[2,512,512]{2,1,0:T(8,128)S(1)} custom-call(bf16[2,512,4096]{2,1,0:T(8,128)(2,1)S(1)} %screened.1.refs_0_, bf16[4,256,512]{2,1,0:T(8,128)(2,1)S(1)} %collective-permute-done.9.refs_1_, bf16[2,256,512]{2,1,0:T(8,128)(2,1)S(1)} %collective-permute-done.10.refs_2_, bf16[2,256,512]{2,1,0:T(8,128)(2,1)S(1)} %collective-permute-done.2.refs_3_, ...), custom_call_target="tpu_custom_call" | custom-call | flops 2147483648 | bytes 1048576 | tf_op jit(solution)/shard_map/sum_3/pallas_call | solution.py:132
  72.0 0.9 sum_5.1
  72.8 0.7 collective-permute-start.15
  73.5 6.5 %collective-permute-start.14 = (bf16[2,256,512]{2,1,0:T(8,128)(2,1)S(1)}, bf16[2,256,512]{2,1,0:T(8,128)(2,1)S(1)}, u32[]{:S(2)}, u32[]{:S(2)}) collective-permute-start(bf16[2,256,512]{2,1,0:T(8,128)(2,1)S(1)} %sum_5.1), channel_id=1, source_target_pairs={{0,1008},{1,1009},{2,1010},{3,1011},{4,1012},{5,1013},{6,1014},{7,... | collective-permute-start | bytes 1572872 | tf_op jit(solution)/shard_map/ppermute | solution.py:63
  80.0 0.7 collective-permute-start.16
  80.7 34.2 %collective-permute-done.14 = bf16[2,256,512]{2,1,0:T(8,128)(2,1)S(1)} collective-permute-done((bf16[2,256,512]{2,1,0:T(8,128)(2,1)S(1)}, bf16[2,256,512]{2,1,0:T(8,128)(2,1)S(1)}, u32[]{:S(2)}, u32[]{:S(2)}) %collective-permute-start.14) | collective-permute-done | bytes 524320 | tf_op jit(solution)/shard_map/ppermute | solution.py:63
  114.9 1.0 add_convert_fusion
  (20 shorter events, 0.1 us)
Async XLA Ops:
  0.0 15.8 %collective-permute-start = (bf16[2,256,512]{2,1,0:T(8,128)(2,1)}, bf16[2,256,512]{2,1,0:T(8,128)(2,1)S(1)}, u32[]{:S(2)}, u32[]{:S(2)}) collective-permute-start(bf16[2,256,512]{2,1,0:T(8,128)(2,1)} %refs_1_.1), channel_id=1, source_target_pairs={{0,2},{2,4},{4,6},{6,8},{8,10},{10,12},{12,14},{14,0},{1,15},{3,1}... | collective-permute-start | bytes 1572872 | tf_op jit(solution)/shard_map/ppermute | solution.py:28
  5.9 24.4 %collective-permute-start.3 = (bf16[2,256,512]{2,1,0:T(8,128)(2,1)}, bf16[2,256,512]{2,1,0:T(8,128)(2,1)S(1)}, u32[]{:S(2)}, u32[]{:S(2)}) collective-permute-start(bf16[2,256,512]{2,1,0:T(8,128)(2,1)} %refs_1_.1), channel_id=1, source_target_pairs={{1,2},{3,4},{5,6},{7,8},{9,10},{11,12},{13,14},{15,0},{0,15},{2,1}... | collective-permute-start | bytes 1572872 | tf_op jit(solution)/shard_map/ppermute | solution.py:28
  9.7 1.6 %copy-start.1 = (bf16[256,4096]{1,0:T(8,128)(2,1)S(1)}, bf16[256,4096]{1,0:T(8,128)(2,1)}, u32[]{:S(2)}) copy-start(bf16[256,4096]{1,0:T(8,128)(2,1)} %fock.1) | copy-start | bytes 6291460
  11.3 1.6 %copy-start.2 = (bf16[256,4096]{1,0:T(8,128)(2,1)S(1)}, bf16[256,4096]{1,0:T(8,128)(2,1)}, u32[]{:S(2)}) copy-start(bf16[256,4096]{1,0:T(8,128)(2,1)} %ladder.1) | copy-start | bytes 6291460
  12.9 30.6 %copy-start = (bf16[2,256,512]{2,1,0:T(8,128)(2,1)S(1)}, bf16[2,256,512]{2,1,0:T(8,128)(2,1)}, u32[]{:S(2)}) copy-start(bf16[2,256,512]{2,1,0:T(8,128)(2,1)} %refs_1_.1) | copy-start | bytes 1572868
  15.8 22.7 %collective-permute-start.1 = (bf16[2,256,512]{2,1,0:T(8,128)(2,1)S(1)}, bf16[2,256,512]{2,1,0:T(8,128)(2,1)S(1)}, u32[]{:S(2)}, u32[]{:S(2)}) collective-permute-start(bf16[2,256,512]{2,1,0:T(8,128)(2,1)S(1)} %collective-permute-done.refs_2_), channel_id=1, source_target_pairs={{0,2},{2,4},{4,6},{6,8},{8,10},{10,12},{12,14},{14,0},{1,15},{3,1}... | collective-permute-start | bytes 1572872 | tf_op jit(solution)/shard_map/ppermute | solution.py:28
  30.3 16.8 %collective-permute-start.6 = (bf16[2,256,512]{2,1,0:T(8,128)(2,1)S(1)}, bf16[2,256,512]{2,1,0:T(8,128)(2,1)S(1)}, u32[]{:S(2)}, u32[]{:S(2)}) collective-permute-start(bf16[2,256,512]{2,1,0:T(8,128)(2,1)S(1)} %collective-permute-done.3.refs_3_), channel_id=1, source_target_pairs={{0,2},{2,4},{4,6},{6,8},{8,10},{10,12},{12,14},{14,0},{1,15},{3,1}... | collective-permute-start | bytes 1572872 | tf_op jit(solution)/shard_map/ppermute | solution.py:28
  33.9 18.1 %collective-permute-start.4 = (bf16[2,256,512]{2,1,0:T(8,128)(2,1)S(1)}, bf16[2,256,512]{2,1,0:T(8,128)(2,1)S(1)}, u32[]{:S(2)}, u32[]{:S(2)}) collective-permute-start(bf16[2,256,512]{2,1,0:T(8,128)(2,1)S(1)} %collective-permute-done.refs_2_), channel_id=1, source_target_pairs={{0,1},{1,0},{2,3},{3,2},{4,5},{5,4},{6,7},{7,6},{8,9},{9,8},{10,11... | collective-permute-start | bytes 1572872 | tf_op jit(solution)/shard_map/ppermute | solution.py:21
  36.6 15.3 %collective-permute-start.5 = (bf16[2,256,512]{2,1,0:T(8,128)(2,1)S(1)}, bf16[2,256,512]{2,1,0:T(8,128)(2,1)S(1)}, u32[]{:S(2)}, u32[]{:S(2)}) collective-permute-start(bf16[2,256,512]{2,1,0:T(8,128)(2,1)S(1)} %collective-permute-done.3.refs_3_), channel_id=1, source_target_pairs={{0,1},{1,0},{2,3},{3,2},{4,5},{5,4},{6,7},{7,6},{8,9},{9,8},{10,11... | collective-permute-start | bytes 1572872 | tf_op jit(solution)/shard_map/ppermute | solution.py:21
  38.6 15.5 %collective-permute-start.2 = (bf16[2,256,512]{2,1,0:T(8,128)(2,1)S(1)}, bf16[2,256,512]{2,1,0:T(8,128)(2,1)S(1)}, u32[]{:S(2)}, u32[]{:S(2)}) collective-permute-start(bf16[2,256,512]{2,1,0:T(8,128)(2,1)S(1)} %collective-permute-done.1.refs_6_), channel_id=1, source_target_pairs={{0,2},{2,4},{4,6},{6,8},{8,10},{10,12},{12,14},{14,0},{1,15},{3,1}... | collective-permute-start | bytes 1572872 | tf_op jit(solution)/shard_map/ppermute | solution.py:28
  43.5 26.1 %collective-permute-start.9 = (bf16[4,256,512]{2,1,0:T(8,128)(2,1)S(1)}, bf16[4,256,512]{2,1,0:T(8,128)(2,1)S(1)}, u32[]{:S(2)}, u32[]{:S(2)}) collective-permute-start(bf16[4,256,512]{2,1,0:T(8,128)(2,1)S(1)} %pad_maximum_fusion), channel_id=1, source_target_pairs={{0,1},{1,0},{2,3},{3,2},{4,5},{5,4},{6,7},{7,6},{8,9},{9,8},{10,11... | collective-permute-start | bytes 3145736 | tf_op jit(solution)/shard_map/ppermute | solution.py:21
  47.1 14.1 %collective-permute-start.12 = (bf16[2,256,512]{2,1,0:T(8,128)(2,1)S(1)}, bf16[2,256,512]{2,1,0:T(8,128)(2,1)S(1)}, u32[]{:S(2)}, u32[]{:S(2)}) collective-permute-start(bf16[2,256,512]{2,1,0:T(8,128)(2,1)S(1)} %collective-permute-done.6.refs_7_), channel_id=1, source_target_pairs={{0,2},{2,4},{4,6},{6,8},{8,10},{10,12},{12,14},{14,0},{1,15},{3,1}... | collective-permute-start | bytes 1572872 | tf_op jit(solution)/shard_map/ppermute | solution.py:28
  54.0 17.9 %copy-start.3 = (bf16[512,512]{1,0:T(8,128)(2,1)S(1)}, bf16[512,512]{1,0:T(8,128)(2,1)}, u32[]{:S(2)}) copy-start(bf16[512,512]{1,0:T(8,128)(2,1)} %refs_3_.1) | copy-start | bytes 1572868
  54.0 10.4 %collective-permute-start.7 = (bf16[2,256,512]{2,1,0:T(8,128)(2,1)S(1)}, bf16[2,256,512]{2,1,0:T(8,128)(2,1)S(1)}, u32[]{:S(2)}, u32[]{:S(2)}) collective-permute-start(bf16[2,256,512]{2,1,0:T(8,128)(2,1)S(1)} %collective-permute-done.2.refs_3_), channel_id=1, source_target_pairs={{0,2},{2,4},{4,6},{6,8},{8,10},{10,12},{12,14},{14,0},{1,15},{3,1}... | collective-permute-start | bytes 1572872 | tf_op jit(solution)/shard_map/ppermute | solution.py:28
  56.1 13.5 %collective-permute-start.10 = (bf16[2,256,512]{2,1,0:T(8,128)(2,1)S(1)}, bf16[2,256,512]{2,1,0:T(8,128)(2,1)S(1)}, u32[]{:S(2)}, u32[]{:S(2)}) collective-permute-start(bf16[2,256,512]{2,1,0:T(8,128)(2,1)S(1)} %collective-permute-done.6.refs_7_), channel_id=1, source_target_pairs={{0,1},{1,0},{2,3},{3,2},{4,5},{5,4},{6,7},{7,6},{8,9},{9,8},{10,11... | collective-permute-start | bytes 1572872 | tf_op jit(solution)/shard_map/ppermute | solution.py:21
  59.2 10.4 %collective-permute-start.11 = (bf16[2,256,512]{2,1,0:T(8,128)(2,1)S(1)}, bf16[2,256,512]{2,1,0:T(8,128)(2,1)S(1)}, u32[]{:S(2)}, u32[]{:S(2)}) collective-permute-start(bf16[2,256,512]{2,1,0:T(8,128)(2,1)S(1)} %collective-permute-done.2.refs_3_), channel_id=1, source_target_pairs={{0,1},{1,0},{2,3},{3,2},{4,5},{5,4},{6,7},{7,6},{8,9},{9,8},{10,11... | collective-permute-start | bytes 1572872 | tf_op jit(solution)/shard_map/ppermute | solution.py:21
  61.2 8.4 %collective-permute-start.13 = (bf16[2,256,512]{2,1,0:T(8,128)(2,1)S(1)}, bf16[2,256,512]{2,1,0:T(8,128)(2,1)S(1)}, u32[]{:S(2)}, u32[]{:S(2)}) collective-permute-start(bf16[2,256,512]{2,1,0:T(8,128)(2,1)S(1)} %collective-permute-done.12.refs_6_), channel_id=1, source_target_pairs={{0,1},{1,0},{2,3},{3,2},{4,5},{5,4},{6,7},{7,6},{8,9},{9,8},{10,11... | collective-permute-start | bytes 1572872 | tf_op jit(solution)/shard_map/ppermute | solution.py:21
  64.4 7.6 %collective-permute-start.8 = (bf16[2,256,512]{2,1,0:T(8,128)(2,1)S(1)}, bf16[2,256,512]{2,1,0:T(8,128)(2,1)S(1)}, u32[]{:S(2)}, u32[]{:S(2)}) collective-permute-start(bf16[2,256,512]{2,1,0:T(8,128)(2,1)S(1)} %collective-permute-done.7.refs_7_), channel_id=1, source_target_pairs={{0,1},{1,0},{2,3},{3,2},{4,5},{5,4},{6,7},{7,6},{8,9},{9,8},{10,11... | collective-permute-start | bytes 1572872 | tf_op jit(solution)/shard_map/ppermute | solution.py:21
  72.8 7.2 %collective-permute-start.15 = (bf16[2,256,512]{2,1,0:T(8,128)(2,1)S(1)}, bf16[2,256,512]{2,1,0:T(8,128)(2,1)S(1)}, u32[]{:S(2)}, u32[]{:S(2)}) collective-permute-start(bf16[2,256,512]{2,1,0:T(8,128)(2,1)S(1)} %sum_5.1), channel_id=1, source_target_pairs={{48,128},{49,129},{50,130},{51,131},{52,132},{53,133},{54,134},{55... | collective-permute-start | bytes 1572872 | tf_op jit(solution)/shard_map/ppermute | solution.py:62
  73.5 41.3 %collective-permute-start.14 = (bf16[2,256,512]{2,1,0:T(8,128)(2,1)S(1)}, bf16[2,256,512]{2,1,0:T(8,128)(2,1)S(1)}, u32[]{:S(2)}, u32[]{:S(2)}) collective-permute-start(bf16[2,256,512]{2,1,0:T(8,128)(2,1)S(1)} %sum_5.1), channel_id=1, source_target_pairs={{0,1008},{1,1009},{2,1010},{3,1011},{4,1012},{5,1013},{6,1014},{7,... | collective-permute-start | bytes 1572872 | tf_op jit(solution)/shard_map/ppermute | solution.py:63
  80.0 34.9 %collective-permute-start.16 = (bf16[2,256,512]{2,1,0:T(8,128)(2,1)S(1)}, bf16[2,256,512]{2,1,0:T(8,128)(2,1)S(1)}, u32[]{:S(2)}, u32[]{:S(2)}) collective-permute-start(bf16[2,256,512]{2,1,0:T(8,128)(2,1)S(1)} %collective-permute-done.15), channel_id=1, source_target_pairs={{128,240},{129,241},{130,242},{131,243},{132,244},{133,245},{134,2... | collective-permute-start | bytes 1572872 | tf_op jit(solution)/shard_map/ppermute | solution.py:64
